TPU v7x, 1024 devices: a whole 4x8x16 slice. The times are simulated.
1024 devices in a mesh: gx: 16 (over y, core), gy: 64 (over x, z).
Axes of the slice: x: 4, y: 8, z: 16, core: 2. Of those that a mesh axis runs over, the one named last changes fastest.
Arguments:
- couplings: bfloat16 [64, 512, 64, 320], P('gx', 'gy'), may hold values from -0.3125 to 0.3125
- prolong: bfloat16 [64, 512, 32, 128], P('gx', 'gy'), may hold values from -1.5 to 1.5
- present: int32 [64, 512, 4], P('gx', 'gy'), may hold values 0 or 1
- entries: int32 [64, 512, 5], P('gx', 'gy'), may hold values from 0 to 31
- owners: int32 [16, 2048, 1], P('gx', 'gy'), may hold values from 0 to 63; in each aligned block of 32 rows (0 to 31, 32 to 63, ..., all dimensions but the last counted through in order) at most 2 rows name the same one
- targets: int32 [16, 2048], P('gx', 'gy'), may hold values from 0 to 15
Outputs:
- coarse: bfloat16 [16, 1024, 32, 128], P('gx', 'gy')
Inputs may be any that keep to these rules, and one draw needn't show every extreme that they name: `owners`: among the 32 partial blocks of one tile at most 2 have the same owner column, and some owner column is named exactly 2 times in some tile.
All inputs are finite; a program needn't handle non-finite values. No bound on the sum of `present` on one device may be relied on, other than what follows from the above.
Results may differ from a plain program's by a relative error of at most 0.014.
Values may be sent and summed in bfloat16 or wider, within the bound.
No kernel may reach another device: no remote copies, remote signals or barrier semaphores. Data moves between devices by JAX's collectives and lax.ppermute only.
A program may use at most 32 MiB of HBM per device.

v0:
```python
import jax
import jax.numpy as jnp
from jax import lax
from jax.sharding import PartitionSpec as P


def extended(cells, sides, width):
    for axis, dim in sides:
        count = lax.axis_size(axis)
        ends = count - 1
        head = lax.slice_in_dim(cells, 0, width, axis=dim)
        tail = lax.slice_in_dim(cells, cells.shape[dim] - width, cells.shape[dim], axis=dim)
        cells = jnp.concatenate(
            [
                lax.ppermute(tail, axis, [(i, (i + 1) % count) for i in range(ends)]),
                cells,
                lax.ppermute(head, axis, [((i + 1) % count, i) for i in range(ends)]),
            ],
            axis=dim,
        )
    return cells


def place_rows(slots, slot_total, partial_value, tags_value):
    place_hot = jnp.arange(slot_total, dtype=jnp.int32)[:, None] == slots[None, :]
    outgoing = jnp.dot(
        place_hot.astype(jnp.bfloat16), partial_value, preferred_element_type=jnp.float32
    ).astype(jnp.bfloat16)
    slot_tags = jnp.dot(
        place_hot.astype(jnp.bfloat16),
        tags_value.astype(jnp.bfloat16)[:, None],
        preferred_element_type=jnp.float32,
    )[:, 0].astype(jnp.bfloat16)
    return (outgoing, slot_tags)


def shards(couplings, prolong, present, entries, owners, targets):
    cells_x = prolong.shape[0]
    cells_y = prolong.shape[1]
    block_size = couplings.shape[2]
    cell_count = cells_x * cells_y
    blocks = couplings.reshape(cells_x, cells_y, block_size, 5, block_size)
    factor = jnp.concatenate(
        [jnp.ones((cells_x, cells_y, 1), jnp.float32), present.astype(jnp.float32)], axis=2
    )
    own_block = prolong.reshape(cells_x, cells_y, block_size, block_size)
    padded = extended(prolong, (("gx", 0), ("gy", 1)), 1)
    padded = padded.reshape(cells_x + 2, cells_y + 2, block_size, block_size)
    neighbours = jnp.concatenate(
        [
            own_block[:, :, None],
            jnp.stack(
                [padded[2:, 1:-1], padded[:-2, 1:-1], padded[1:-1, 2:], padded[1:-1, :-2]], axis=2
            ),
        ],
        axis=2,
    )
    images = jnp.einsum(
        "xyrdk,xydkc->xydrc", blocks, neighbours, preferred_element_type=jnp.float32
    )
    images = (images * factor[:, :, 0 : 0 + 5, None, None]).astype(jnp.bfloat16)
    terms = jnp.einsum("xykr,xydkc->xydrc", own_block, images, preferred_element_type=jnp.float32)
    flat_terms = terms.reshape(cell_count * 5, block_size * block_size)
    entry_flat = entries.reshape(cell_count * 5)
    gather_hot = (jnp.arange(cell_count, dtype=jnp.int32)[:, None] == entry_flat[None, :]).astype(
        jnp.bfloat16
    )
    high_part = flat_terms.astype(jnp.bfloat16)
    low_part = (flat_terms - high_part.astype(jnp.float32)).astype(jnp.bfloat16)
    partial_sum = jnp.dot(gather_hot, high_part, preferred_element_type=jnp.float32)
    partial_sum = partial_sum + jnp.dot(gather_hot, low_part, preferred_element_type=jnp.float32)
    partial_value = partial_sum.astype(jnp.bfloat16)
    owner_ids = owners.reshape(cell_count)
    target_ids = targets.reshape(cell_count)
    peer_count = lax.axis_size("gy")
    capacity = max(2, (3 * cell_count + 2 * peer_count - 1) // (2 * peer_count))
    positions = jnp.arange(cell_count, dtype=jnp.int32)
    earlier = (owner_ids[None, :] == owner_ids[:, None]) & (positions[None, :] < positions[:, None])
    slot_rank = jnp.sum(earlier.astype(jnp.int32), axis=1)
    tags_value = (target_ids + 1).astype(jnp.float32)
    slot_total = peer_count * capacity
    slots = owner_ids * capacity + slot_rank
    outgoing, slot_tags = place_rows(slots, slot_total, partial_value, tags_value)
    received, got_tags = (
        lax.all_to_all(outgoing, "gy", split_axis=0, concat_axis=0, tiled=True),
        lax.all_to_all(slot_tags, "gy", split_axis=0, concat_axis=0, tiled=True),
    )
    owned_count = max(2, cell_count // 2)
    levels = jnp.arange(1, owned_count + 1, dtype=jnp.int32).astype(jnp.float32)
    sum_hot = (levels[:, None] == got_tags.astype(jnp.float32)[None, :]).astype(jnp.bfloat16)
    coarse = jnp.dot(sum_hot, received, preferred_element_type=jnp.float32).astype(jnp.bfloat16)
    return coarse.reshape(1, owned_count, block_size // 2, 2 * block_size)


def solution(mesh):
    in_specs = (
        P("gx", "gy", None, None),
        P("gx", "gy", None, None),
        P("gx", "gy", None),
        P("gx", "gy", None),
        P("gx", "gy", None),
        P("gx", "gy"),
    )
    out_specs = P("gx", "gy", None, None)
    return jax.shard_map(shards, mesh=mesh, in_specs=in_specs, out_specs=out_specs, check_vma=False)
```

profile of v0, /device:TPU:24, one launch (start us, length us, event | category | flops | bytes accessed | tf_op | source)
XLA Modules:
  0.0 157.1 jit_solution(5361583347964306037)
XLA Ops:
  0.0 0.9 fusion.27
  0.9 1.9 %collective-permute-start = (bf16[1,8,32,128]{3,2,1,0:T(8,128)(2,1)S(1)}, bf16[1,8,32,128]{3,2,1,0:T(8,128)(2,1)S(1)}, u32[]{:S(2)}, u32[]{:S(2)}) collective-permute-start(bf16[1,8,32,128]{3,2,1,0:T(8,128)(2,1)S(1)} %get-tuple-element.12), channel_id=1, source_target_pairs={{0,64},{64,128},{128,192},{192,256},{256,320},{320,384},{384,448},... | collective-permute-start | bytes 196616 | tf_op jit(solution)/shard_map/ppermute | solution.py:15
  2.9 3.6 %collective-permute-start.1 = (bf16[1,8,32,128]{3,2,1,0:T(8,128)(2,1)S(1)}, bf16[1,8,32,128]{3,2,1,0:T(8,128)(2,1)S(1)}, u32[]{:S(2)}, u32[]{:S(2)}) collective-permute-start(bf16[1,8,32,128]{3,2,1,0:T(8,128)(2,1)S(1)} %get-tuple-element.11), channel_id=1, source_target_pairs={{64,0},{128,64},{192,128},{256,192},{320,256},{384,320},{448,384},... | collective-permute-start | bytes 196616 | tf_op jit(solution)/shard_map/ppermute | solution.py:17
  6.5 0.9 convert_reduce_fusion.1
  9.1 0.8 copy.34
  9.8 22.2 %all-to-all-start = ((bf16[64,2,1]{1,2,0:T(2,128)(2,1)}), bf16[64,2,1]{1,2,0:T(2,128)(2,1)S(1)}, u32[]{:S(2)}, u32[]{:S(2)}) async-start(bf16[64,2,1]{1,2,0:T(2,128)(2,1)} %copy.34), calls=%async_computation | async-start | bytes 65536 | tf_op jit(solution)/shard_map/all_to_all | solution.py:86
  32.1 1.2 broadcast_in_dim_reshape.2
  33.6 1.0 constant_dynamic-update-slice_fusion.1
  34.6 3.5 %collective-permute-start.2 = (bf16[6,1,32,128]{3,2,1,0:T(8,128)(2,1)S(1)}, bf16[6,1,32,128]{3,2,1,0:T(8,128)(2,1)S(1)}, u32[]{:S(2)}, u32[]{:S(2)}) collective-permute-start(bf16[6,1,32,128]{3,2,1,0:T(8,128)(2,1)S(1)} %get-tuple-element.9), channel_id=1, source_target_pairs={{0,1},{1,2},{2,3},{3,4},{4,5},{5,6},{6,7},{7,8},{8,9},{9,10},{10,1... | collective-permute-start | bytes 147464 | tf_op jit(solution)/shard_map/ppermute | solution.py:15
  38.1 1.3 collective-permute-start.3
  39.4 1.0 constant_dynamic-update-slice_fusion.3
  40.4 1.1 reshape.82
  41.5 3.1 %copy.41 = bf16[4,8,64,320]{2,3,1,0:T(8,128)(2,1)S(1)} copy(bf16[4,8,64,320]{3,2,1,0:T(8,128)(2,1)} %param.6) | data formatting | bytes 2621440 | tf_op args[0]
  46.2 0.9 pad_maximum_fusion
  47.1 1.4 reshape.74
  48.5 2.8 %fusion.25 = (bf16[4,8,64,64]{3,2,1,0:T(8,128)(2,1)}, bf16[4,8,64,64]{3,2,1,0:T(8,128)(2,1)}, bf16[4,8,64,64]{3,2,1,0:T(8,128)(2,1)S(1)}, bf16[4,8,64,64]{3,2,1,0:T(8,128)(2,1)}) fusion(bf16[6,10,64,64]{3,2,1,0:T(8,128)(2,1)} %reshape.74), kind=kLoop, calls=%fused_computation.43 | loop fusion | bytes 2097152 | tf_op jit(solution)/shard_map/slice | solution.py:53
  51.3 2.0 %copy.52 = bf16[4,8,64,64]{2,3,1,0:T(8,128)(2,1)} copy(bf16[4,8,64,64]{3,2,1,0:T(8,128)(2,1)} %get-tuple-element.8) | data formatting | bytes 524288
  53.3 1.1 copy.53
  54.4 1.3 copy.54
  55.7 2.0 %copy.55 = bf16[4,8,64,64]{2,3,1,0:T(8,128)(2,1)} copy(bf16[4,8,64,64]{3,2,1,0:T(8,128)(2,1)} %get-tuple-element.5) | data formatting | bytes 524288
  57.7 2.0 %bitcast_dynamic-update-slice_fusion.3 = bf16[4,8,5,64,64]{3,4,2,1,0:T(8,128)(2,1)} fusion(bf16[4,8,5,64,64]{3,4,2,1,0:T(8,128)(2,1)} %constant_dynamic-update-slice_fusion.3, bf16[4,8,64,64]{2,3,1,0:T(8,128)(2,1)} %copy.52), kind=kLoop, calls=%fused_computation.19 | loop fusion | bytes 1048576
  59.8 2.0 %bitcast_dynamic-update-slice_fusion.2 = bf16[4,8,5,64,64]{3,4,2,1,0:T(8,128)(2,1)} fusion(bf16[4,8,5,64,64]{3,4,2,1,0:T(8,128)(2,1)} %bitcast_dynamic-update-slice_fusion.3, bf16[4,8,64,64]{2,3,1,0:T(8,128)(2,1)} %copy.53), kind=kLoop, calls=%fused_computation.18 | loop fusion | bytes 1048576
  61.7 1.0 bitcast_dynamic-update-slice_fusion.1
  62.7 0.9 bitcast_dynamic-update-slice_fusion
  63.6 5.6 %fusion.7 = f32[4,8,5,64,64]{3,4,2,1,0:T(8,128)} fusion(f32[4,8,5]{2,1,0:T(8,128)S(1)} %concatenate.15.clone, bf16[4,8,5,64,64]{3,4,2,1,0:T(8,128)(2,1)} %bitcast_dynamic-update-slice_fusion, bf16[4,8,64,5,64]{2,4,3,1,0:T(8,128)(2,1)S(1)} %bitcast.43, bf16[4,8,64,64,1]{3,2,1,0,4:T(8,128)(2,1)} %reshape.82), kind=kOutput, calls=%fused_computation.10 | convolution fusion | flops 169082880 | bytes 5505664 | tf_op jit(solution)/shard_map/xykr,xydkc->xydrc/dot_general | solution.py:62
  69.3 5.9 %copy.44 = f32[4,8,5,64,64]{4,3,2,1,0:T(8,128)} copy(f32[4,8,5,64,64]{3,4,2,1,0:T(8,128)} %fusion.7) | data formatting | bytes 5242880 | tf_op jit(solution)/shard_map/xykr,xydkc->xydrc/transpose | solution.py:62
  75.2 4.0 %reshape.77 = f32[160,4096]{1,0:T(8,128)S(1)} reshape(f32[4,8,5,64,64]{4,3,2,1,0:T(8,128)} %copy.44) | data formatting | bytes 5242880 | tf_op jit(solution)/shard_map/reshape | solution.py:63
  79.9 1.6 %convolution_convert_fusion = bf16[128,4096]{1,0:T(8,128)(2,1)} fusion(f32[32,4096]{1,0:T(8,128)S(1)} %fusion.13, f32[160,4096]{1,0:T(8,128)S(1)} %reshape.77, s32[32]{0:T(128)S(1)} %copy-done.7, s32[160]{0:T(256)S(1)} %copy-done.4), kind=kOutput, calls=%fused_computation.1 | convolution fusion | flops 78914560 | bytes 4195072 | tf_op jit(solution)/shard_map/dot_general | solution.py:26
  81.5 2.5 %all_to_all.13 = bf16[64,2,4096]{2,1,0:T(2,128)(2,1)} reshape(bf16[128,4096]{1,0:T(8,128)(2,1)} %convolution_convert_fusion) | data formatting | bytes 2097152 | tf_op jit(solution)/shard_map/all_to_all | solution.py:85
  84.0 17.4 %all-to-all-start.1 = ((bf16[64,2,4096]{2,1,0:T(2,128)(2,1)}), bf16[64,2,4096]{2,1,0:T(2,128)(2,1)S(1)}, u32[]{:S(2)}, u32[]{:S(2)}) async-start(bf16[64,2,4096]{2,1,0:T(2,128)(2,1)} %all_to_all.13), calls=%async_computation.1 | async-start | bytes 2097152 | tf_op jit(solution)/shard_map/all_to_all | solution.py:85
  101.7 54.0 %all-to-all-done.1 = bf16[64,2,4096]{2,1,0:T(2,128)(2,1)S(1)} async-done(((bf16[64,2,4096]{2,1,0:T(2,128)(2,1)}), bf16[64,2,4096]{2,1,0:T(2,128)(2,1)S(1)}, u32[]{:S(2)}, u32[]{:S(2)}) %all-to-all-start.1) | async-done | bytes 1048608 | tf_op jit(solution)/shard_map/all_to_all | solution.py:85
  156.4 0.7 copy.57
  (41 shorter events, 5.1 us)
Async XLA Ops:
  0.0 40.4 %copy-start = (bf16[4,8,32,128]{3,2,1,0:T(8,128)(2,1)S(1)}, bf16[4,8,32,128]{3,2,1,0:T(8,128)(2,1)}, u32[]{:S(2)}) copy-start(bf16[4,8,32,128]{3,2,1,0:T(8,128)(2,1)} %param.7) | copy-start | bytes 786436
  0.9 32.6 %collective-permute-start = (bf16[1,8,32,128]{3,2,1,0:T(8,128)(2,1)S(1)}, bf16[1,8,32,128]{3,2,1,0:T(8,128)(2,1)S(1)}, u32[]{:S(2)}, u32[]{:S(2)}) collective-permute-start(bf16[1,8,32,128]{3,2,1,0:T(8,128)(2,1)S(1)} %get-tuple-element.12), channel_id=1, source_target_pairs={{0,64},{64,128},{128,192},{192,256},{256,320},{320,384},{384,448},... | collective-permute-start | bytes 196616 | tf_op jit(solution)/shard_map/ppermute | solution.py:15
  2.9 31.7 %collective-permute-start.1 = (bf16[1,8,32,128]{3,2,1,0:T(8,128)(2,1)S(1)}, bf16[1,8,32,128]{3,2,1,0:T(8,128)(2,1)S(1)}, u32[]{:S(2)}, u32[]{:S(2)}) collective-permute-start(bf16[1,8,32,128]{3,2,1,0:T(8,128)(2,1)S(1)} %get-tuple-element.11), channel_id=1, source_target_pairs={{64,0},{128,64},{192,128},{256,192},{320,256},{384,320},{448,384},... | collective-permute-start | bytes 196616 | tf_op jit(solution)/shard_map/ppermute | solution.py:17
  8.1 24.0 %copy-start.6 = (s32[32]{0:T(128)}, s32[32]{0:T(128)S(1)}, u32[]{:S(2)}) copy-start(s32[32]{0:T(128)S(1)} %multiply_add_fusion.1) | copy-start | bytes 388
  9.8 74.2 %all-to-all-start = ((bf16[64,2,1]{1,2,0:T(2,128)(2,1)}), bf16[64,2,1]{1,2,0:T(2,128)(2,1)S(1)}, u32[]{:S(2)}, u32[]{:S(2)}) async-start(bf16[64,2,1]{1,2,0:T(2,128)(2,1)} %copy.34), calls=%async_computation | async-start | bytes 65536 | tf_op jit(solution)/shard_map/all_to_all | solution.py:86
  34.6 10.9 %collective-permute-start.2 = (bf16[6,1,32,128]{3,2,1,0:T(8,128)(2,1)S(1)}, bf16[6,1,32,128]{3,2,1,0:T(8,128)(2,1)S(1)}, u32[]{:S(2)}, u32[]{:S(2)}) collective-permute-start(bf16[6,1,32,128]{3,2,1,0:T(8,128)(2,1)S(1)} %get-tuple-element.9), channel_id=1, source_target_pairs={{0,1},{1,2},{2,3},{3,4},{4,5},{5,6},{6,7},{7,8},{8,9},{9,10},{10,1... | collective-permute-start | bytes 147464 | tf_op jit(solution)/shard_map/ppermute | solution.py:15
  38.1 8.1 %collective-permute-start.3 = (bf16[6,1,32,128]{3,2,1,0:T(8,128)(2,1)S(1)}, bf16[6,1,32,128]{3,2,1,0:T(8,128)(2,1)}, u32[]{:S(2)}, u32[]{:S(2)}) collective-permute-start(bf16[6,1,32,128]{3,2,1,0:T(8,128)(2,1)S(1)} %get-tuple-element.10), channel_id=1, source_target_pairs={{1,0},{2,1},{3,2},{4,3},{5,4},{6,5},{7,6},{8,7},{9,8},{10,9},{11,1... | collective-permute-start | bytes 147464 | tf_op jit(solution)/shard_map/ppermute | solution.py:17
  40.4 4.2 %copy-start.5 = (s32[4,8,4]{1,2,0:T(4,128)S(1)}, s32[4,8,4]{1,2,0:T(4,128)}, u32[]{:S(2)}) copy-start(s32[4,8,4]{1,2,0:T(4,128)} %param.8) | copy-start | bytes 1540
  40.4 4.4 %copy-start.3 = (s32[4,8,5]{1,0,2:T(4,128)S(1)}, s32[4,8,5]{1,0,2:T(4,128)}, u32[]{:S(2)}) copy-start(s32[4,8,5]{1,0,2:T(4,128)} %param.9) | copy-start | bytes 1924
  45.6 0.6 copy-start.2
  57.7 5.0 %copy-start.1 = (bf16[4,8,64,64]{2,3,1,0:T(8,128)(2,1)S(1)}, bf16[4,8,64,64]{2,3,1,0:T(8,128)(2,1)}, u32[]{:S(2)}) copy-start(bf16[4,8,64,64]{2,3,1,0:T(8,128)(2,1)} %copy.55) | copy-start | bytes 786436
  75.2 4.1 %copy-start.4 = (s32[160]{0:T(256)S(1)}, s32[160]{0:T(256)}, u32[]{:S(2)}) copy-start(s32[160]{0:T(256)} %eq.93) | copy-start | bytes 1924
  79.3 0.6 copy-start.7
  84.0 71.7 %all-to-all-start.1 = ((bf16[64,2,4096]{2,1,0:T(2,128)(2,1)}), bf16[64,2,4096]{2,1,0:T(2,128)(2,1)S(1)}, u32[]{:S(2)}, u32[]{:S(2)}) async-start(bf16[64,2,4096]{2,1,0:T(2,128)(2,1)} %all_to_all.13), calls=%async_computation.1 | async-start | bytes 2097152 | tf_op jit(solution)/shard_map/all_to_all | solution.py:85
where the time goes:
time: 158 us; the launch traced here: 157 us
  waiting for transfers between devices  54 us (34%)
  starting transfers between devices  50 us (32%)
  local copies, waits for them, and re-layouts  41.6 us (26%)
  matrix products  7.84 us (5%)
  other arithmetic  3.47 us (2%)
    all_to_all x1, waiting for transfers between devices, shards(): lax.all_to_all(outgoing, 'gy', split_axis=0, concat_axis=0, tiled=True)  54 us
    all_to_all x1, starting transfers between devices, shards(): lax.all_to_all(slot_tags, 'gy', split_axis=0, concat_axis=0, tiled=True)  22.2 us
    unnamed x31, local copies, waits for them, and re-layouts  18.4 us
    all_to_all x1, starting transfers between devices, shards(): lax.all_to_all(outgoing, 'gy', split_axis=0, concat_axis=0, tiled=True)  17.4 us
    transpose x1, local copies, waits for them, and re-layouts, shards(): jnp.einsum('xykr,xydkc->xydrc', own_block, images, preferred_element_type...  5.94 us
    dot_general x1, matrix products, shards(): jnp.einsum('xykr,xydkc->xydrc', own_block, images, preferred_element_type...  5.64 us
    ppermute x2, starting transfers between devices, extended(): lax.ppermute(tail, axis, [(i, (i + 1) % count) for i in range(ends)])  5.4 us
    ppermute x2, starting transfers between devices, extended(): lax.ppermute(head, axis, [((i + 1) % count, i) for i in range(ends)])  4.93 us
  transfers between devices with their start and end apart: 6, of which 1 were waited for; matrix products, arithmetic and copies ran while one was open for 30% of the time, Pallas kernels for 0%

commit v1 on v0

v1 whole, which is shorter than its diff:
```python
import jax
import jax.numpy as jnp
from jax import lax
from jax.experimental import pallas as pl
from jax.experimental.pallas import tpu as pltpu
from jax.sharding import PartitionSpec as P

RING = 16
SLOTS = 8
VMEM = pl.BlockSpec(memory_space=pltpu.VMEM)
SMEM = pl.BlockSpec(memory_space=pltpu.SMEM)
PARAMS = pltpu.CompilerParams(vmem_limit_bytes=40 * 1024 * 1024)


def unpacked(lines, wide_ref):
    lines = lines.astype(jnp.float32)
    wide_ref[pl.ds(0, 32, stride=2), :] = lines
    wide_ref[pl.ds(1, 32, stride=2), :] = pltpu.roll(lines, 64, 1)
    return wide_ref[...].astype(jnp.bfloat16)


def left_kernel(prolong_ref, couplings_ref, left_ref, rows_ref, wide_ref):
    for cell in range(prolong_ref.shape[0]):
        rows = unpacked(prolong_ref[cell], wide_ref.at[cell % 4])
        rows_ref[cell] = rows
        product = lax.dot_general(
            rows[:, :64],
            couplings_ref[cell],
            (((0,), (0,)), ((), ())),
            preferred_element_type=jnp.float32,
        ).astype(jnp.bfloat16)
        for d in range(5):
            left_ref[cell, d] = product[:, d * 64 : d * 64 + 64]


def partial_kernel(
    cx,
    cy,
    left_ref,
    rows_ref,
    next_x_ref,
    last_x_ref,
    next_y_ref,
    last_y_ref,
    entries_ref,
    present_ref,
    owners_ref,
    targets_ref,
    out_ref,
    sums_ref,
    wide_ref,
    count_ref,
):
    count = cx * cy
    sums_ref[...] = jnp.zeros_like(sums_ref)

    def add(block, users):
        stack = [left_ref[x * cy + y, d] for x, y, d in users]
        stack = stack[0] if len(stack) == 1 else jnp.concatenate(stack, axis=0)
        terms = jnp.dot(stack, block, preferred_element_type=jnp.float32)
        for n, (x, y, d) in enumerate(users):
            entry = entries_ref[d, x, y]
            if d:
                entry = jnp.where(present_ref[x, d - 1, y] != 0, entry, count)
            sums_ref[entry] = sums_ref[entry] + terms[n * 64 : n * 64 + 64]

    for x in range(cx):
        for y in range(cy):
            users = [(x, y, 0), (x - 1, y, 1), (x + 1, y, 2), (x, y - 1, 3), (x, y + 1, 4)]
            users = [u for u in users if 0 <= u[0] < cx and 0 <= u[1] < cy]
            add(rows_ref[x * cy + y], users)
    for y in range(cy):
        add(unpacked(next_x_ref[y], wide_ref.at[y % 4]), [(cx - 1, y, 1)])
    for y in range(cy):
        add(unpacked(last_x_ref[y], wide_ref.at[y % 4]), [(0, y, 2)])
    for x in range(cx):
        add(unpacked(next_y_ref[x], wide_ref.at[x % 4]), [(x, cy - 1, 3)])
    for x in range(cx):
        add(unpacked(last_y_ref[x], wide_ref.at[x % 4]), [(x, 0, 4)])

    for ring in range(RING):
        count_ref[ring] = 0
    row_id = lax.broadcasted_iota(jnp.int32, (RING, 128), 0)
    lane_id = lax.broadcasted_iota(jnp.int32, (RING, 128), 1)
    low = lax.broadcasted_iota(jnp.int32, (32, 128), 1) < 64
    tags = jnp.full((RING, 128), 1.0, jnp.float32) * (RING * SLOTS)
    for e in range(count):
        owner = owners_ref[e]
        ring = owner % RING
        slot = count_ref[ring]
        count_ref[ring] = slot + 1
        even = sums_ref[e, pl.ds(0, 32, stride=2), :]
        odd = sums_ref[e, pl.ds(1, 32, stride=2), :]
        block = jnp.where(low, even, pltpu.roll(odd, 64, 1)).astype(jnp.bfloat16)
        out_ref[ring, pl.ds(pl.multiple_of(slot * 32, 32), 32), :] = block
        tag = (owner // RING) * 16 + targets_ref[e]
        tags = jnp.where((row_id == ring) & (lane_id == slot), tag.astype(jnp.float32), tags)
    for ring in range(RING):
        row = jnp.broadcast_to(tags[ring : ring + 1, :], (16, 128))
        out_ref[ring, SLOTS * 32 : SLOTS * 32 + 16, :] = row.astype(jnp.bfloat16)


def gather_kernel(blocks, got_ref, tags_ref, out_ref, sums_ref):
    sums_ref[...] = jnp.zeros_like(sums_ref)
    for ring in range(RING):
        for slot in range(SLOTS):
            tag = jnp.minimum(tags_ref[ring, slot], blocks)
            piece = got_ref[ring, slot * 32 : slot * 32 + 32, :].astype(jnp.float32)
            sums_ref[tag] = sums_ref[tag] + piece
    out_ref[...] = sums_ref[:blocks].astype(jnp.bfloat16)


def shards(couplings, prolong, present, entries, owners, targets):
    cx, cy = prolong.shape[0], prolong.shape[1]
    cells = cx * cy
    nx, ny = lax.axis_size("gx"), lax.axis_size("gy")
    across = ny // RING
    along = [[x * RING + z for z in range(RING)] for x in range(across)]
    aside = [[x * RING + z for x in range(across)] for z in range(RING)]
    owned = 16

    up_x = [(i, i + 1) for i in range(nx - 1)]
    down_x = [(i + 1, i) for i in range(nx - 1)]
    up_y = [(i, i + 1) for i in range(ny - 1)]
    down_y = [(i + 1, i) for i in range(ny - 1)]
    next_y = lax.ppermute(prolong[:, 0], "gy", down_y)
    last_y = lax.ppermute(prolong[:, cy - 1], "gy", up_y)
    next_x = lax.ppermute(prolong[0], "gx", down_x)
    last_x = lax.ppermute(prolong[cx - 1], "gx", up_x)

    left, rows = pl.pallas_call(
        left_kernel,
        out_shape=(
            jax.ShapeDtypeStruct((cells, 5, 64, 64), jnp.bfloat16),
            jax.ShapeDtypeStruct((cells, 64, 128), jnp.bfloat16),
        ),
        in_specs=[VMEM, VMEM],
        out_specs=(VMEM, VMEM),
        scratch_shapes=[pltpu.VMEM((4, 64, 128), jnp.float32)],
        compiler_params=PARAMS,
        cost_estimate=pl.CostEstimate(
            flops=cells * 5 * 2 * 64**3 * 8, bytes_accessed=cells * 90000, transcendentals=0
        ),
        name="left_factor",
    )(prolong.reshape(cells, 32, 128), couplings.reshape(cells, 64, 320))

    outgoing = pl.pallas_call(
        lambda *refs: partial_kernel(cx, cy, *refs),
        out_shape=jax.ShapeDtypeStruct((RING, SLOTS * 32 + 16, 128), jnp.bfloat16),
        in_specs=[VMEM] * 6 + [SMEM] * 4,
        out_specs=VMEM,
        scratch_shapes=[
            pltpu.VMEM((cells + 1, 64, 128), jnp.float32),
            pltpu.VMEM((4, 64, 128), jnp.float32),
            pltpu.SMEM((RING,), jnp.int32),
        ],
        compiler_params=PARAMS,
        name="partial_blocks",
    )(
        left,
        rows,
        next_x,
        last_x,
        next_y,
        last_y,
        jnp.transpose(entries, (2, 0, 1)),
        jnp.transpose(present, (0, 2, 1)),
        owners.reshape(cells),
        targets.reshape(cells),
    )
    got = lax.all_to_all(outgoing, "gy", 0, 0, axis_index_groups=along, tiled=True)
    tags = got[:, SLOTS * 32, :SLOTS].astype(jnp.int32)
    blocks = across * owned
    dense = pl.pallas_call(
        lambda *refs: gather_kernel(blocks, *refs),
        out_shape=jax.ShapeDtypeStruct((blocks, 32, 128), jnp.bfloat16),
        in_specs=[VMEM, SMEM],
        out_specs=VMEM,
        scratch_shapes=[pltpu.VMEM((blocks + 1, 32, 128), jnp.float32)],
        compiler_params=PARAMS,
        name="ring_sums",
    )(got, tags)
    pieces = lax.all_to_all(
        dense.reshape(across, owned * 32, 128), "gy", 0, 0, axis_index_groups=aside, tiled=True
    )
    coarse = jnp.sum(pieces.astype(jnp.float32), axis=0).astype(jnp.bfloat16)
    return coarse.reshape(1, owned, 32, 128)


def solution(mesh):
    in_specs = (
        P("gx", "gy", None, None),
        P("gx", "gy", None, None),
        P("gx", "gy", None),
        P("gx", "gy", None),
        P("gx", "gy", None),
        P("gx", "gy"),
    )
    out_specs = P("gx", "gy", None, None)
    return jax.shard_map(shards, mesh=mesh, in_specs=in_specs, out_specs=out_specs, check_vma=False)
```

time: 158 us -> 115 us (0.73)
  blocking collectives: 0 us -> 90.8 us
  waiting for transfers between devices: 54 us -> 0.01 us
  starting transfers between devices: 50 us -> 11.1 us
  local copies, waits for them, and re-layouts: 41.6 us -> 4.04 us
  Pallas kernels: 0 us -> 8.06 us
  matrix products: 7.84 us -> 0 us
  other arithmetic: 3.47 us -> 0.75 us
    all_to_all x0 -> x2, blocking collectives: none -> 90.8 us  [the longest x1 78.2 us: shards(): lax.all_to_all(outgoing, 'gy', 0, 0, axis_index_groups=along, tiled=True)]
    all_to_all x2 -> x0, waiting for transfers between devices: 54 us -> none  [the longest x1 54 us: shards(): lax.all_to_all(outgoing, 'gy', split_axis=0, concat_axis=0, tiled=True)]
    all_to_all x2 -> x0, starting transfers between devices: 39.6 us -> none  [the longest x1 22.2 us: shards(): lax.all_to_all(slot_tags, 'gy', split_axis=0, concat_axis=0, tiled=True)]
    unnamed x31 -> x12, local copies, waits for them, and re-layouts: 18.4 us -> 2.37 us
    pallas_call x0 -> x3, Pallas kernels: none -> 8.06 us  [the longest x1 4.04 us: shards(): pl.pallas_call(left_kernel, out_shape=(jax.ShapeDtypeStruct((cells, 5, 64...]
    dot_general x4 -> x0, matrix products: 7.84 us -> none  [the longest x1 5.64 us: shards(): jnp.einsum('xykr,xydkc->xydrc', own_block, images, preferred_element_type...]
    reshape x3 -> x0, local copies, waits for them, and re-layouts: 6.52 us -> none  [the longest x1 4.05 us: shards(): flat_terms = terms.reshape(cell_count * 5, block_size * block_size)]
    transpose x1 -> x0, local copies, waits for them, and re-layouts: 5.94 us -> none  [shards(): jnp.einsum('xykr,xydkc->xydrc', own_block, images, preferred_element_type...]
  transfers between devices with their start and end apart: 6 -> 4, of which waited for: 1 -> 0; matrix products, arithmetic and copies ran while one was open for 30% -> 1% of each run, Pallas kernels for 0% -> 4%
where the time goes in v1:
time: 115 us
  blocking collectives  90.8 us (79%)
  starting transfers between devices  11.1 us (10%)
  Pallas kernels  8.06 us (7%)
  local copies, waits for them, and re-layouts  4.04 us (4%)
    all_to_all x1, blocking collectives, shards(): lax.all_to_all(outgoing, 'gy', 0, 0, axis_index_groups=along, tiled=True)  78.2 us
    all_to_all x1, blocking collectives, shards(): lax.all_to_all(dense.reshape(across, owned * 32, 128), 'gy', 0, 0, axis_i...  12.6 us
    ppermute x1, starting transfers between devices, shards(): last_y = lax.ppermute(prolong[:, cy - 1], 'gy', up_y)  4.27 us
    pallas_call x1, Pallas kernels, shards(): pl.pallas_call(left_kernel, out_shape=(jax.ShapeDtypeStruct((cells, 5, 64...  4.04 us
    ppermute x1, starting transfers between devices, shards(): next_x = lax.ppermute(prolong[0], 'gx', down_x)  3.64 us
    pallas_call x1, Pallas kernels, shards(): pl.pallas_call(lambda *refs: partial_kernel(cx, cy, *refs), out_shape=jax...  2.41 us
    unnamed x12, local copies, waits for them, and re-layouts  2.37 us
  transfers between devices with their start and end apart: 4, of which 0 were waited for; matrix products, arithmetic and copies ran while one was open for 1% of the time, Pallas kernels for 4%

profile of v1, /device:TPU:24, one launch (start us, length us, event | category | flops | bytes accessed | tf_op | source)
XLA Modules:
  0.0 114.9 jit_solution(5816616052315795742)
XLA Ops:
  0.0 0.9 slice_bitcast_fusion
  0.9 1.9 %collective-permute-start.1 = (bf16[8,32,128]{2,1,0:T(8,128)(2,1)S(1)}, bf16[8,32,128]{2,1,0:T(8,128)(2,1)S(1)}, u32[]{:S(2)}, u32[]{:S(2)}) collective-permute-start(bf16[8,32,128]{2,1,0:T(8,128)(2,1)S(1)} %get-tuple-element.11), channel_id=1, source_target_pairs={{0,64},{64,128},{128,192},{192,256},{256,320},{320,384},{384,448},... | collective-permute-start | bytes 196616 | tf_op jit(solution)/shard_map/ppermute | solution.py:129
  2.8 3.6 %collective-permute-start = (bf16[8,32,128]{2,1,0:T(8,128)(2,1)S(1)}, bf16[8,32,128]{2,1,0:T(8,128)(2,1)S(1)}, u32[]{:S(2)}, u32[]{:S(2)}) collective-permute-start(bf16[8,32,128]{2,1,0:T(8,128)(2,1)S(1)} %get-tuple-element.12), channel_id=1, source_target_pairs={{64,0},{128,64},{192,128},{256,192},{320,256},{384,320},{448,384},... | collective-permute-start | bytes 196616 | tf_op jit(solution)/shard_map/ppermute | solution.py:128
  6.5 0.8 slice_bitcast_fusion.2
  7.3 4.3 %collective-permute-start.3 = (bf16[4,32,128]{2,1,0:T(8,128)(2,1)S(1)}, bf16[4,32,128]{2,1,0:T(8,128)(2,1)S(1)}, u32[]{:S(2)}, u32[]{:S(2)}) collective-permute-start(bf16[4,32,128]{2,1,0:T(8,128)(2,1)S(1)} %get-tuple-element.9), channel_id=1, source_target_pairs={{0,1},{1,2},{2,3},{3,4},{4,5},{5,6},{6,7},{7,8},{8,9},{9,10},{10,1... | collective-permute-start | bytes 98312 | tf_op jit(solution)/shard_map/ppermute | solution.py:127
  11.5 1.3 %collective-permute-start.2 = (bf16[4,32,128]{2,1,0:T(8,128)(2,1)S(1)}, bf16[4,32,128]{2,1,0:T(8,128)(2,1)S(1)}, u32[]{:S(2)}, u32[]{:S(2)}) collective-permute-start(bf16[4,32,128]{2,1,0:T(8,128)(2,1)S(1)} %get-tuple-element.10), channel_id=1, source_target_pairs={{1,0},{2,1},{3,2},{4,3},{5,4},{6,5},{7,6},{8,7},{9,8},{10,9},{11,1... | collective-permute-start | bytes 98312 | tf_op jit(solution)/shard_map/ppermute | solution.py:126
  12.8 0.0 copy-start
  12.8 0.9 copy-done
  13.8 0.0 copy-start.5
  13.8 1.4 %copy-done.5 = bf16[4,8,64,320]{3,2,1,0:T(8,128)(2,1)S(1)} copy-done((bf16[4,8,64,320]{3,2,1,0:T(8,128)(2,1)S(1)}, bf16[4,8,64,320]{3,2,1,0:T(8,128)(2,1)}, u32[]{:S(2)}) %copy-start.5) | copy-done | bytes 1310744
  15.2 0.0 copy-start.1
  15.2 0.0 copy-start.2
  15.2 0.0 copy-start.3
  15.2 0.0 copy-start.4
  15.2 4.0 %left_factor.1 = (bf16[32,5,64,64]{3,2,1,0:T(8,128)(2,1)S(1)}, bf16[32,64,128]{2,1,0:T(8,128)(2,1)S(1)}) custom-call(bf16[32,32,128]{2,1,0:T(8,128)(2,1)S(1)} %bitcast.22, bf16[32,64,320]{2,1,0:T(8,128)(2,1)S(1)} %bitcast.28), custom_call_target="tpu_custom_call" | custom-call | flops 671088640 | bytes 2880000 | tf_op jit(solution)/shard_map/left_factor/pallas_call | solution.py:131
  19.2 0.0 collective-permute-done.3.refs_5_
  19.3 0.0 collective-permute-done.2.refs_4_
  19.3 0.0 collective-permute-done.1.refs_3_
  19.3 0.0 collective-permute-done.refs_2_
  19.3 0.0 copy-done.1
  19.3 0.0 copy-done.2
  19.3 0.0 copy-done.3
  19.3 0.0 copy-done.4
  19.3 2.4 %partial_blocks.1 = bf16[16,272,128]{2,1,0:T(8,128)(2,1)S(1)} custom-call(bf16[32,5,64,64]{3,2,1,0:T(8,128)(2,1)S(1)} %get-tuple-element.7.refs_0_, bf16[32,64,128]{2,1,0:T(8,128)(2,1)S(1)} %get-tuple-element.8.refs_1_, bf16[8,32,128]{2,1,0:T(8,128)(2,1)S(1)} %collective-permute-done.refs_2_, bf16[8,32,128]{2,1,0:T(8,128)(2,1)S(1)} %collective-permute-done.1.refs_3_, ...), custom_call_target="tpu_custom_call" | custom-call | tf_op jit(solution)/shard_map/partial_blocks/pallas_call | solution.py:147
  21.7 78.2 %all_to_all.10.refs_0_ = bf16[16,272,128]{2,1,0:T(8,128)(2,1)S(1)} all-to-all(bf16[16,272,128]{2,1,0:T(8,128)(2,1)S(1)} %partial_blocks.1), channel_id=1, replica_groups={{0,1,2,3,4,5,6,7,8,9,10,11,12,13,14,15},{16,17,18,19,20,21,22,23,24,25,..., dimensions={0} | all-to-all | bytes 2228224 | tf_op jit(solution)/shard_map/all_to_all | solution.py:171
  100.0 1.6 %ring_sums.1 = bf16[64,32,128]{2,1,0:T(8,128)(2,1)S(1)} custom-call(bf16[16,272,128]{2,1,0:T(8,128)(2,1)S(1)} %all_to_all.10.refs_0_, s32[16,8]{1,0:T(8,128)S(1)} %bitcast.23), custom_call_target="tpu_custom_call" | custom-call | tf_op jit(solution)/shard_map/ring_sums/pallas_call | solution.py:174
  101.6 12.6 %all_to_all.11 = bf16[4,512,128]{2,1,0:T(8,128)(2,1)S(1)} all-to-all(bf16[4,512,128]{2,1,0:T(8,128)(2,1)S(1)} %bitcast.21), channel_id=1, replica_groups={{0,16,32,48},{1,17,33,49},{2,18,34,50},{3,19,35,51},{4,20,36,52},{5,21,..., dimensions={0} | all-to-all | bytes 1048576 | tf_op jit(solution)/shard_map/all_to_all | solution.py:183
  114.2 0.7 reduce_sum.12
  (1 shorter events, 0.0 us)
Async XLA Ops:
  0.9 18.4 %collective-permute-start.1 = (bf16[8,32,128]{2,1,0:T(8,128)(2,1)S(1)}, bf16[8,32,128]{2,1,0:T(8,128)(2,1)S(1)}, u32[]{:S(2)}, u32[]{:S(2)}) collective-permute-start(bf16[8,32,128]{2,1,0:T(8,128)(2,1)S(1)} %get-tuple-element.11), channel_id=1, source_target_pairs={{0,64},{64,128},{128,192},{192,256},{256,320},{320,384},{384,448},... | collective-permute-start | bytes 196616 | tf_op jit(solution)/shard_map/ppermute | solution.py:129
  2.8 16.5 %collective-permute-start = (bf16[8,32,128]{2,1,0:T(8,128)(2,1)S(1)}, bf16[8,32,128]{2,1,0:T(8,128)(2,1)S(1)}, u32[]{:S(2)}, u32[]{:S(2)}) collective-permute-start(bf16[8,32,128]{2,1,0:T(8,128)(2,1)S(1)} %get-tuple-element.12), channel_id=1, source_target_pairs={{64,0},{128,64},{192,128},{256,192},{320,256},{384,320},{448,384},... | collective-permute-start | bytes 196616 | tf_op jit(solution)/shard_map/ppermute | solution.py:128
  7.3 12.0 %collective-permute-start.3 = (bf16[4,32,128]{2,1,0:T(8,128)(2,1)S(1)}, bf16[4,32,128]{2,1,0:T(8,128)(2,1)S(1)}, u32[]{:S(2)}, u32[]{:S(2)}) collective-permute-start(bf16[4,32,128]{2,1,0:T(8,128)(2,1)S(1)} %get-tuple-element.9), channel_id=1, source_target_pairs={{0,1},{1,2},{2,3},{3,4},{4,5},{5,6},{6,7},{7,8},{8,9},{9,10},{10,1... | collective-permute-start | bytes 98312 | tf_op jit(solution)/shard_map/ppermute | solution.py:127
  11.5 7.7 %collective-permute-start.2 = (bf16[4,32,128]{2,1,0:T(8,128)(2,1)S(1)}, bf16[4,32,128]{2,1,0:T(8,128)(2,1)S(1)}, u32[]{:S(2)}, u32[]{:S(2)}) collective-permute-start(bf16[4,32,128]{2,1,0:T(8,128)(2,1)S(1)} %get-tuple-element.10), channel_id=1, source_target_pairs={{1,0},{2,1},{3,2},{4,3},{5,4},{6,5},{7,6},{8,7},{9,8},{10,9},{11,1... | collective-permute-start | bytes 98312 | tf_op jit(solution)/shard_map/ppermute | solution.py:126
  12.8 1.0 copy-start
  13.8 1.4 %copy-start.5 = (bf16[4,8,64,320]{3,2,1,0:T(8,128)(2,1)S(1)}, bf16[4,8,64,320]{3,2,1,0:T(8,128)(2,1)}, u32[]{:S(2)}) copy-start(bf16[4,8,64,320]{3,2,1,0:T(8,128)(2,1)} %param.6) | copy-start | bytes 3932164
  15.2 4.1 %copy-start.1 = (s32[4,8,5]{1,0,2:T(4,128)S(1)}, s32[4,8,5]{1,0,2:T(4,128)}, u32[]{:S(2)}) copy-start(s32[4,8,5]{1,0,2:T(4,128)} %param.9) | copy-start | bytes 1924
  15.2 4.1 %copy-start.2 = (s32[4,8,4]{1,2,0:T(4,128)S(1)}, s32[4,8,4]{1,2,0:T(4,128)}, u32[]{:S(2)}) copy-start(s32[4,8,4]{1,2,0:T(4,128)} %param.8) | copy-start | bytes 1540
  15.2 4.1 %copy-start.3 = (s32[1,32,1]{1,2,0:T(1,128)S(1)}, s32[1,32,1]{1,2,0:T(1,128)}, u32[]{:S(2)}) copy-start(s32[1,32,1]{1,2,0:T(1,128)} %param.10) | copy-start | bytes 388
  15.2 4.1 %copy-start.4 = (s32[1,32]{1,0:T(1,128)S(1)}, s32[1,32]{1,0:T(1,128)}, u32[]{:S(2)}) copy-start(s32[1,32]{1,0:T(1,128)} %param.11) | copy-start | bytes 388

commit v2 on v1

--- a/solution.py
+++ b/solution.py
@@ -7,6 +7,7 @@
 
 RING = 16
 SLOTS = 8
+FIRST = 4
 VMEM = pl.BlockSpec(memory_space=pltpu.VMEM)
 SMEM = pl.BlockSpec(memory_space=pltpu.SMEM)
 PARAMS = pltpu.CompilerParams(vmem_limit_bytes=40 * 1024 * 1024)
@@ -47,6 +48,7 @@
     owners_ref,
     targets_ref,
     out_ref,
+    late_ref,
     sums_ref,
     wide_ref,
     count_ref,
@@ -83,7 +85,8 @@
     row_id = lax.broadcasted_iota(jnp.int32, (RING, 128), 0)
     lane_id = lax.broadcasted_iota(jnp.int32, (RING, 128), 1)
     low = lax.broadcasted_iota(jnp.int32, (32, 128), 1) < 64
-    tags = jnp.full((RING, 128), 1.0, jnp.float32) * (RING * SLOTS)
+    tags = jnp.full((RING, 128), 128.0, jnp.float32)
+    most = jnp.int32(0)
     for e in range(count):
         owner = owners_ref[e]
         ring = owner % RING
@@ -92,21 +95,43 @@
         even = sums_ref[e, pl.ds(0, 32, stride=2), :]
         odd = sums_ref[e, pl.ds(1, 32, stride=2), :]
         block = jnp.where(low, even, pltpu.roll(odd, 64, 1)).astype(jnp.bfloat16)
-        out_ref[ring, pl.ds(pl.multiple_of(slot * 32, 32), 32), :] = block
+        most = jnp.maximum(most, slot)
+
+        @pl.when(slot < FIRST)
+        def _():
+            out_ref[ring, pl.ds(pl.multiple_of(slot * 32, 32), 32), :] = block
+
+        @pl.when(slot >= FIRST)
+        def _():
+            late_ref[ring, pl.ds(pl.multiple_of((slot - FIRST) * 32, 32), 32), :] = block
+
         tag = (owner // RING) * 16 + targets_ref[e]
         tags = jnp.where((row_id == ring) & (lane_id == slot), tag.astype(jnp.float32), tags)
+    late = (most >= FIRST).astype(jnp.float32)
+    tags = jnp.where(lane_id == SLOTS, late, tags)
     for ring in range(RING):
         row = jnp.broadcast_to(tags[ring : ring + 1, :], (16, 128))
-        out_ref[ring, SLOTS * 32 : SLOTS * 32 + 16, :] = row.astype(jnp.bfloat16)
-
-
-def gather_kernel(blocks, got_ref, tags_ref, out_ref, sums_ref):
+        out_ref[ring, FIRST * 32 : FIRST * 32 + 16, :] = row.astype(jnp.bfloat16)
+
+
+def gather_kernel(blocks, got_ref, late_ref, tags_ref, any_ref, out_ref, sums_ref):
     sums_ref[...] = jnp.zeros_like(sums_ref)
+
+    def add(ring, slot, from_ref, place):
+        tag = jnp.minimum(tags_ref[ring, slot], blocks)
+        piece = from_ref[ring, place * 32 : place * 32 + 32, :].astype(jnp.float32)
+        sums_ref[tag] = sums_ref[tag] + piece
+
     for ring in range(RING):
-        for slot in range(SLOTS):
-            tag = jnp.minimum(tags_ref[ring, slot], blocks)
-            piece = got_ref[ring, slot * 32 : slot * 32 + 32, :].astype(jnp.float32)
-            sums_ref[tag] = sums_ref[tag] + piece
+        for slot in range(FIRST):
+            add(ring, slot, got_ref, slot)
+
+    @pl.when(any_ref[0] != 0)
+    def _():
+        for ring in range(RING):
+            for slot in range(FIRST, SLOTS):
+                add(ring, slot, late_ref, slot - FIRST)
+
     out_ref[...] = sums_ref[:blocks].astype(jnp.bfloat16)
 
 
@@ -144,11 +169,14 @@
         name="left_factor",
     )(prolong.reshape(cells, 32, 128), couplings.reshape(cells, 64, 320))
 
-    outgoing = pl.pallas_call(
+    outgoing, outgoing_late = pl.pallas_call(
         lambda *refs: partial_kernel(cx, cy, *refs),
-        out_shape=jax.ShapeDtypeStruct((RING, SLOTS * 32 + 16, 128), jnp.bfloat16),
+        out_shape=(
+            jax.ShapeDtypeStruct((RING, FIRST * 32 + 16, 128), jnp.bfloat16),
+            jax.ShapeDtypeStruct((RING, (SLOTS - FIRST) * 32, 128), jnp.bfloat16),
+        ),
         in_specs=[VMEM] * 6 + [SMEM] * 4,
-        out_specs=VMEM,
+        out_specs=(VMEM, VMEM),
         scratch_shapes=[
             pltpu.VMEM((cells + 1, 64, 128), jnp.float32),
             pltpu.VMEM((4, 64, 128), jnp.float32),
@@ -168,18 +196,25 @@
         owners.reshape(cells),
         targets.reshape(cells),
     )
-    got = lax.all_to_all(outgoing, "gy", 0, 0, axis_index_groups=along, tiled=True)
-    tags = got[:, SLOTS * 32, :SLOTS].astype(jnp.int32)
+
+    def exchange(array):
+        return lax.all_to_all(array, "gy", 0, 0, axis_index_groups=along, tiled=True)
+
+    got = exchange(outgoing)
+    heads = got[:, FIRST * 32, : SLOTS + 1].astype(jnp.int32)
+    tags = heads[:, :SLOTS]
+    any_late = jnp.max(heads[:, SLOTS])
+    got_late = lax.cond(any_late > 0, exchange, lambda array: array, outgoing_late)
     blocks = across * owned
     dense = pl.pallas_call(
         lambda *refs: gather_kernel(blocks, *refs),
         out_shape=jax.ShapeDtypeStruct((blocks, 32, 128), jnp.bfloat16),
-        in_specs=[VMEM, SMEM],
+        in_specs=[VMEM, VMEM, SMEM, SMEM],
         out_specs=VMEM,
         scratch_shapes=[pltpu.VMEM((blocks + 1, 32, 128), jnp.float32)],
         compiler_params=PARAMS,
         name="ring_sums",
-    )(got, tags)
+    )(got, got_late, tags, any_late.reshape(1))
     pieces = lax.all_to_all(
         dense.reshape(across, owned * 32, 128), "gy", 0, 0, axis_index_groups=aside, tiled=True
     )

time: 115 us -> 129 us (1.12)
  blocking collectives: 90.8 us -> 100 us
  Pallas kernels: 8.06 us -> 10.7 us
    all_to_all x1 -> x2, blocking collectives: 78.2 us -> 88 us  [exchange(): lax.all_to_all(array, 'gy', 0, 0, axis_index_groups=along, tiled=True)]
    pallas_call x1, Pallas kernels: 2.41 us -> 4.47 us  [shards(): pl.pallas_call(lambda *refs: partial_kernel(cx, cy, *refs), out_shape=(ja...]
  transfers between devices with their start and end apart: 4 -> 4, of which waited for: 0 -> 0; matrix products, arithmetic and copies ran while one was open for 1% -> 1% of each run, Pallas kernels for 4% -> 3%
where the time goes in v2:
time: 129 us; the launch traced here: 128 us
  blocking collectives  100 us (78%)
  starting transfers between devices  11.1 us (9%)
  Pallas kernels  10.7 us (8%)
  local copies, waits for them, and re-layouts  4.13 us (3%)
  other arithmetic  1.46 us (1%)
    all_to_all x2, blocking collectives, exchange(): lax.all_to_all(array, 'gy', 0, 0, axis_index_groups=along, tiled=True)  88 us
    all_to_all x1, blocking collectives, shards(): lax.all_to_all(dense.reshape(across, owned * 32, 128), 'gy', 0, 0, axis_i...  12.2 us
    pallas_call x1, Pallas kernels, shards(): pl.pallas_call(lambda *refs: partial_kernel(cx, cy, *refs), out_shape=(ja...  4.47 us
    ppermute x1, starting transfers between devices, shards(): last_y = lax.ppermute(prolong[:, cy - 1], 'gy', up_y)  4.27 us
    pallas_call x1, Pallas kernels, shards(): pl.pallas_call(left_kernel, out_shape=(jax.ShapeDtypeStruct((cells, 5, 64...  4.04 us
    ppermute x1, starting transfers between devices, shards(): next_x = lax.ppermute(prolong[0], 'gx', down_x)  3.64 us
  transfers between devices with their start and end apart: 4, of which 0 were waited for; matrix products, arithmetic and copies ran while one was open for 1% of the time, Pallas kernels for 3%

profile of v2, /device:TPU:24, one launch (start us, length us, event | category | flops | bytes accessed | tf_op | source)
XLA Modules:
  0.0 128.4 jit_solution(15058587181998951130)
XLA Ops:
  0.0 0.0 copy-start.4
  0.0 0.0 copy-start.3
  0.0 0.0 copy-start.1
  0.0 0.0 copy-start.2
  0.0 0.9 slice_bitcast_fusion
  0.9 1.9 %collective-permute-start.1 = (bf16[8,32,128]{2,1,0:T(8,128)(2,1)S(1)}, bf16[8,32,128]{2,1,0:T(8,128)(2,1)S(1)}, u32[]{:S(2)}, u32[]{:S(2)}) collective-permute-start(bf16[8,32,128]{2,1,0:T(8,128)(2,1)S(1)} %get-tuple-element.20), channel_id=1, source_target_pairs={{0,64},{64,128},{128,192},{192,256},{256,320},{320,384},{384,448},... | collective-permute-start | bytes 196616 | tf_op jit(solution)/shard_map/ppermute | solution.py:154
  2.9 3.6 %collective-permute-start = (bf16[8,32,128]{2,1,0:T(8,128)(2,1)S(1)}, bf16[8,32,128]{2,1,0:T(8,128)(2,1)S(1)}, u32[]{:S(2)}, u32[]{:S(2)}) collective-permute-start(bf16[8,32,128]{2,1,0:T(8,128)(2,1)S(1)} %get-tuple-element.21), channel_id=1, source_target_pairs={{64,0},{128,64},{192,128},{256,192},{320,256},{384,320},{448,384},... | collective-permute-start | bytes 196616 | tf_op jit(solution)/shard_map/ppermute | solution.py:153
  6.5 0.8 slice_bitcast_fusion.2
  7.3 4.3 %collective-permute-start.3 = (bf16[4,32,128]{2,1,0:T(8,128)(2,1)S(1)}, bf16[4,32,128]{2,1,0:T(8,128)(2,1)S(1)}, u32[]{:S(2)}, u32[]{:S(2)}) collective-permute-start(bf16[4,32,128]{2,1,0:T(8,128)(2,1)S(1)} %get-tuple-element.18), channel_id=1, source_target_pairs={{0,1},{1,2},{2,3},{3,4},{4,5},{5,6},{6,7},{7,8},{8,9},{9,10},{10,1... | collective-permute-start | bytes 98312 | tf_op jit(solution)/shard_map/ppermute | solution.py:152
  11.6 1.3 %collective-permute-start.2 = (bf16[4,32,128]{2,1,0:T(8,128)(2,1)S(1)}, bf16[4,32,128]{2,1,0:T(8,128)(2,1)S(1)}, u32[]{:S(2)}, u32[]{:S(2)}) collective-permute-start(bf16[4,32,128]{2,1,0:T(8,128)(2,1)S(1)} %get-tuple-element.19), channel_id=1, source_target_pairs={{1,0},{2,1},{3,2},{4,3},{5,4},{6,5},{7,6},{8,7},{9,8},{10,9},{11,1... | collective-permute-start | bytes 98312 | tf_op jit(solution)/shard_map/ppermute | solution.py:151
  12.9 0.0 copy-start
  12.9 0.9 copy-done
  13.8 0.0 copy-start.5
  13.8 1.4 %copy-done.5 = bf16[4,8,64,320]{3,2,1,0:T(8,128)(2,1)S(1)} copy-done((bf16[4,8,64,320]{3,2,1,0:T(8,128)(2,1)S(1)}, bf16[4,8,64,320]{3,2,1,0:T(8,128)(2,1)}, u32[]{:S(2)}) %copy-start.5) | copy-done | bytes 1310744
  15.2 4.0 %left_factor.1 = (bf16[32,5,64,64]{3,2,1,0:T(8,128)(2,1)S(1)}, bf16[32,64,128]{2,1,0:T(8,128)(2,1)S(1)}) custom-call(bf16[32,32,128]{2,1,0:T(8,128)(2,1)S(1)} %bitcast.28, bf16[32,64,320]{2,1,0:T(8,128)(2,1)S(1)} %bitcast.34), custom_call_target="tpu_custom_call" | custom-call | flops 671088640 | bytes 2880000 | tf_op jit(solution)/shard_map/left_factor/pallas_call | solution.py:156
  19.3 0.0 collective-permute-done.3.refs_5_
  19.3 0.0 collective-permute-done.2.refs_4_
  19.3 0.0 collective-permute-done.1.refs_3_
  19.3 0.0 collective-permute-done.refs_2_
  19.3 0.0 copy-done.4
  19.3 0.0 copy-done.3
  19.4 0.0 copy-done.1
  19.4 0.0 copy-done.2
  19.4 4.5 %partial_blocks.1 = (bf16[16,144,128]{2,1,0:T(8,128)(2,1)S(1)}, bf16[16,128,128]{2,1,0:T(8,128)(2,1)S(1)}) custom-call(bf16[32,5,64,64]{3,2,1,0:T(8,128)(2,1)S(1)} %get-tuple-element.14.refs_0_, bf16[32,64,128]{2,1,0:T(8,128)(2,1)S(1)} %get-tuple-element.15.refs_1_, bf16[8,32,128]{2,1,0:T(8,128)(2,1)S(1)} %collective-permute-done.refs_2_, ...), custom_call_target="tpu_custom_call" | custom-call | tf_op jit(solution)/shard_map/partial_blocks/pallas_call | solution.py:172
  23.8 55.7 %all_to_all.15.refs_0_ = bf16[16,144,128]{2,1,0:T(8,128)(2,1)S(1)} all-to-all(bf16[16,144,128]{2,1,0:T(8,128)(2,1)S(1)} %get-tuple-element.16), channel_id=1, replica_groups={{0,1,2,3,4,5,6,7,8,9,10,11,12,13,14,15},{16,17,18,19,20,21,22,23,24,25,..., dimensions={0} | all-to-all | bytes 1179648 | tf_op jit(solution)/shard_map/all_to_all | solution.py:201
  79.6 0.7 slice_reduce_fusion
  81.0 32.3 %conditional.1 = (bf16[16,128,128]{2,1,0:T(8,128)(2,1)S(1)}) conditional(s32[]{:T(128)} %convert_element_type.13, bf16[16,128,128]{2,1,0:T(8,128)(2,1)S(1)} %get-tuple-element.17, bf16[16,128,128]{2,1,0:T(8,128)(2,1)S(1)} %get-tuple-element.17), branch_computations={%region_1.0_spmd, %region_2.0_spmd} | conditional | bytes 2097160 | solution.py:207
  81.0 32.2 %all_to_all.14 = bf16[16,128,128]{2,1,0:T(8,128)(2,1)S(1)} all-to-all(bf16[16,128,128]{2,1,0:T(8,128)(2,1)S(1)} %copy.22), channel_id=1, replica_groups={{0,1,2,3,4,5,6,7,8,9,10,11,12,13,14,15},{16,17,18,19,20,21,22,23,24,25,..., dimensions={0} | all-to-all | bytes 1048576 | tf_op jit(solution)/shard_map/cond/branch_1_fun/all_to_all | solution.py:201
  113.3 2.2 %ring_sums.1 = bf16[64,32,128]{2,1,0:T(8,128)(2,1)S(1)} custom-call(bf16[16,144,128]{2,1,0:T(8,128)(2,1)S(1)} %all_to_all.15.refs_0_, bf16[16,128,128]{2,1,0:T(8,128)(2,1)S(1)} %get-tuple-element.22.refs_1_, s32[16,8]{1,0:T(8,128)S(1)} %bitcast.29, s32[1]{0:T(128)} %bitcast.12.refs_3_), custom_call_target="tpu_custom_call" | custom-call | tf_op jit(solution)/shard_map/ring_sums/pallas_call | solution.py:209
  115.5 12.2 %all_to_all.16 = bf16[4,512,128]{2,1,0:T(8,128)(2,1)S(1)} all-to-all(bf16[4,512,128]{2,1,0:T(8,128)(2,1)S(1)} %bitcast.27), channel_id=1, replica_groups={{0,16,32,48},{1,17,33,49},{2,18,34,50},{3,19,35,51},{4,20,36,52},{5,21,..., dimensions={0} | all-to-all | bytes 1048576 | tf_op jit(solution)/shard_map/all_to_all | solution.py:218
  127.7 0.7 reduce_sum.12
  (3 shorter events, 0.1 us)
Async XLA Ops:
  0.0 19.3 %copy-start.4 = (s32[1,32]{1,0:T(1,128)S(1)}, s32[1,32]{1,0:T(1,128)}, u32[]{:S(2)}) copy-start(s32[1,32]{1,0:T(1,128)} %param.13) | copy-start | bytes 388
  0.0 19.3 %copy-start.3 = (s32[1,32,1]{1,2,0:T(1,128)S(1)}, s32[1,32,1]{1,2,0:T(1,128)}, u32[]{:S(2)}) copy-start(s32[1,32,1]{1,2,0:T(1,128)} %param.12) | copy-start | bytes 388
  0.0 19.4 %copy-start.1 = (s32[4,8,5]{1,0,2:T(4,128)S(1)}, s32[4,8,5]{1,0,2:T(4,128)}, u32[]{:S(2)}) copy-start(s32[4,8,5]{1,0,2:T(4,128)} %param.11) | copy-start | bytes 1924
  0.0 19.4 %copy-start.2 = (s32[4,8,4]{1,2,0:T(4,128)S(1)}, s32[4,8,4]{1,2,0:T(4,128)}, u32[]{:S(2)}) copy-start(s32[4,8,4]{1,2,0:T(4,128)} %param.10) | copy-start | bytes 1540
  0.9 18.4 %collective-permute-start.1 = (bf16[8,32,128]{2,1,0:T(8,128)(2,1)S(1)}, bf16[8,32,128]{2,1,0:T(8,128)(2,1)S(1)}, u32[]{:S(2)}, u32[]{:S(2)}) collective-permute-start(bf16[8,32,128]{2,1,0:T(8,128)(2,1)S(1)} %get-tuple-element.20), channel_id=1, source_target_pairs={{0,64},{64,128},{128,192},{192,256},{256,320},{320,384},{384,448},... | collective-permute-start | bytes 196616 | tf_op jit(solution)/shard_map/ppermute | solution.py:154
  2.9 16.5 %collective-permute-start = (bf16[8,32,128]{2,1,0:T(8,128)(2,1)S(1)}, bf16[8,32,128]{2,1,0:T(8,128)(2,1)S(1)}, u32[]{:S(2)}, u32[]{:S(2)}) collective-permute-start(bf16[8,32,128]{2,1,0:T(8,128)(2,1)S(1)} %get-tuple-element.21), channel_id=1, source_target_pairs={{64,0},{128,64},{192,128},{256,192},{320,256},{384,320},{448,384},... | collective-permute-start | bytes 196616 | tf_op jit(solution)/shard_map/ppermute | solution.py:153
  7.3 12.0 %collective-permute-start.3 = (bf16[4,32,128]{2,1,0:T(8,128)(2,1)S(1)}, bf16[4,32,128]{2,1,0:T(8,128)(2,1)S(1)}, u32[]{:S(2)}, u32[]{:S(2)}) collective-permute-start(bf16[4,32,128]{2,1,0:T(8,128)(2,1)S(1)} %get-tuple-element.18), channel_id=1, source_target_pairs={{0,1},{1,2},{2,3},{3,4},{4,5},{5,6},{6,7},{7,8},{8,9},{9,10},{10,1... | collective-permute-start | bytes 98312 | tf_op jit(solution)/shard_map/ppermute | solution.py:152
  11.6 7.7 %collective-permute-start.2 = (bf16[4,32,128]{2,1,0:T(8,128)(2,1)S(1)}, bf16[4,32,128]{2,1,0:T(8,128)(2,1)S(1)}, u32[]{:S(2)}, u32[]{:S(2)}) collective-permute-start(bf16[4,32,128]{2,1,0:T(8,128)(2,1)S(1)} %get-tuple-element.19), channel_id=1, source_target_pairs={{1,0},{2,1},{3,2},{4,3},{5,4},{6,5},{7,6},{8,7},{9,8},{10,9},{11,1... | collective-permute-start | bytes 98312 | tf_op jit(solution)/shard_map/ppermute | solution.py:151
  12.9 1.0 copy-start
  13.8 1.4 %copy-start.5 = (bf16[4,8,64,320]{3,2,1,0:T(8,128)(2,1)S(1)}, bf16[4,8,64,320]{3,2,1,0:T(8,128)(2,1)}, u32[]{:S(2)}) copy-start(bf16[4,8,64,320]{3,2,1,0:T(8,128)(2,1)} %param.8) | copy-start | bytes 3932164

commit v3 on v2

--- a/solution.py
+++ b/solution.py
@@ -7,7 +7,7 @@
 
 RING = 16
 SLOTS = 8
-FIRST = 4
+FIRST = 6
 VMEM = pl.BlockSpec(memory_space=pltpu.VMEM)
 SMEM = pl.BlockSpec(memory_space=pltpu.SMEM)
 PARAMS = pltpu.CompilerParams(vmem_limit_bytes=40 * 1024 * 1024)

time: 129 us -> 105 us (0.81)
  blocking collectives: 100 us -> 76.7 us
    all_to_all x2 -> x1, blocking collectives: 88 us -> 64.5 us  [exchange(): lax.all_to_all(array, 'gy', 0, 0, axis_index_groups=along, tiled=True)]
  transfers between devices with their start and end apart: 4 -> 4, of which waited for: 0 -> 0; matrix products, arithmetic and copies ran while one was open for 1% -> 1% of each run, Pallas kernels for 3% -> 4%
where the time goes in v3:
time: 105 us
  blocking collectives  76.7 us (73%)
  starting transfers between devices  11.1 us (11%)
  Pallas kernels  10.5 us (10%)
  local copies, waits for them, and re-layouts  4.09 us (4%)
  other arithmetic  1.46 us (1%)
    all_to_all x1, blocking collectives, exchange(): lax.all_to_all(array, 'gy', 0, 0, axis_index_groups=along, tiled=True)  64.5 us
    all_to_all x1, blocking collectives, shards(): lax.all_to_all(dense.reshape(across, owned * 32, 128), 'gy', 0, 0, axis_i...  12.2 us
    pallas_call x1, Pallas kernels, shards(): pl.pallas_call(lambda *refs: partial_kernel(cx, cy, *refs), out_shape=(ja...  4.47 us
    ppermute x1, starting transfers between devices, shards(): last_y = lax.ppermute(prolong[:, cy - 1], 'gy', up_y)  4.27 us
    pallas_call x1, Pallas kernels, shards(): pl.pallas_call(left_kernel, out_shape=(jax.ShapeDtypeStruct((cells, 5, 64...  4.04 us
    ppermute x1, starting transfers between devices, shards(): next_x = lax.ppermute(prolong[0], 'gx', down_x)  3.64 us
    unnamed x12, local copies, waits for them, and re-layouts  2.37 us
  transfers between devices with their start and end apart: 4, of which 0 were waited for; matrix products, arithmetic and copies ran while one was open for 1% of the time, Pallas kernels for 4%

profile of v3, /device:TPU:24, one launch (start us, length us, event | category | flops | bytes accessed | tf_op | source)
XLA Modules:
  0.0 104.7 jit_solution(3693161487351330574)
XLA Ops:
  0.0 0.0 copy-start.4
  0.0 0.0 copy-start.3
  0.0 0.0 copy-start.1
  0.0 0.0 copy-start.2
  0.0 0.9 slice_bitcast_fusion
  0.9 1.9 %collective-permute-start.1 = (bf16[8,32,128]{2,1,0:T(8,128)(2,1)S(1)}, bf16[8,32,128]{2,1,0:T(8,128)(2,1)S(1)}, u32[]{:S(2)}, u32[]{:S(2)}) collective-permute-start(bf16[8,32,128]{2,1,0:T(8,128)(2,1)S(1)} %get-tuple-element.20), channel_id=1, source_target_pairs={{0,64},{64,128},{128,192},{192,256},{256,320},{320,384},{384,448},... | collective-permute-start | bytes 196616 | tf_op jit(solution)/shard_map/ppermute | solution.py:154
  2.9 3.6 %collective-permute-start = (bf16[8,32,128]{2,1,0:T(8,128)(2,1)S(1)}, bf16[8,32,128]{2,1,0:T(8,128)(2,1)S(1)}, u32[]{:S(2)}, u32[]{:S(2)}) collective-permute-start(bf16[8,32,128]{2,1,0:T(8,128)(2,1)S(1)} %get-tuple-element.21), channel_id=1, source_target_pairs={{64,0},{128,64},{192,128},{256,192},{320,256},{384,320},{448,384},... | collective-permute-start | bytes 196616 | tf_op jit(solution)/shard_map/ppermute | solution.py:153
  6.5 0.8 slice_bitcast_fusion.2
  7.3 4.3 %collective-permute-start.3 = (bf16[4,32,128]{2,1,0:T(8,128)(2,1)S(1)}, bf16[4,32,128]{2,1,0:T(8,128)(2,1)S(1)}, u32[]{:S(2)}, u32[]{:S(2)}) collective-permute-start(bf16[4,32,128]{2,1,0:T(8,128)(2,1)S(1)} %get-tuple-element.18), channel_id=1, source_target_pairs={{0,1},{1,2},{2,3},{3,4},{4,5},{5,6},{6,7},{7,8},{8,9},{9,10},{10,1... | collective-permute-start | bytes 98312 | tf_op jit(solution)/shard_map/ppermute | solution.py:152
  11.6 1.3 %collective-permute-start.2 = (bf16[4,32,128]{2,1,0:T(8,128)(2,1)S(1)}, bf16[4,32,128]{2,1,0:T(8,128)(2,1)S(1)}, u32[]{:S(2)}, u32[]{:S(2)}) collective-permute-start(bf16[4,32,128]{2,1,0:T(8,128)(2,1)S(1)} %get-tuple-element.19), channel_id=1, source_target_pairs={{1,0},{2,1},{3,2},{4,3},{5,4},{6,5},{7,6},{8,7},{9,8},{10,9},{11,1... | collective-permute-start | bytes 98312 | tf_op jit(solution)/shard_map/ppermute | solution.py:151
  12.9 0.0 copy-start
  12.9 0.9 copy-done
  13.8 0.0 copy-start.5
  13.8 1.4 %copy-done.5 = bf16[4,8,64,320]{3,2,1,0:T(8,128)(2,1)S(1)} copy-done((bf16[4,8,64,320]{3,2,1,0:T(8,128)(2,1)S(1)}, bf16[4,8,64,320]{3,2,1,0:T(8,128)(2,1)}, u32[]{:S(2)}) %copy-start.5) | copy-done | bytes 1310744
  15.2 4.0 %left_factor.1 = (bf16[32,5,64,64]{3,2,1,0:T(8,128)(2,1)S(1)}, bf16[32,64,128]{2,1,0:T(8,128)(2,1)S(1)}) custom-call(bf16[32,32,128]{2,1,0:T(8,128)(2,1)S(1)} %bitcast.28, bf16[32,64,320]{2,1,0:T(8,128)(2,1)S(1)} %bitcast.34), custom_call_target="tpu_custom_call" | custom-call | flops 671088640 | bytes 2880000 | tf_op jit(solution)/shard_map/left_factor/pallas_call | solution.py:156
  19.3 0.0 collective-permute-done.3.refs_5_
  19.3 0.0 collective-permute-done.2.refs_4_
  19.3 0.0 collective-permute-done.1.refs_3_
  19.3 0.0 collective-permute-done.refs_2_
  19.3 0.0 copy-done.4
  19.3 0.0 copy-done.3
  19.4 0.0 copy-done.1
  19.4 0.0 copy-done.2
  19.4 4.5 %partial_blocks.1 = (bf16[16,208,128]{2,1,0:T(8,128)(2,1)S(1)}, bf16[16,64,128]{2,1,0:T(8,128)(2,1)S(1)}) custom-call(bf16[32,5,64,64]{3,2,1,0:T(8,128)(2,1)S(1)} %get-tuple-element.14.refs_0_, bf16[32,64,128]{2,1,0:T(8,128)(2,1)S(1)} %get-tuple-element.15.refs_1_, bf16[8,32,128]{2,1,0:T(8,128)(2,1)S(1)} %collective-permute-done.refs_2_, ...), custom_call_target="tpu_custom_call" | custom-call | tf_op jit(solution)/shard_map/partial_blocks/pallas_call | solution.py:172
  23.8 64.5 %all_to_all.15.refs_0_ = bf16[16,208,128]{2,1,0:T(8,128)(2,1)S(1)} all-to-all(bf16[16,208,128]{2,1,0:T(8,128)(2,1)S(1)} %get-tuple-element.16), channel_id=1, replica_groups={{0,1,2,3,4,5,6,7,8,9,10,11,12,13,14,15},{16,17,18,19,20,21,22,23,24,25,..., dimensions={0} | all-to-all | bytes 1703936 | tf_op jit(solution)/shard_map/all_to_all | solution.py:201
  88.4 0.7 slice_reduce_fusion
  89.8 2.0 %ring_sums.1 = bf16[64,32,128]{2,1,0:T(8,128)(2,1)S(1)} custom-call(bf16[16,208,128]{2,1,0:T(8,128)(2,1)S(1)} %all_to_all.15.refs_0_, bf16[16,64,128]{2,1,0:T(8,128)(2,1)S(1)} %get-tuple-element.22.refs_1_, s32[16,8]{1,0:T(8,128)S(1)} %bitcast.29, s32[1]{0:T(128)} %bitcast.12.refs_3_), custom_call_target="tpu_custom_call" | custom-call | tf_op jit(solution)/shard_map/ring_sums/pallas_call | solution.py:209
  91.8 12.2 %all_to_all.16 = bf16[4,512,128]{2,1,0:T(8,128)(2,1)S(1)} all-to-all(bf16[4,512,128]{2,1,0:T(8,128)(2,1)S(1)} %bitcast.27), channel_id=1, replica_groups={{0,16,32,48},{1,17,33,49},{2,18,34,50},{3,19,35,51},{4,20,36,52},{5,21,..., dimensions={0} | all-to-all | bytes 1048576 | tf_op jit(solution)/shard_map/all_to_all | solution.py:218
  104.0 0.7 reduce_sum.12
  (3 shorter events, 0.0 us)
Async XLA Ops:
  0.0 19.3 %copy-start.4 = (s32[1,32]{1,0:T(1,128)S(1)}, s32[1,32]{1,0:T(1,128)}, u32[]{:S(2)}) copy-start(s32[1,32]{1,0:T(1,128)} %param.13) | copy-start | bytes 388
  0.0 19.3 %copy-start.3 = (s32[1,32,1]{1,2,0:T(1,128)S(1)}, s32[1,32,1]{1,2,0:T(1,128)}, u32[]{:S(2)}) copy-start(s32[1,32,1]{1,2,0:T(1,128)} %param.12) | copy-start | bytes 388
  0.0 19.4 %copy-start.1 = (s32[4,8,5]{1,0,2:T(4,128)S(1)}, s32[4,8,5]{1,0,2:T(4,128)}, u32[]{:S(2)}) copy-start(s32[4,8,5]{1,0,2:T(4,128)} %param.11) | copy-start | bytes 1924
  0.0 19.4 %copy-start.2 = (s32[4,8,4]{1,2,0:T(4,128)S(1)}, s32[4,8,4]{1,2,0:T(4,128)}, u32[]{:S(2)}) copy-start(s32[4,8,4]{1,2,0:T(4,128)} %param.10) | copy-start | bytes 1540
  0.9 18.4 %collective-permute-start.1 = (bf16[8,32,128]{2,1,0:T(8,128)(2,1)S(1)}, bf16[8,32,128]{2,1,0:T(8,128)(2,1)S(1)}, u32[]{:S(2)}, u32[]{:S(2)}) collective-permute-start(bf16[8,32,128]{2,1,0:T(8,128)(2,1)S(1)} %get-tuple-element.20), channel_id=1, source_target_pairs={{0,64},{64,128},{128,192},{192,256},{256,320},{320,384},{384,448},... | collective-permute-start | bytes 196616 | tf_op jit(solution)/shard_map/ppermute | solution.py:154
  2.9 16.5 %collective-permute-start = (bf16[8,32,128]{2,1,0:T(8,128)(2,1)S(1)}, bf16[8,32,128]{2,1,0:T(8,128)(2,1)S(1)}, u32[]{:S(2)}, u32[]{:S(2)}) collective-permute-start(bf16[8,32,128]{2,1,0:T(8,128)(2,1)S(1)} %get-tuple-element.21), channel_id=1, source_target_pairs={{64,0},{128,64},{192,128},{256,192},{320,256},{384,320},{448,384},... | collective-permute-start | bytes 196616 | tf_op jit(solution)/shard_map/ppermute | solution.py:153
  7.3 12.0 %collective-permute-start.3 = (bf16[4,32,128]{2,1,0:T(8,128)(2,1)S(1)}, bf16[4,32,128]{2,1,0:T(8,128)(2,1)S(1)}, u32[]{:S(2)}, u32[]{:S(2)}) collective-permute-start(bf16[4,32,128]{2,1,0:T(8,128)(2,1)S(1)} %get-tuple-element.18), channel_id=1, source_target_pairs={{0,1},{1,2},{2,3},{3,4},{4,5},{5,6},{6,7},{7,8},{8,9},{9,10},{10,1... | collective-permute-start | bytes 98312 | tf_op jit(solution)/shard_map/ppermute | solution.py:152
  11.6 7.7 %collective-permute-start.2 = (bf16[4,32,128]{2,1,0:T(8,128)(2,1)S(1)}, bf16[4,32,128]{2,1,0:T(8,128)(2,1)S(1)}, u32[]{:S(2)}, u32[]{:S(2)}) collective-permute-start(bf16[4,32,128]{2,1,0:T(8,128)(2,1)S(1)} %get-tuple-element.19), channel_id=1, source_target_pairs={{1,0},{2,1},{3,2},{4,3},{5,4},{6,5},{7,6},{8,7},{9,8},{10,9},{11,1... | collective-permute-start | bytes 98312 | tf_op jit(solution)/shard_map/ppermute | solution.py:151
  12.9 1.0 copy-start
  13.8 1.4 %copy-start.5 = (bf16[4,8,64,320]{3,2,1,0:T(8,128)(2,1)S(1)}, bf16[4,8,64,320]{3,2,1,0:T(8,128)(2,1)}, u32[]{:S(2)}) copy-start(bf16[4,8,64,320]{3,2,1,0:T(8,128)(2,1)} %param.8) | copy-start | bytes 3932164

commit v4 on v1

--- a/solution.py
+++ b/solution.py
@@ -7,6 +7,7 @@
 
 RING = 16
 SLOTS = 8
+FIRST = 6
 VMEM = pl.BlockSpec(memory_space=pltpu.VMEM)
 SMEM = pl.BlockSpec(memory_space=pltpu.SMEM)
 PARAMS = pltpu.CompilerParams(vmem_limit_bytes=40 * 1024 * 1024)
@@ -46,11 +47,10 @@
     present_ref,
     owners_ref,
     targets_ref,
-    out_ref,
-    sums_ref,
-    wide_ref,
-    count_ref,
+    place_ref,
+    *rest,
 ):
+    out_refs, (late_ref, sums_ref, wide_ref, slots_ref, count_ref) = rest[:RING], rest[RING:]
     count = cx * cy
     sums_ref[...] = jnp.zeros_like(sums_ref)
 
@@ -78,35 +78,56 @@
     for x in range(cx):
         add(unpacked(last_y_ref[x], wide_ref.at[x % 4]), [(x, 0, 4)])
 
+    place = place_ref[0]
     for ring in range(RING):
         count_ref[ring] = 0
     row_id = lax.broadcasted_iota(jnp.int32, (RING, 128), 0)
     lane_id = lax.broadcasted_iota(jnp.int32, (RING, 128), 1)
     low = lax.broadcasted_iota(jnp.int32, (32, 128), 1) < 64
-    tags = jnp.full((RING, 128), 1.0, jnp.float32) * (RING * SLOTS)
+    tags = jnp.full((RING, 128), 128.0, jnp.float32)
+    most = jnp.int32(0)
     for e in range(count):
         owner = owners_ref[e]
-        ring = owner % RING
+        ring = (owner - place + RING) % RING
         slot = count_ref[ring]
         count_ref[ring] = slot + 1
         even = sums_ref[e, pl.ds(0, 32, stride=2), :]
         odd = sums_ref[e, pl.ds(1, 32, stride=2), :]
         block = jnp.where(low, even, pltpu.roll(odd, 64, 1)).astype(jnp.bfloat16)
-        out_ref[ring, pl.ds(pl.multiple_of(slot * 32, 32), 32), :] = block
+        most = jnp.maximum(most, slot)
+
+        slots_ref[ring, pl.ds(pl.multiple_of(slot * 32, 32), 32), :] = block
         tag = (owner // RING) * 16 + targets_ref[e]
         tags = jnp.where((row_id == ring) & (lane_id == slot), tag.astype(jnp.float32), tags)
+    late = (most >= FIRST).astype(jnp.float32)
+    tags = jnp.where(lane_id == SLOTS, late, tags)
     for ring in range(RING):
         row = jnp.broadcast_to(tags[ring : ring + 1, :], (16, 128))
-        out_ref[ring, SLOTS * 32 : SLOTS * 32 + 16, :] = row.astype(jnp.bfloat16)
-
-
-def gather_kernel(blocks, got_ref, tags_ref, out_ref, sums_ref):
+        out_refs[ring][: FIRST * 32, :] = slots_ref[ring, : FIRST * 32, :]
+        out_refs[ring][FIRST * 32 :, :] = row.astype(jnp.bfloat16)
+        late_ref[(ring + place) % RING] = slots_ref[ring, FIRST * 32 :, :]
+
+
+def gather_kernel(blocks, place_ref, tags_ref, any_ref, late_ref, *rest):
+    got_refs, (out_ref, sums_ref) = rest[:RING], rest[RING:]
     sums_ref[...] = jnp.zeros_like(sums_ref)
+
+    def add(tag, piece):
+        tag = jnp.minimum(tag, blocks)
+        sums_ref[tag] = sums_ref[tag] + piece.astype(jnp.float32)
+
     for ring in range(RING):
-        for slot in range(SLOTS):
-            tag = jnp.minimum(tags_ref[ring, slot], blocks)
-            piece = got_ref[ring, slot * 32 : slot * 32 + 32, :].astype(jnp.float32)
-            sums_ref[tag] = sums_ref[tag] + piece
+        for slot in range(FIRST):
+            add(tags_ref[ring, slot], got_refs[ring][slot * 32 : slot * 32 + 32, :])
+
+    @pl.when(any_ref[0] != 0)
+    def _():
+        for source in range(RING):
+            ring = (place_ref[0] - source + RING) % RING
+            for slot in range(FIRST, SLOTS):
+                start = (slot - FIRST) * 32
+                add(tags_ref[ring, slot], late_ref[source, start : start + 32, :])
+
     out_ref[...] = sums_ref[:blocks].astype(jnp.bfloat16)
 
 
@@ -144,14 +165,17 @@
         name="left_factor",
     )(prolong.reshape(cells, 32, 128), couplings.reshape(cells, 64, 320))
 
-    outgoing = pl.pallas_call(
+    place = (lax.axis_index("gy") % RING).astype(jnp.int32).reshape(1)
+    *outgoing, outgoing_late = pl.pallas_call(
         lambda *refs: partial_kernel(cx, cy, *refs),
-        out_shape=jax.ShapeDtypeStruct((RING, SLOTS * 32 + 16, 128), jnp.bfloat16),
-        in_specs=[VMEM] * 6 + [SMEM] * 4,
-        out_specs=VMEM,
+        out_shape=(jax.ShapeDtypeStruct((FIRST * 32 + 16, 128), jnp.bfloat16),) * RING
+        + (jax.ShapeDtypeStruct((RING, (SLOTS - FIRST) * 32, 128), jnp.bfloat16),),
+        in_specs=[VMEM] * 6 + [SMEM] * 5,
+        out_specs=(VMEM,) * (RING + 1),
         scratch_shapes=[
             pltpu.VMEM((cells + 1, 64, 128), jnp.float32),
             pltpu.VMEM((4, 64, 128), jnp.float32),
+            pltpu.VMEM((RING, SLOTS * 32, 128), jnp.bfloat16),
             pltpu.SMEM((RING,), jnp.int32),
         ],
         compiler_params=PARAMS,
@@ -167,19 +191,32 @@
         jnp.transpose(present, (0, 2, 1)),
         owners.reshape(cells),
         targets.reshape(cells),
-    )
-    got = lax.all_to_all(outgoing, "gy", 0, 0, axis_index_groups=along, tiled=True)
-    tags = got[:, SLOTS * 32, :SLOTS].astype(jnp.int32)
+        place,
+    )
+
+    got = [outgoing[0]] + [None] * (RING - 1)
+    for step in sorted(range(1, RING), key=lambda n: -min(n, RING - n)):
+        pairs = [(ring[z], ring[(z + step) % RING]) for ring in along for z in range(RING)]
+        got[step] = lax.ppermute(outgoing[step], "gy", pairs)
+    heads = jnp.stack([g[FIRST * 32, : SLOTS + 1] for g in got]).astype(jnp.int32)
+    tags = heads[:, :SLOTS]
+    any_late = jnp.max(heads[:, SLOTS])
+    got_late = lax.cond(
+        any_late > 0,
+        lambda array: lax.all_to_all(array, "gy", 0, 0, axis_index_groups=along, tiled=True),
+        lambda array: array,
+        outgoing_late,
+    )
     blocks = across * owned
     dense = pl.pallas_call(
         lambda *refs: gather_kernel(blocks, *refs),
         out_shape=jax.ShapeDtypeStruct((blocks, 32, 128), jnp.bfloat16),
-        in_specs=[VMEM, SMEM],
+        in_specs=[SMEM] * 3 + [VMEM] * (RING + 1),
         out_specs=VMEM,
         scratch_shapes=[pltpu.VMEM((blocks + 1, 32, 128), jnp.float32)],
         compiler_params=PARAMS,
         name="ring_sums",
-    )(got, tags)
+    )(place, tags, any_late.reshape(1), got_late, *got)
     pieces = lax.all_to_all(
         dense.reshape(across, owned * 32, 128), "gy", 0, 0, axis_index_groups=aside, tiled=True
     )

time: 115 us -> 135 us (1.17)
  starting transfers between devices: 11.1 us -> 100 us
  blocking collectives: 90.8 us -> 14.1 us
  waiting for transfers between devices: 0.01 us -> 4.75 us
    ppermute x0 -> x15, starting transfers between devices: none -> 89.1 us  [shards(): got[step] = lax.ppermute(outgoing[step], 'gy', pairs)]
    all_to_all x1 -> x0, blocking collectives: 78.2 us -> none  [shards(): lax.all_to_all(outgoing, 'gy', 0, 0, axis_index_groups=along, tiled=True)]
    ppermute x0 -> x15, waiting for transfers between devices: none -> 4.74 us  [shards(): got[step] = lax.ppermute(outgoing[step], 'gy', pairs)]
    all_to_all x1, blocking collectives: 12.6 us -> 14.1 us  [shards(): lax.all_to_all(dense.reshape(across, owned * 32, 128), 'gy', 0, 0, axis_i...]
  transfers between devices with their start and end apart: 4 -> 19, of which waited for: 0 -> 4; matrix products, arithmetic and copies ran while one was open for 1% -> 1% of each run, Pallas kernels for 4% -> 3%
where the time goes in v4:
time: 135 us; the launch traced here: 134 us
  starting transfers between devices  100 us (74%)
  blocking collectives  14.1 us (10%)
  Pallas kernels  8.62 us (6%)
  waiting for transfers between devices  4.75 us (4%)
  local copies, waits for them, and re-layouts  4.18 us (3%)
  other arithmetic  1.47 us (1%)
    ppermute x15, starting transfers between devices, shards(): got[step] = lax.ppermute(outgoing[step], 'gy', pairs)  89.1 us
    all_to_all x1, blocking collectives, shards(): lax.all_to_all(dense.reshape(across, owned * 32, 128), 'gy', 0, 0, axis_i...  14.1 us
    ppermute x15, waiting for transfers between devices, shards(): got[step] = lax.ppermute(outgoing[step], 'gy', pairs)  4.74 us
    ppermute x1, starting transfers between devices, shards(): last_y = lax.ppermute(prolong[:, cy - 1], 'gy', up_y)  4.27 us
    pallas_call x1, Pallas kernels, shards(): pl.pallas_call(left_kernel, out_shape=(jax.ShapeDtypeStruct((cells, 5, 64...  4.04 us
    ppermute x1, starting transfers between devices, shards(): next_x = lax.ppermute(prolong[0], 'gx', down_x)  3.64 us
  transfers between devices with their start and end apart: 19, of which 4 were waited for; matrix products, arithmetic and copies ran while one was open for 1% of the time, Pallas kernels for 3%

profile of v4, /device:TPU:24, one launch (start us, length us, event | category | flops | bytes accessed | tf_op | source)
XLA Modules:
  0.0 134.4 jit_solution(7702561554635371971)
XLA Ops:
  0.0 0.9 slice_bitcast_fusion
  0.9 1.9 %collective-permute-start.1 = (bf16[8,32,128]{2,1,0:T(8,128)(2,1)S(1)}, bf16[8,32,128]{2,1,0:T(8,128)(2,1)S(1)}, u32[]{:S(2)}, u32[]{:S(2)}) collective-permute-start(bf16[8,32,128]{2,1,0:T(8,128)(2,1)S(1)} %get-tuple-element.50), channel_id=1, source_target_pairs={{0,64},{64,128},{128,192},{192,256},{256,320},{320,384},{384,448},... | collective-permute-start | bytes 196616 | tf_op jit(solution)/shard_map/ppermute | solution.py:150
  2.9 3.6 %collective-permute-start = (bf16[8,32,128]{2,1,0:T(8,128)(2,1)S(1)}, bf16[8,32,128]{2,1,0:T(8,128)(2,1)S(1)}, u32[]{:S(2)}, u32[]{:S(2)}) collective-permute-start(bf16[8,32,128]{2,1,0:T(8,128)(2,1)S(1)} %get-tuple-element.51), channel_id=1, source_target_pairs={{64,0},{128,64},{192,128},{256,192},{320,256},{384,320},{448,384},... | collective-permute-start | bytes 196616 | tf_op jit(solution)/shard_map/ppermute | solution.py:149
  6.5 0.8 slice_bitcast_fusion.2
  7.3 4.3 %collective-permute-start.3 = (bf16[4,32,128]{2,1,0:T(8,128)(2,1)S(1)}, bf16[4,32,128]{2,1,0:T(8,128)(2,1)S(1)}, u32[]{:S(2)}, u32[]{:S(2)}) collective-permute-start(bf16[4,32,128]{2,1,0:T(8,128)(2,1)S(1)} %get-tuple-element.48), channel_id=1, source_target_pairs={{0,1},{1,2},{2,3},{3,4},{4,5},{5,6},{6,7},{7,8},{8,9},{9,10},{10,1... | collective-permute-start | bytes 98312 | tf_op jit(solution)/shard_map/ppermute | solution.py:148
  11.6 1.3 collective-permute-start.2
  12.9 0.9 copy-done
  13.9 1.4 %copy-done.5 = bf16[4,8,64,320]{3,2,1,0:T(8,128)(2,1)S(1)} copy-done((bf16[4,8,64,320]{3,2,1,0:T(8,128)(2,1)S(1)}, bf16[4,8,64,320]{3,2,1,0:T(8,128)(2,1)}, u32[]{:S(2)}) %copy-start.5) | copy-done | bytes 1310744
  15.3 4.0 %left_factor.1 = (bf16[32,5,64,64]{3,2,1,0:T(8,128)(2,1)S(1)}, bf16[32,64,128]{2,1,0:T(8,128)(2,1)S(1)}) custom-call(bf16[32,32,128]{2,1,0:T(8,128)(2,1)S(1)} %bitcast.24, bf16[32,64,320]{2,1,0:T(8,128)(2,1)S(1)} %bitcast.30), custom_call_target="tpu_custom_call" | custom-call | flops 671088640 | bytes 2880000 | tf_op jit(solution)/shard_map/left_factor/pallas_call | solution.py:152
  19.4 2.6 %partial_blocks.1 = (bf16[208,128]{1,0:T(8,128)(2,1)S(1)}, bf16[208,128]{1,0:T(8,128)(2,1)S(1)}, bf16[208,128]{1,0:T(8,128)(2,1)S(1)}, bf16[208,128]{1,0:T(8,128...) custom-call(bf16[32,5,64,64]{3,2,1,0:T(8,128)(2,1)S(1)} %get-tuple-e, ...), custom_call_target="tpu_custom_call" | custom-call | tf_op jit(solution)/shard_map/partial_blocks/pallas_call | solution.py:169
  22.0 4.9 %collective-permute-start.4 = (bf16[208,128]{1,0:T(8,128)(2,1)S(1)}, bf16[208,128]{1,0:T(8,128)(2,1)S(1)}, u32[]{:S(2)}, u32[]{:S(2)}) collective-permute-start(bf16[208,128]{1,0:T(8,128)(2,1)S(1)} %get-tuple-element.32), channel_id=1, source_target_pairs={{0,1},{1,2},{2,3},{3,4},{4,5},{5,6},{6,7},{7,8},{8,9},{9,10},{10,1... | collective-permute-start | bytes 159752 | tf_op jit(solution)/shard_map/ppermute | solution.py:200
  26.9 7.3 %collective-permute-start.5 = (bf16[208,128]{1,0:T(8,128)(2,1)S(1)}, bf16[208,128]{1,0:T(8,128)(2,1)S(1)}, u32[]{:S(2)}, u32[]{:S(2)}) collective-permute-start(bf16[208,128]{1,0:T(8,128)(2,1)S(1)} %get-tuple-element.33), channel_id=1, source_target_pairs={{0,2},{1,3},{2,4},{3,5},{4,6},{5,7},{6,8},{7,9},{8,10},{9,11},{10,... | collective-permute-start | bytes 159752 | tf_op jit(solution)/shard_map/ppermute | solution.py:200
  34.2 7.9 %collective-permute-start.6 = (bf16[208,128]{1,0:T(8,128)(2,1)S(1)}, bf16[208,128]{1,0:T(8,128)(2,1)S(1)}, u32[]{:S(2)}, u32[]{:S(2)}) collective-permute-start(bf16[208,128]{1,0:T(8,128)(2,1)S(1)} %get-tuple-element.34), channel_id=1, source_target_pairs={{0,3},{1,4},{2,5},{3,6},{4,7},{5,8},{6,9},{7,10},{8,11},{9,12},{10... | collective-permute-start | bytes 159752 | tf_op jit(solution)/shard_map/ppermute | solution.py:200
  42.1 8.8 %collective-permute-start.7 = (bf16[208,128]{1,0:T(8,128)(2,1)S(1)}, bf16[208,128]{1,0:T(8,128)(2,1)S(1)}, u32[]{:S(2)}, u32[]{:S(2)}) collective-permute-start(bf16[208,128]{1,0:T(8,128)(2,1)S(1)} %get-tuple-element.35), channel_id=1, source_target_pairs={{0,4},{1,5},{2,6},{3,7},{4,8},{5,9},{6,10},{7,11},{8,12},{9,13},{1... | collective-permute-start | bytes 159752 | tf_op jit(solution)/shard_map/ppermute | solution.py:200
  50.9 7.0 %collective-permute-start.8 = (bf16[208,128]{1,0:T(8,128)(2,1)S(1)}, bf16[208,128]{1,0:T(8,128)(2,1)S(1)}, u32[]{:S(2)}, u32[]{:S(2)}) collective-permute-start(bf16[208,128]{1,0:T(8,128)(2,1)S(1)} %get-tuple-element.36), channel_id=1, source_target_pairs={{0,5},{1,6},{2,7},{3,8},{4,9},{5,10},{6,11},{7,12},{8,13},{9,14},{... | collective-permute-start | bytes 159752 | tf_op jit(solution)/shard_map/ppermute | solution.py:200
  57.9 1.9 %collective-permute-start.9 = (bf16[208,128]{1,0:T(8,128)(2,1)S(1)}, bf16[208,128]{1,0:T(8,128)(2,1)S(1)}, u32[]{:S(2)}, u32[]{:S(2)}) collective-permute-start(bf16[208,128]{1,0:T(8,128)(2,1)S(1)} %get-tuple-element.37), channel_id=1, source_target_pairs={{0,6},{1,7},{2,8},{3,9},{4,10},{5,11},{6,12},{7,13},{8,14},{9,15},... | collective-permute-start | bytes 159752 | tf_op jit(solution)/shard_map/ppermute | solution.py:200
  59.9 11.1 %collective-permute-start.10 = (bf16[208,128]{1,0:T(8,128)(2,1)S(1)}, bf16[208,128]{1,0:T(8,128)(2,1)S(1)}, u32[]{:S(2)}, u32[]{:S(2)}) collective-permute-start(bf16[208,128]{1,0:T(8,128)(2,1)S(1)} %get-tuple-element.38), channel_id=1, source_target_pairs={{0,7},{1,8},{2,9},{3,10},{4,11},{5,12},{6,13},{7,14},{8,15},{9,0},... | collective-permute-start | bytes 159752 | tf_op jit(solution)/shard_map/ppermute | solution.py:200
  71.0 3.4 %collective-permute-start.11 = (bf16[208,128]{1,0:T(8,128)(2,1)S(1)}, bf16[208,128]{1,0:T(8,128)(2,1)S(1)}, u32[]{:S(2)}, u32[]{:S(2)}) collective-permute-start(bf16[208,128]{1,0:T(8,128)(2,1)S(1)} %get-tuple-element.39), channel_id=1, source_target_pairs={{0,8},{1,9},{2,10},{3,11},{4,12},{5,13},{6,14},{7,15},{8,0},{9,1},... | collective-permute-start | bytes 159752 | tf_op jit(solution)/shard_map/ppermute | solution.py:200
  74.5 9.9 %collective-permute-start.12 = (bf16[208,128]{1,0:T(8,128)(2,1)S(1)}, bf16[208,128]{1,0:T(8,128)(2,1)S(1)}, u32[]{:S(2)}, u32[]{:S(2)}) collective-permute-start(bf16[208,128]{1,0:T(8,128)(2,1)S(1)} %get-tuple-element.40), channel_id=1, source_target_pairs={{0,9},{1,10},{2,11},{3,12},{4,13},{5,14},{6,15},{7,0},{8,1},{9,2},... | collective-permute-start | bytes 159752 | tf_op jit(solution)/shard_map/ppermute | solution.py:200
  84.4 4.3 %collective-permute-start.13 = (bf16[208,128]{1,0:T(8,128)(2,1)S(1)}, bf16[208,128]{1,0:T(8,128)(2,1)S(1)}, u32[]{:S(2)}, u32[]{:S(2)}) collective-permute-start(bf16[208,128]{1,0:T(8,128)(2,1)S(1)} %get-tuple-element.41), channel_id=1, source_target_pairs={{0,10},{1,11},{2,12},{3,13},{4,14},{5,15},{6,0},{7,1},{8,2},{9,3},... | collective-permute-start | bytes 159752 | tf_op jit(solution)/shard_map/ppermute | solution.py:200
  88.7 5.8 %collective-permute-start.14 = (bf16[208,128]{1,0:T(8,128)(2,1)S(1)}, bf16[208,128]{1,0:T(8,128)(2,1)S(1)}, u32[]{:S(2)}, u32[]{:S(2)}) collective-permute-start(bf16[208,128]{1,0:T(8,128)(2,1)S(1)} %get-tuple-element.42), channel_id=1, source_target_pairs={{0,11},{1,12},{2,13},{3,14},{4,15},{5,0},{6,1},{7,2},{8,3},{9,4},{... | collective-permute-start | bytes 159752 | tf_op jit(solution)/shard_map/ppermute | solution.py:200
  94.5 6.9 %collective-permute-start.15 = (bf16[208,128]{1,0:T(8,128)(2,1)S(1)}, bf16[208,128]{1,0:T(8,128)(2,1)S(1)}, u32[]{:S(2)}, u32[]{:S(2)}) collective-permute-start(bf16[208,128]{1,0:T(8,128)(2,1)S(1)} %get-tuple-element.43), channel_id=1, source_target_pairs={{0,12},{1,13},{2,14},{3,15},{4,0},{5,1},{6,2},{7,3},{8,4},{9,5},{1... | collective-permute-start | bytes 159752 | tf_op jit(solution)/shard_map/ppermute | solution.py:200
  101.5 3.6 %collective-permute-start.16 = (bf16[208,128]{1,0:T(8,128)(2,1)S(1)}, bf16[208,128]{1,0:T(8,128)(2,1)S(1)}, u32[]{:S(2)}, u32[]{:S(2)}) collective-permute-start(bf16[208,128]{1,0:T(8,128)(2,1)S(1)} %get-tuple-element.44), channel_id=1, source_target_pairs={{0,13},{1,14},{2,15},{3,0},{4,1},{5,2},{6,3},{7,4},{8,5},{9,6},{10... | collective-permute-start | bytes 159752 | tf_op jit(solution)/shard_map/ppermute | solution.py:200
  105.1 2.5 %collective-permute-start.17 = (bf16[208,128]{1,0:T(8,128)(2,1)S(1)}, bf16[208,128]{1,0:T(8,128)(2,1)S(1)}, u32[]{:S(2)}, u32[]{:S(2)}) collective-permute-start(bf16[208,128]{1,0:T(8,128)(2,1)S(1)} %get-tuple-element.45), channel_id=1, source_target_pairs={{0,14},{1,15},{2,0},{3,1},{4,2},{5,3},{6,4},{7,5},{8,6},{9,7},{10,... | collective-permute-start | bytes 159752 | tf_op jit(solution)/shard_map/ppermute | solution.py:200
  107.6 3.7 %collective-permute-start.18 = (bf16[208,128]{1,0:T(8,128)(2,1)S(1)}, bf16[208,128]{1,0:T(8,128)(2,1)S(1)}, u32[]{:S(2)}, u32[]{:S(2)}) collective-permute-start(bf16[208,128]{1,0:T(8,128)(2,1)S(1)} %get-tuple-element.46), channel_id=1, source_target_pairs={{0,15},{1,0},{2,1},{3,2},{4,3},{5,4},{6,5},{7,6},{8,7},{9,8},{10,9... | collective-permute-start | bytes 159752 | tf_op jit(solution)/shard_map/ppermute | solution.py:200
  111.4 1.2 collective-permute-done.15.refs_16_
  112.6 2.5 %collective-permute-done.16.refs_17_ = bf16[208,128]{1,0:T(8,128)(2,1)S(1)} collective-permute-done((bf16[208,128]{1,0:T(8,128)(2,1)S(1)}, bf16[208,128]{1,0:T(8,128)(2,1)S(1)}, u32[]{:S(2)}, u32[]{:S(2)}) %collective-permute-start.16) | collective-permute-done | bytes 53280 | tf_op jit(solution)/shard_map/ppermute | solution.py:200
  115.5 0.6 collective-permute-done.18.refs_19_
  116.2 0.7 slice_reduce_fusion
  117.6 2.0 %ring_sums.1 = bf16[64,32,128]{2,1,0:T(8,128)(2,1)S(1)} custom-call(s32[1]{0:T(128)} %bitcast.refs_10_.refs_0_, s32[16,8]{1,0:T(8,128)S(1)} %bitcast.25, s32[1]{0:T(128)} %bitcast.11.refs_2_, bf16[16,64,128]{2,1,0:T(8,128)(2,1)S(1)} %get-tuple-element.52.refs_3_, bf16[208,128]{1,0:T(8,128)(2,1)S(1)} %get-tuple-element.31.refs_4_, ...), custom_call_target="tpu_custom_call" | custom-call | tf_op jit(solution)/shard_map/ring_sums/pallas_call | solution.py:211
  119.6 14.1 %all_to_all.10 = bf16[4,512,128]{2,1,0:T(8,128)(2,1)S(1)} all-to-all(bf16[4,512,128]{2,1,0:T(8,128)(2,1)S(1)} %bitcast.23), channel_id=1, replica_groups={{0,16,32,48},{1,17,33,49},{2,18,34,50},{3,19,35,51},{4,20,36,52},{5,21,..., dimensions={0} | all-to-all | bytes 1048576 | tf_op jit(solution)/shard_map/all_to_all | solution.py:220
  133.7 0.7 reduce_sum.12
  (45 shorter events, 0.6 us)
Async XLA Ops:
  0.0 19.4 %copy-start.4 = (s32[1,32]{1,0:T(1,128)S(1)}, s32[1,32]{1,0:T(1,128)}, u32[]{:S(2)}) copy-start(s32[1,32]{1,0:T(1,128)} %param.13) | copy-start | bytes 388
  0.0 19.4 %copy-start.3 = (s32[1,32,1]{1,2,0:T(1,128)S(1)}, s32[1,32,1]{1,2,0:T(1,128)}, u32[]{:S(2)}) copy-start(s32[1,32,1]{1,2,0:T(1,128)} %param.12) | copy-start | bytes 388
  0.0 19.4 %copy-start.1 = (s32[4,8,5]{1,0,2:T(4,128)S(1)}, s32[4,8,5]{1,0,2:T(4,128)}, u32[]{:S(2)}) copy-start(s32[4,8,5]{1,0,2:T(4,128)} %param.11) | copy-start | bytes 1924
  0.0 19.4 %copy-start.2 = (s32[4,8,4]{1,2,0:T(4,128)S(1)}, s32[4,8,4]{1,2,0:T(4,128)}, u32[]{:S(2)}) copy-start(s32[4,8,4]{1,2,0:T(4,128)} %param.10) | copy-start | bytes 1540
  0.9 18.4 %collective-permute-start.1 = (bf16[8,32,128]{2,1,0:T(8,128)(2,1)S(1)}, bf16[8,32,128]{2,1,0:T(8,128)(2,1)S(1)}, u32[]{:S(2)}, u32[]{:S(2)}) collective-permute-start(bf16[8,32,128]{2,1,0:T(8,128)(2,1)S(1)} %get-tuple-element.50), channel_id=1, source_target_pairs={{0,64},{64,128},{128,192},{192,256},{256,320},{320,384},{384,448},... | collective-permute-start | bytes 196616 | tf_op jit(solution)/shard_map/ppermute | solution.py:150
  2.9 16.5 %collective-permute-start = (bf16[8,32,128]{2,1,0:T(8,128)(2,1)S(1)}, bf16[8,32,128]{2,1,0:T(8,128)(2,1)S(1)}, u32[]{:S(2)}, u32[]{:S(2)}) collective-permute-start(bf16[8,32,128]{2,1,0:T(8,128)(2,1)S(1)} %get-tuple-element.51), channel_id=1, source_target_pairs={{64,0},{128,64},{192,128},{256,192},{320,256},{384,320},{448,384},... | collective-permute-start | bytes 196616 | tf_op jit(solution)/shard_map/ppermute | solution.py:149
  7.3 12.0 %collective-permute-start.3 = (bf16[4,32,128]{2,1,0:T(8,128)(2,1)S(1)}, bf16[4,32,128]{2,1,0:T(8,128)(2,1)S(1)}, u32[]{:S(2)}, u32[]{:S(2)}) collective-permute-start(bf16[4,32,128]{2,1,0:T(8,128)(2,1)S(1)} %get-tuple-element.48), channel_id=1, source_target_pairs={{0,1},{1,2},{2,3},{3,4},{4,5},{5,6},{6,7},{7,8},{8,9},{9,10},{10,1... | collective-permute-start | bytes 98312 | tf_op jit(solution)/shard_map/ppermute | solution.py:148
  11.6 7.7 %collective-permute-start.2 = (bf16[4,32,128]{2,1,0:T(8,128)(2,1)S(1)}, bf16[4,32,128]{2,1,0:T(8,128)(2,1)S(1)}, u32[]{:S(2)}, u32[]{:S(2)}) collective-permute-start(bf16[4,32,128]{2,1,0:T(8,128)(2,1)S(1)} %get-tuple-element.49), channel_id=1, source_target_pairs={{1,0},{2,1},{3,2},{4,3},{5,4},{6,5},{7,6},{8,7},{9,8},{10,9},{11,1... | collective-permute-start | bytes 98312 | tf_op jit(solution)/shard_map/ppermute | solution.py:147
  12.9 1.0 copy-start
  13.9 1.4 %copy-start.5 = (bf16[4,8,64,320]{3,2,1,0:T(8,128)(2,1)S(1)}, bf16[4,8,64,320]{3,2,1,0:T(8,128)(2,1)}, u32[]{:S(2)}) copy-start(bf16[4,8,64,320]{3,2,1,0:T(8,128)(2,1)} %param.8) | copy-start | bytes 3932164
  22.0 35.9 %collective-permute-start.4 = (bf16[208,128]{1,0:T(8,128)(2,1)S(1)}, bf16[208,128]{1,0:T(8,128)(2,1)S(1)}, u32[]{:S(2)}, u32[]{:S(2)}) collective-permute-start(bf16[208,128]{1,0:T(8,128)(2,1)S(1)} %get-tuple-element.32), channel_id=1, source_target_pairs={{0,1},{1,2},{2,3},{3,4},{4,5},{5,6},{6,7},{7,8},{8,9},{9,10},{10,1... | collective-permute-start | bytes 159752 | tf_op jit(solution)/shard_map/ppermute | solution.py:200
  26.9 32.9 %collective-permute-start.5 = (bf16[208,128]{1,0:T(8,128)(2,1)S(1)}, bf16[208,128]{1,0:T(8,128)(2,1)S(1)}, u32[]{:S(2)}, u32[]{:S(2)}) collective-permute-start(bf16[208,128]{1,0:T(8,128)(2,1)S(1)} %get-tuple-element.33), channel_id=1, source_target_pairs={{0,2},{1,3},{2,4},{3,5},{4,6},{5,7},{6,8},{7,9},{8,10},{9,11},{10,... | collective-permute-start | bytes 159752 | tf_op jit(solution)/shard_map/ppermute | solution.py:200
  34.2 36.8 %collective-permute-start.6 = (bf16[208,128]{1,0:T(8,128)(2,1)S(1)}, bf16[208,128]{1,0:T(8,128)(2,1)S(1)}, u32[]{:S(2)}, u32[]{:S(2)}) collective-permute-start(bf16[208,128]{1,0:T(8,128)(2,1)S(1)} %get-tuple-element.34), channel_id=1, source_target_pairs={{0,3},{1,4},{2,5},{3,6},{4,7},{5,8},{6,9},{7,10},{8,11},{9,12},{10... | collective-permute-start | bytes 159752 | tf_op jit(solution)/shard_map/ppermute | solution.py:200
  42.1 32.3 %collective-permute-start.7 = (bf16[208,128]{1,0:T(8,128)(2,1)S(1)}, bf16[208,128]{1,0:T(8,128)(2,1)S(1)}, u32[]{:S(2)}, u32[]{:S(2)}) collective-permute-start(bf16[208,128]{1,0:T(8,128)(2,1)S(1)} %get-tuple-element.35), channel_id=1, source_target_pairs={{0,4},{1,5},{2,6},{3,7},{4,8},{5,9},{6,10},{7,11},{8,12},{9,13},{1... | collective-permute-start | bytes 159752 | tf_op jit(solution)/shard_map/ppermute | solution.py:200
  50.9 33.5 %collective-permute-start.8 = (bf16[208,128]{1,0:T(8,128)(2,1)S(1)}, bf16[208,128]{1,0:T(8,128)(2,1)S(1)}, u32[]{:S(2)}, u32[]{:S(2)}) collective-permute-start(bf16[208,128]{1,0:T(8,128)(2,1)S(1)} %get-tuple-element.36), channel_id=1, source_target_pairs={{0,5},{1,6},{2,7},{3,8},{4,9},{5,10},{6,11},{7,12},{8,13},{9,14},{... | collective-permute-start | bytes 159752 | tf_op jit(solution)/shard_map/ppermute | solution.py:200
  57.9 30.8 %collective-permute-start.9 = (bf16[208,128]{1,0:T(8,128)(2,1)S(1)}, bf16[208,128]{1,0:T(8,128)(2,1)S(1)}, u32[]{:S(2)}, u32[]{:S(2)}) collective-permute-start(bf16[208,128]{1,0:T(8,128)(2,1)S(1)} %get-tuple-element.37), channel_id=1, source_target_pairs={{0,6},{1,7},{2,8},{3,9},{4,10},{5,11},{6,12},{7,13},{8,14},{9,15},... | collective-permute-start | bytes 159752 | tf_op jit(solution)/shard_map/ppermute | solution.py:200
  59.9 34.7 %collective-permute-start.10 = (bf16[208,128]{1,0:T(8,128)(2,1)S(1)}, bf16[208,128]{1,0:T(8,128)(2,1)S(1)}, u32[]{:S(2)}, u32[]{:S(2)}) collective-permute-start(bf16[208,128]{1,0:T(8,128)(2,1)S(1)} %get-tuple-element.38), channel_id=1, source_target_pairs={{0,7},{1,8},{2,9},{3,10},{4,11},{5,12},{6,13},{7,14},{8,15},{9,0},... | collective-permute-start | bytes 159752 | tf_op jit(solution)/shard_map/ppermute | solution.py:200
  71.0 30.5 %collective-permute-start.11 = (bf16[208,128]{1,0:T(8,128)(2,1)S(1)}, bf16[208,128]{1,0:T(8,128)(2,1)S(1)}, u32[]{:S(2)}, u32[]{:S(2)}) collective-permute-start(bf16[208,128]{1,0:T(8,128)(2,1)S(1)} %get-tuple-element.39), channel_id=1, source_target_pairs={{0,8},{1,9},{2,10},{3,11},{4,12},{5,13},{6,14},{7,15},{8,0},{9,1},... | collective-permute-start | bytes 159752 | tf_op jit(solution)/shard_map/ppermute | solution.py:200
  74.5 30.7 %collective-permute-start.12 = (bf16[208,128]{1,0:T(8,128)(2,1)S(1)}, bf16[208,128]{1,0:T(8,128)(2,1)S(1)}, u32[]{:S(2)}, u32[]{:S(2)}) collective-permute-start(bf16[208,128]{1,0:T(8,128)(2,1)S(1)} %get-tuple-element.40), channel_id=1, source_target_pairs={{0,9},{1,10},{2,11},{3,12},{4,13},{5,14},{6,15},{7,0},{8,1},{9,2},... | collective-permute-start | bytes 159752 | tf_op jit(solution)/shard_map/ppermute | solution.py:200
  84.4 23.2 %collective-permute-start.13 = (bf16[208,128]{1,0:T(8,128)(2,1)S(1)}, bf16[208,128]{1,0:T(8,128)(2,1)S(1)}, u32[]{:S(2)}, u32[]{:S(2)}) collective-permute-start(bf16[208,128]{1,0:T(8,128)(2,1)S(1)} %get-tuple-element.41), channel_id=1, source_target_pairs={{0,10},{1,11},{2,12},{3,13},{4,14},{5,15},{6,0},{7,1},{8,2},{9,3},... | collective-permute-start | bytes 159752 | tf_op jit(solution)/shard_map/ppermute | solution.py:200
  88.7 22.7 %collective-permute-start.14 = (bf16[208,128]{1,0:T(8,128)(2,1)S(1)}, bf16[208,128]{1,0:T(8,128)(2,1)S(1)}, u32[]{:S(2)}, u32[]{:S(2)}) collective-permute-start(bf16[208,128]{1,0:T(8,128)(2,1)S(1)} %get-tuple-element.42), channel_id=1, source_target_pairs={{0,11},{1,12},{2,13},{3,14},{4,15},{5,0},{6,1},{7,2},{8,3},{9,4},{... | collective-permute-start | bytes 159752 | tf_op jit(solution)/shard_map/ppermute | solution.py:200
  94.5 18.1 %collective-permute-start.15 = (bf16[208,128]{1,0:T(8,128)(2,1)S(1)}, bf16[208,128]{1,0:T(8,128)(2,1)S(1)}, u32[]{:S(2)}, u32[]{:S(2)}) collective-permute-start(bf16[208,128]{1,0:T(8,128)(2,1)S(1)} %get-tuple-element.43), channel_id=1, source_target_pairs={{0,12},{1,13},{2,14},{3,15},{4,0},{5,1},{6,2},{7,3},{8,4},{9,5},{1... | collective-permute-start | bytes 159752 | tf_op jit(solution)/shard_map/ppermute | solution.py:200
  101.5 13.6 %collective-permute-start.16 = (bf16[208,128]{1,0:T(8,128)(2,1)S(1)}, bf16[208,128]{1,0:T(8,128)(2,1)S(1)}, u32[]{:S(2)}, u32[]{:S(2)}) collective-permute-start(bf16[208,128]{1,0:T(8,128)(2,1)S(1)} %get-tuple-element.44), channel_id=1, source_target_pairs={{0,13},{1,14},{2,15},{3,0},{4,1},{5,2},{6,3},{7,4},{8,5},{9,6},{10... | collective-permute-start | bytes 159752 | tf_op jit(solution)/shard_map/ppermute | solution.py:200
  105.1 10.4 %collective-permute-start.17 = (bf16[208,128]{1,0:T(8,128)(2,1)S(1)}, bf16[208,128]{1,0:T(8,128)(2,1)S(1)}, u32[]{:S(2)}, u32[]{:S(2)}) collective-permute-start(bf16[208,128]{1,0:T(8,128)(2,1)S(1)} %get-tuple-element.45), channel_id=1, source_target_pairs={{0,14},{1,15},{2,0},{3,1},{4,2},{5,3},{6,4},{7,5},{8,6},{9,7},{10,... | collective-permute-start | bytes 159752 | tf_op jit(solution)/shard_map/ppermute | solution.py:200
  107.6 8.5 %collective-permute-start.18 = (bf16[208,128]{1,0:T(8,128)(2,1)S(1)}, bf16[208,128]{1,0:T(8,128)(2,1)S(1)}, u32[]{:S(2)}, u32[]{:S(2)}) collective-permute-start(bf16[208,128]{1,0:T(8,128)(2,1)S(1)} %get-tuple-element.46), channel_id=1, source_target_pairs={{0,15},{1,0},{2,1},{3,2},{4,3},{5,4},{6,5},{7,6},{8,7},{9,8},{10,9... | collective-permute-start | bytes 159752 | tf_op jit(solution)/shard_map/ppermute | solution.py:200

commit v5 on v3

--- a/solution.py
+++ b/solution.py
@@ -39,10 +39,10 @@
     cy,
     left_ref,
     rows_ref,
-    next_x_ref,
-    last_x_ref,
-    next_y_ref,
-    last_y_ref,
+    near_x_ref,
+    far_x_ref,
+    near_y_ref,
+    far_y_ref,
     entries_ref,
     present_ref,
     owners_ref,
@@ -51,6 +51,7 @@
     late_ref,
     sums_ref,
     wide_ref,
+    slots_ref,
     count_ref,
 ):
     count = cx * cy
@@ -62,7 +63,7 @@
         terms = jnp.dot(stack, block, preferred_element_type=jnp.float32)
         for n, (x, y, d) in enumerate(users):
             entry = entries_ref[d, x, y]
-            if d:
+            if not isinstance(d, int) or d > 0:
                 entry = jnp.where(present_ref[x, d - 1, y] != 0, entry, count)
             sums_ref[entry] = sums_ref[entry] + terms[n * 64 : n * 64 + 64]
 
@@ -71,14 +72,20 @@
             users = [(x, y, 0), (x - 1, y, 1), (x + 1, y, 2), (x, y - 1, 3), (x, y + 1, 4)]
             users = [u for u in users if 0 <= u[0] < cx and 0 <= u[1] < cy]
             add(rows_ref[x * cy + y], users)
-    for y in range(cy):
-        add(unpacked(next_x_ref[y], wide_ref.at[y % 4]), [(cx - 1, y, 1)])
-    for y in range(cy):
-        add(unpacked(last_x_ref[y], wide_ref.at[y % 4]), [(0, y, 2)])
-    for x in range(cx):
-        add(unpacked(next_y_ref[x], wide_ref.at[x % 4]), [(x, cy - 1, 3)])
-    for x in range(cx):
-        add(unpacked(last_y_ref[x], wide_ref.at[x % 4]), [(x, 0, 4)])
+    for axis, far, block_ref in (
+        ("gx", 0, near_x_ref),
+        ("gx", 1, far_x_ref),
+        ("gy", 0, near_y_ref),
+        ("gy", 1, far_y_ref),
+    ):
+        is_next = lax.axis_index(axis) % 2 == far
+        for n in range(cy if axis == "gx" else cx):
+            block = unpacked(block_ref[n], wide_ref.at[n % 4])
+            if axis == "gx":
+                user = (jnp.where(is_next, cx - 1, 0), n, jnp.where(is_next, 1, 2))
+            else:
+                user = (n, jnp.where(is_next, cy - 1, 0), jnp.where(is_next, 3, 4))
+            add(block, [user])
 
     for ring in range(RING):
         count_ref[ring] = 0
@@ -97,18 +104,13 @@
         block = jnp.where(low, even, pltpu.roll(odd, 64, 1)).astype(jnp.bfloat16)
         most = jnp.maximum(most, slot)
 
-        @pl.when(slot < FIRST)
-        def _():
-            out_ref[ring, pl.ds(pl.multiple_of(slot * 32, 32), 32), :] = block
-
-        @pl.when(slot >= FIRST)
-        def _():
-            late_ref[ring, pl.ds(pl.multiple_of((slot - FIRST) * 32, 32), 32), :] = block
-
+        slots_ref[ring, pl.ds(pl.multiple_of(slot * 32, 32), 32), :] = block
         tag = (owner // RING) * 16 + targets_ref[e]
         tags = jnp.where((row_id == ring) & (lane_id == slot), tag.astype(jnp.float32), tags)
     late = (most >= FIRST).astype(jnp.float32)
     tags = jnp.where(lane_id == SLOTS, late, tags)
+    out_ref[:, : FIRST * 32, :] = slots_ref[:, : FIRST * 32, :]
+    late_ref[...] = slots_ref[:, FIRST * 32 :, :]
     for ring in range(RING):
         row = jnp.broadcast_to(tags[ring : ring + 1, :], (16, 128))
         out_ref[ring, FIRST * 32 : FIRST * 32 + 16, :] = row.astype(jnp.bfloat16)
@@ -138,20 +140,24 @@
 def shards(couplings, prolong, present, entries, owners, targets):
     cx, cy = prolong.shape[0], prolong.shape[1]
     cells = cx * cy
-    nx, ny = lax.axis_size("gx"), lax.axis_size("gy")
-    across = ny // RING
+    across = lax.axis_size("gy") // RING
     along = [[x * RING + z for z in range(RING)] for x in range(across)]
     aside = [[x * RING + z for x in range(across)] for z in range(RING)]
     owned = 16
 
-    up_x = [(i, i + 1) for i in range(nx - 1)]
-    down_x = [(i + 1, i) for i in range(nx - 1)]
-    up_y = [(i, i + 1) for i in range(ny - 1)]
-    down_y = [(i + 1, i) for i in range(ny - 1)]
-    next_y = lax.ppermute(prolong[:, 0], "gy", down_y)
-    last_y = lax.ppermute(prolong[:, cy - 1], "gy", up_y)
-    next_x = lax.ppermute(prolong[0], "gx", down_x)
-    last_x = lax.ppermute(prolong[cx - 1], "gx", up_x)
+    def swapped(head, tail, axis):
+        size = lax.axis_size(axis)
+        even = lax.axis_index(axis) % 2 == 0
+        near = [(i, i ^ 1) for i in range(size)]
+        far = [(i, i + 1) for i in range(1, size - 1, 2)]
+        far = far + [(j, i) for i, j in far]
+        return (
+            lax.ppermute(jnp.where(even, tail, head), axis, near),
+            lax.ppermute(jnp.where(even, head, tail), axis, far),
+        )
+
+    near_x, far_x = swapped(prolong[0], prolong[cx - 1], "gx")
+    near_y, far_y = swapped(prolong[:, 0], prolong[:, cy - 1], "gy")
 
     left, rows = pl.pallas_call(
         left_kernel,
@@ -180,6 +186,7 @@
         scratch_shapes=[
             pltpu.VMEM((cells + 1, 64, 128), jnp.float32),
             pltpu.VMEM((4, 64, 128), jnp.float32),
+            pltpu.VMEM((RING, SLOTS * 32, 128), jnp.bfloat16),
             pltpu.SMEM((RING,), jnp.int32),
         ],
         compiler_params=PARAMS,
@@ -187,10 +194,10 @@
     )(
         left,
         rows,
-        next_x,
-        last_x,
-        next_y,
-        last_y,
+        near_x,
+        far_x,
+        near_y,
+        far_y,
         jnp.transpose(entries, (2, 0, 1)),
         jnp.transpose(present, (0, 2, 1)),
         owners.reshape(cells),

time: 105 us -> 103 us (0.981)
  blocking collectives: 76.7 us -> 72.2 us
  starting transfers between devices: 11.1 us -> 15.3 us
  Pallas kernels: 10.5 us -> 8.53 us
  local copies, waits for them, and re-layouts: 4.09 us -> 2.38 us
  other arithmetic: 1.46 us -> 3.16 us
    all_to_all x1, blocking collectives: 64.5 us -> 60.1 us  [exchange(): lax.all_to_all(array, 'gy', 0, 0, axis_index_groups=along, tiled=True)]
    ppermute x4, starting transfers between devices: 11.1 us -> 15.3 us  [the longest x2 12.7 us: swapped(): lax.ppermute(jnp.where(even, tail, head), axis, near)]
    pallas_call x1, Pallas kernels: 4.47 us -> 2.5 us  [shards(): pl.pallas_call(lambda *refs: partial_kernel(cx, cy, *refs), out_shape=(ja...]
    squeeze x2 -> x0, local copies, waits for them, and re-layouts: 1.71 us -> none  [the longest x1 0.92 us: shards(): last_x = lax.ppermute(prolong[cx - 1], 'gx', up_x)]
    select_n x0 -> x2, other arithmetic: none -> 1.7 us  [swapped(): jnp.where(even, head, tail)]
where the time goes in v5:
time: 103 us; the launch traced here: 102 us
  blocking collectives  72.2 us (70%)
  starting transfers between devices  15.3 us (15%)
  Pallas kernels  8.53 us (8%)
  other arithmetic  3.16 us (3%)
  local copies, waits for them, and re-layouts  2.38 us (2%)
    all_to_all x1, blocking collectives, exchange(): lax.all_to_all(array, 'gy', 0, 0, axis_index_groups=along, tiled=True)  60.1 us
    ppermute x2, starting transfers between devices, swapped(): lax.ppermute(jnp.where(even, tail, head), axis, near)  12.7 us
    all_to_all x1, blocking collectives, shards(): lax.all_to_all(dense.reshape(across, owned * 32, 128), 'gy', 0, 0, axis_i...  12.2 us
    pallas_call x1, Pallas kernels, shards(): pl.pallas_call(left_kernel, out_shape=(jax.ShapeDtypeStruct((cells, 5, 64...  4.04 us
    ppermute x2, starting transfers between devices, swapped(): lax.ppermute(jnp.where(even, head, tail), axis, far)  2.58 us
    pallas_call x1, Pallas kernels, shards(): pl.pallas_call(lambda *refs: partial_kernel(cx, cy, *refs), out_shape=(ja...  2.5 us
    unnamed x12, local copies, waits for them, and re-layouts  2.37 us
  transfers between devices with their start and end apart: 4, of which 0 were waited for; matrix products, arithmetic and copies ran while one was open for 1% of the time, Pallas kernels for 4%

profile of v5, /device:TPU:24, one launch (start us, length us, event | category | flops | bytes accessed | tf_op | source)
XLA Modules:
  0.0 102.4 jit_solution(1035678768268451951)
XLA Ops:
  0.0 0.0 copy-start.4
  0.0 0.0 copy-start.3
  0.0 0.0 copy-start.1
  0.0 0.0 copy-start.2
  0.0 0.9 select_bitcast_fusion
  0.9 1.9 %collective-permute-start.1 = (bf16[8,32,128]{2,1,0:T(8,128)(2,1)S(1)}, bf16[8,32,128]{2,1,0:T(8,128)(2,1)S(1)}, u32[]{:S(2)}, u32[]{:S(2)}) collective-permute-start(bf16[8,32,128]{2,1,0:T(8,128)(2,1)S(1)} %get-tuple-element.20), channel_id=1, source_target_pairs={{64,128},{192,256},{320,384},{448,512},{576,640},{704,768},{832,89... | collective-permute-start | bytes 196616 | tf_op jit(solution)/shard_map/ppermute | solution.py:156
  2.9 4.8 %collective-permute-start = (bf16[8,32,128]{2,1,0:T(8,128)(2,1)S(1)}, bf16[8,32,128]{2,1,0:T(8,128)(2,1)S(1)}, u32[]{:S(2)}, u32[]{:S(2)}) collective-permute-start(bf16[8,32,128]{2,1,0:T(8,128)(2,1)S(1)} %get-tuple-element.21), channel_id=1, source_target_pairs={{0,64},{64,0},{128,192},{192,128},{256,320},{320,256},{384,448},{4... | collective-permute-start | bytes 196616 | tf_op jit(solution)/shard_map/ppermute | solution.py:155
  7.7 0.8 fusion.1
  8.5 0.7 collective-permute-start.3
  9.1 7.9 %collective-permute-start.2 = (bf16[4,32,128]{2,1,0:T(8,128)(2,1)S(1)}, bf16[4,32,128]{2,1,0:T(8,128)(2,1)S(1)}, u32[]{:S(2)}, u32[]{:S(2)}) collective-permute-start(bf16[4,32,128]{2,1,0:T(8,128)(2,1)S(1)} %get-tuple-element.19), channel_id=1, source_target_pairs={{0,1},{1,0},{2,3},{3,2},{4,5},{5,4},{6,7},{7,6},{8,9},{9,8},{10,11... | collective-permute-start | bytes 98312 | tf_op jit(solution)/shard_map/ppermute | solution.py:155
  17.1 0.0 copy-start
  17.1 0.9 copy-done
  18.0 0.0 copy-start.5
  18.0 1.4 %copy-done.5 = bf16[4,8,64,320]{3,2,1,0:T(8,128)(2,1)S(1)} copy-done((bf16[4,8,64,320]{3,2,1,0:T(8,128)(2,1)S(1)}, bf16[4,8,64,320]{3,2,1,0:T(8,128)(2,1)}, u32[]{:S(2)}) %copy-start.5) | copy-done | bytes 1310744
  19.4 4.0 %left_factor.1 = (bf16[32,5,64,64]{3,2,1,0:T(8,128)(2,1)S(1)}, bf16[32,64,128]{2,1,0:T(8,128)(2,1)S(1)}) custom-call(bf16[32,32,128]{2,1,0:T(8,128)(2,1)S(1)} %bitcast.34, bf16[32,64,320]{2,1,0:T(8,128)(2,1)S(1)} %bitcast.40), custom_call_target="tpu_custom_call" | custom-call | flops 671088640 | bytes 2880000 | tf_op jit(solution)/shard_map/left_factor/pallas_call | solution.py:162
  23.5 0.0 collective-permute-done.3.refs_5_
  23.5 0.0 collective-permute-done.2.refs_4_
  23.5 0.0 collective-permute-done.1.refs_3_
  23.5 0.0 collective-permute-done.refs_2_
  23.5 0.0 copy-done.4
  23.5 0.0 copy-done.3
  23.5 0.0 copy-done.1
  23.5 0.0 copy-done.2
  23.5 2.5 %partial_blocks.1 = (bf16[16,208,128]{2,1,0:T(8,128)(2,1)S(1)}, bf16[16,64,128]{2,1,0:T(8,128)(2,1)S(1)}) custom-call(bf16[32,5,64,64]{3,2,1,0:T(8,128)(2,1)S(1)} %get-tuple-element.14.refs_0_, bf16[32,64,128]{2,1,0:T(8,128)(2,1)S(1)} %get-tuple-element.15.refs_1_, bf16[8,32,128]{2,1,0:T(8,128)(2,1)S(1)} %collective-permute-done.refs_2_, ...), custom_call_target="tpu_custom_call" | custom-call | tf_op jit(solution)/shard_map/partial_blocks/pallas_call | solution.py:178
  26.1 60.1 %all_to_all.15.refs_0_ = bf16[16,208,128]{2,1,0:T(8,128)(2,1)S(1)} all-to-all(bf16[16,208,128]{2,1,0:T(8,128)(2,1)S(1)} %get-tuple-element.16), channel_id=1, replica_groups={{0,1,2,3,4,5,6,7,8,9,10,11,12,13,14,15},{16,17,18,19,20,21,22,23,24,25,..., dimensions={0} | all-to-all | bytes 1703936 | tf_op jit(solution)/shard_map/all_to_all | solution.py:208
  86.2 0.7 slice_reduce_fusion
  87.5 2.0 %ring_sums.1 = bf16[64,32,128]{2,1,0:T(8,128)(2,1)S(1)} custom-call(bf16[16,208,128]{2,1,0:T(8,128)(2,1)S(1)} %all_to_all.15.refs_0_, bf16[16,64,128]{2,1,0:T(8,128)(2,1)S(1)} %get-tuple-element.22.refs_1_, s32[16,8]{1,0:T(8,128)S(1)} %bitcast.35, s32[1]{0:T(128)} %bitcast.12.refs_3_), custom_call_target="tpu_custom_call" | custom-call | tf_op jit(solution)/shard_map/ring_sums/pallas_call | solution.py:216
  89.5 12.2 %all_to_all.16 = bf16[4,512,128]{2,1,0:T(8,128)(2,1)S(1)} all-to-all(bf16[4,512,128]{2,1,0:T(8,128)(2,1)S(1)} %bitcast.33), channel_id=1, replica_groups={{0,16,32,48},{1,17,33,49},{2,18,34,50},{3,19,35,51},{4,20,36,52},{5,21,..., dimensions={0} | all-to-all | bytes 1048576 | tf_op jit(solution)/shard_map/all_to_all | solution.py:225
  101.7 0.7 reduce_sum.12
  (3 shorter events, 0.0 us)
Async XLA Ops:
  0.0 23.5 %copy-start.4 = (s32[1,32]{1,0:T(1,128)S(1)}, s32[1,32]{1,0:T(1,128)}, u32[]{:S(2)}) copy-start(s32[1,32]{1,0:T(1,128)} %param.13) | copy-start | bytes 388
  0.0 23.5 %copy-start.3 = (s32[1,32,1]{1,2,0:T(1,128)S(1)}, s32[1,32,1]{1,2,0:T(1,128)}, u32[]{:S(2)}) copy-start(s32[1,32,1]{1,2,0:T(1,128)} %param.12) | copy-start | bytes 388
  0.0 23.5 %copy-start.1 = (s32[4,8,5]{1,0,2:T(4,128)S(1)}, s32[4,8,5]{1,0,2:T(4,128)}, u32[]{:S(2)}) copy-start(s32[4,8,5]{1,0,2:T(4,128)} %param.11) | copy-start | bytes 1924
  0.0 23.5 %copy-start.2 = (s32[4,8,4]{1,2,0:T(4,128)S(1)}, s32[4,8,4]{1,2,0:T(4,128)}, u32[]{:S(2)}) copy-start(s32[4,8,4]{1,2,0:T(4,128)} %param.10) | copy-start | bytes 1540
  0.9 22.5 %collective-permute-start.1 = (bf16[8,32,128]{2,1,0:T(8,128)(2,1)S(1)}, bf16[8,32,128]{2,1,0:T(8,128)(2,1)S(1)}, u32[]{:S(2)}, u32[]{:S(2)}) collective-permute-start(bf16[8,32,128]{2,1,0:T(8,128)(2,1)S(1)} %get-tuple-element.20), channel_id=1, source_target_pairs={{64,128},{192,256},{320,384},{448,512},{576,640},{704,768},{832,89... | collective-permute-start | bytes 196616 | tf_op jit(solution)/shard_map/ppermute | solution.py:156
  2.9 20.6 %collective-permute-start = (bf16[8,32,128]{2,1,0:T(8,128)(2,1)S(1)}, bf16[8,32,128]{2,1,0:T(8,128)(2,1)S(1)}, u32[]{:S(2)}, u32[]{:S(2)}) collective-permute-start(bf16[8,32,128]{2,1,0:T(8,128)(2,1)S(1)} %get-tuple-element.21), channel_id=1, source_target_pairs={{0,64},{64,0},{128,192},{192,128},{256,320},{320,256},{384,448},{4... | collective-permute-start | bytes 196616 | tf_op jit(solution)/shard_map/ppermute | solution.py:155
  8.5 15.0 %collective-permute-start.3 = (bf16[4,32,128]{2,1,0:T(8,128)(2,1)S(1)}, bf16[4,32,128]{2,1,0:T(8,128)(2,1)S(1)}, u32[]{:S(2)}, u32[]{:S(2)}) collective-permute-start(bf16[4,32,128]{2,1,0:T(8,128)(2,1)S(1)} %get-tuple-element.18), channel_id=1, source_target_pairs={{1,2},{3,4},{5,6},{7,8},{9,10},{11,12},{13,14},{15,16},{17,18},{19... | collective-permute-start | bytes 98312 | tf_op jit(solution)/shard_map/ppermute | solution.py:156
  9.1 14.3 %collective-permute-start.2 = (bf16[4,32,128]{2,1,0:T(8,128)(2,1)S(1)}, bf16[4,32,128]{2,1,0:T(8,128)(2,1)S(1)}, u32[]{:S(2)}, u32[]{:S(2)}) collective-permute-start(bf16[4,32,128]{2,1,0:T(8,128)(2,1)S(1)} %get-tuple-element.19), channel_id=1, source_target_pairs={{0,1},{1,0},{2,3},{3,2},{4,5},{5,4},{6,7},{7,6},{8,9},{9,8},{10,11... | collective-permute-start | bytes 98312 | tf_op jit(solution)/shard_map/ppermute | solution.py:155
  17.1 1.0 copy-start
  18.0 1.4 %copy-start.5 = (bf16[4,8,64,320]{3,2,1,0:T(8,128)(2,1)S(1)}, bf16[4,8,64,320]{3,2,1,0:T(8,128)(2,1)}, u32[]{:S(2)}) copy-start(bf16[4,8,64,320]{3,2,1,0:T(8,128)(2,1)} %param.8) | copy-start | bytes 3932164

commit v6 on v5

--- a/solution.py
+++ b/solution.py
@@ -9,6 +9,8 @@
 SLOTS = 8
 FIRST = 6
 VMEM = pl.BlockSpec(memory_space=pltpu.VMEM)
+ANY = pl.BlockSpec(memory_space=pl.ANY)
+CHUNKS = 8
 SMEM = pl.BlockSpec(memory_space=pltpu.SMEM)
 PARAMS = pltpu.CompilerParams(vmem_limit_bytes=40 * 1024 * 1024)
 
@@ -20,8 +22,45 @@
     return wide_ref[...].astype(jnp.bfloat16)
 
 
-def left_kernel(prolong_ref, couplings_ref, left_ref, rows_ref, wide_ref):
-    for cell in range(prolong_ref.shape[0]):
+def in_hbm(array):
+    return pltpu.with_memory_space_constraint(array, pltpu.HBM)
+
+
+def edge_kernel(cx, cy, prolong_hbm, near_x_ref, far_x_ref, near_y_ref, far_y_ref, sems):
+    even_x = lax.axis_index("gx") % 2 == 0
+    even_y = lax.axis_index("gy") % 2 == 0
+    copies = [
+        pltpu.make_async_copy(prolong_hbm.at[jnp.where(even_x, cx - 1, 0)], near_x_ref, sems.at[0]),
+        pltpu.make_async_copy(prolong_hbm.at[jnp.where(even_x, 0, cx - 1)], far_x_ref, sems.at[1]),
+        pltpu.make_async_copy(
+            prolong_hbm.at[:, jnp.where(even_y, cy - 1, 0)], near_y_ref, sems.at[2]
+        ),
+        pltpu.make_async_copy(
+            prolong_hbm.at[:, jnp.where(even_y, 0, cy - 1)], far_y_ref, sems.at[3]
+        ),
+    ]
+    for copy in copies:
+        copy.start()
+    for copy in copies:
+        copy.wait()
+
+
+def left_kernel(
+    prolong_hbm, couplings_hbm, left_ref, rows_ref, prolong_ref, couplings_ref, wide_ref, sems
+):
+    size = prolong_hbm.shape[0] // CHUNKS
+    fetch = [pltpu.make_async_copy(prolong_hbm, prolong_ref, sems.at[CHUNKS])]
+    for chunk in range(CHUNKS):
+        part = pl.ds(chunk * size, size)
+        fetch.append(
+            pltpu.make_async_copy(couplings_hbm.at[part], couplings_ref.at[part], sems.at[chunk])
+        )
+    for copy in fetch:
+        copy.start()
+    fetch[0].wait()
+    for cell in range(prolong_hbm.shape[0]):
+        if cell % size == 0:
+            fetch[1 + cell // size].wait()
         rows = unpacked(prolong_ref[cell], wide_ref.at[cell % 4])
         rows_ref[cell] = rows
         product = lax.dot_general(
@@ -116,7 +155,8 @@
         out_ref[ring, FIRST * 32 : FIRST * 32 + 16, :] = row.astype(jnp.bfloat16)
 
 
-def gather_kernel(blocks, got_ref, late_ref, tags_ref, any_ref, out_ref, sums_ref):
+def ring_kernel(blocks, with_late, got_ref, *rest):
+    late_ref, (tags_ref, out_ref, any_ref, sums_ref) = rest[0] if with_late else None, rest[-4:]
     sums_ref[...] = jnp.zeros_like(sums_ref)
 
     def add(ring, slot, from_ref, place):
@@ -127,14 +167,15 @@
     for ring in range(RING):
         for slot in range(FIRST):
             add(ring, slot, got_ref, slot)
-
-    @pl.when(any_ref[0] != 0)
-    def _():
-        for ring in range(RING):
+        if with_late:
             for slot in range(FIRST, SLOTS):
                 add(ring, slot, late_ref, slot - FIRST)
 
     out_ref[...] = sums_ref[:blocks].astype(jnp.bfloat16)
+    any_late = tags_ref[0, SLOTS]
+    for ring in range(1, RING):
+        any_late = jnp.maximum(any_late, tags_ref[ring, SLOTS])
+    any_ref[0] = any_late
 
 
 def shards(couplings, prolong, present, entries, owners, targets):
@@ -145,19 +186,27 @@
     aside = [[x * RING + z for x in range(across)] for z in range(RING)]
     owned = 16
 
-    def swapped(head, tail, axis):
+    edges = pl.pallas_call(
+        lambda *refs: edge_kernel(cx, cy, *refs),
+        out_shape=(jax.ShapeDtypeStruct((cy, 32, 128), jnp.bfloat16),) * 2
+        + (jax.ShapeDtypeStruct((cx, 32, 128), jnp.bfloat16),) * 2,
+        in_specs=[ANY],
+        out_specs=(ANY,) * 4,
+        scratch_shapes=[pltpu.SemaphoreType.DMA((4,))],
+        name="edge_blocks",
+    )(in_hbm(prolong))
+
+    def swapped(near, far, axis):
         size = lax.axis_size(axis)
-        even = lax.axis_index(axis) % 2 == 0
-        near = [(i, i ^ 1) for i in range(size)]
-        far = [(i, i + 1) for i in range(1, size - 1, 2)]
-        far = far + [(j, i) for i, j in far]
+        pairs = [(i, i + 1) for i in range(1, size - 1, 2)]
+        pairs = pairs + [(j, i) for i, j in pairs]
         return (
-            lax.ppermute(jnp.where(even, tail, head), axis, near),
-            lax.ppermute(jnp.where(even, head, tail), axis, far),
+            lax.ppermute(near, axis, [(i, i ^ 1) for i in range(size)]),
+            lax.ppermute(far, axis, pairs),
         )
 
-    near_x, far_x = swapped(prolong[0], prolong[cx - 1], "gx")
-    near_y, far_y = swapped(prolong[:, 0], prolong[:, cy - 1], "gy")
+    near_x, far_x = swapped(edges[0], edges[1], "gx")
+    near_y, far_y = swapped(edges[2], edges[3], "gy")
 
     left, rows = pl.pallas_call(
         left_kernel,
@@ -165,15 +214,20 @@
             jax.ShapeDtypeStruct((cells, 5, 64, 64), jnp.bfloat16),
             jax.ShapeDtypeStruct((cells, 64, 128), jnp.bfloat16),
         ),
-        in_specs=[VMEM, VMEM],
+        in_specs=[ANY, ANY],
         out_specs=(VMEM, VMEM),
-        scratch_shapes=[pltpu.VMEM((4, 64, 128), jnp.float32)],
+        scratch_shapes=[
+            pltpu.VMEM((cells, 32, 128), jnp.bfloat16),
+            pltpu.VMEM((cells, 64, 320), jnp.bfloat16),
+            pltpu.VMEM((4, 64, 128), jnp.float32),
+            pltpu.SemaphoreType.DMA((CHUNKS + 1,)),
+        ],
         compiler_params=PARAMS,
         cost_estimate=pl.CostEstimate(
             flops=cells * 5 * 2 * 64**3 * 8, bytes_accessed=cells * 90000, transcendentals=0
         ),
         name="left_factor",
-    )(prolong.reshape(cells, 32, 128), couplings.reshape(cells, 64, 320))
+    )(in_hbm(prolong.reshape(cells, 32, 128)), in_hbm(couplings.reshape(cells, 64, 320)))
 
     outgoing, outgoing_late = pl.pallas_call(
         lambda *refs: partial_kernel(cx, cy, *refs),
@@ -208,20 +262,29 @@
         return lax.all_to_all(array, "gy", 0, 0, axis_index_groups=along, tiled=True)
 
     got = exchange(outgoing)
-    heads = got[:, FIRST * 32, : SLOTS + 1].astype(jnp.int32)
-    tags = heads[:, :SLOTS]
-    any_late = jnp.max(heads[:, SLOTS])
-    got_late = lax.cond(any_late > 0, exchange, lambda array: array, outgoing_late)
+    tags = got[:, FIRST * 32, : SLOTS + 1].astype(jnp.int32)
     blocks = across * owned
-    dense = pl.pallas_call(
-        lambda *refs: gather_kernel(blocks, *refs),
-        out_shape=jax.ShapeDtypeStruct((blocks, 32, 128), jnp.bfloat16),
-        in_specs=[VMEM, VMEM, SMEM, SMEM],
-        out_specs=VMEM,
-        scratch_shapes=[pltpu.VMEM((blocks + 1, 32, 128), jnp.float32)],
-        compiler_params=PARAMS,
-        name="ring_sums",
-    )(got, got_late, tags, any_late.reshape(1))
+
+    def ring_sums(*arrays):
+        return pl.pallas_call(
+            lambda *refs: ring_kernel(blocks, len(arrays) == 2, *refs),
+            out_shape=(
+                jax.ShapeDtypeStruct((blocks, 32, 128), jnp.bfloat16),
+                jax.ShapeDtypeStruct((1,), jnp.int32),
+            ),
+            in_specs=[VMEM] * len(arrays) + [SMEM],
+            out_specs=(VMEM, SMEM),
+            scratch_shapes=[pltpu.VMEM((blocks + 1, 32, 128), jnp.float32)],
+            compiler_params=PARAMS,
+            name="ring_sums" if len(arrays) == 1 else "ring_sums_late",
+        )(*arrays, tags)
+
+    dense, any_late = ring_sums(got)
+    dense = lax.cond(
+        any_late[0] > 0,
+        lambda: ring_sums(got, exchange(outgoing_late))[0],
+        lambda: dense,
+    )
     pieces = lax.all_to_all(
         dense.reshape(across, owned * 32, 128), "gy", 0, 0, axis_index_groups=aside, tiled=True
     )

time: 103 us -> 104 us (level)
  the two profiles are of different devices: /device:TPU:24 before, /device:TPU:25 now
where the time goes in v6:
time: 104 us
  blocking collectives  75 us (72%)
  Pallas kernels  15.7 us (15%)
  starting transfers between devices  11.6 us (11%)
    all_to_all x1, blocking collectives, exchange(): lax.all_to_all(array, 'gy', 0, 0, axis_index_groups=along, tiled=True)  64.1 us
    all_to_all x1, blocking collectives, shards(): lax.all_to_all(dense.reshape(across, owned * 32, 128), 'gy', 0, 0, axis_i...  10.9 us
    pallas_call x1, Pallas kernels, shards(): pl.pallas_call(lambda *refs: edge_kernel(cx, cy, *refs), out_shape=(jax.S...  7.11 us
    ppermute x2, starting transfers between devices, swapped(): lax.ppermute(near, axis, [(i, i ^ 1) for i in range(size)])  6.58 us
    ppermute x2, starting transfers between devices, swapped(): lax.ppermute(far, axis, pairs)  4.98 us
    pallas_call x1, Pallas kernels, shards(): pl.pallas_call(left_kernel, out_shape=(jax.ShapeDtypeStruct((cells, 5, 64...  4.29 us
    pallas_call x1, Pallas kernels, shards(): pl.pallas_call(lambda *refs: partial_kernel(cx, cy, *refs), out_shape=(ja...  2.49 us
  transfers between devices with their start and end apart: 4, of which 0 were waited for; matrix products, arithmetic and copies ran while one was open for 0% of the time, Pallas kernels for 4%

profile of v6, /device:TPU:25, one launch (start us, length us, event | category | flops | bytes accessed | tf_op | source)
XLA Modules:
  0.0 103.8 jit_solution(9488092848827533163)
XLA Ops:
  0.0 0.0 copy-start.3
  0.0 0.0 copy-start.2
  0.0 0.0 copy-start
  0.0 0.0 copy-start.1
  0.0 7.1 %edge_blocks.1 = (bf16[8,32,128]{2,1,0:T(8,128)(2,1)}, bf16[8,32,128]{2,1,0:T(8,128)(2,1)}, bf16[4,32,128]{2,1,0:T(8,128)(2,1)}, bf16[4,32,128]{2,1,0:T(8,128)(2,1)}) custom-call(bf16[4,8,32,128]{3,2,1,0:T(8,128)(2,1)} %refs_0_.1), custom_call_target="tpu_custom_call" | custom-call | tf_op jit(solution)/shard_map/edge_blocks/pallas_call | solution.py:189
  7.1 2.6 %collective-permute-start = (bf16[8,32,128]{2,1,0:T(8,128)(2,1)}, bf16[8,32,128]{2,1,0:T(8,128)(2,1)S(1)}, u32[]{:S(2)}, u32[]{:S(2)}) collective-permute-start(bf16[8,32,128]{2,1,0:T(8,128)(2,1)} %get-tuple-element.31), channel_id=1, source_target_pairs={{0,64},{64,0},{128,192},{192,128},{256,320},{320,256},{384,448},{4... | collective-permute-start | bytes 196616 | tf_op jit(solution)/shard_map/ppermute | solution.py:204
  9.7 4.3 %collective-permute-start.1 = (bf16[8,32,128]{2,1,0:T(8,128)(2,1)}, bf16[8,32,128]{2,1,0:T(8,128)(2,1)S(1)}, u32[]{:S(2)}, u32[]{:S(2)}) collective-permute-start(bf16[8,32,128]{2,1,0:T(8,128)(2,1)} %get-tuple-element.32), channel_id=1, source_target_pairs={{64,128},{192,256},{320,384},{448,512},{576,640},{704,768},{832,89... | collective-permute-start | bytes 196616 | tf_op jit(solution)/shard_map/ppermute | solution.py:205
  14.0 4.0 %collective-permute-start.2 = (bf16[4,32,128]{2,1,0:T(8,128)(2,1)}, bf16[4,32,128]{2,1,0:T(8,128)(2,1)S(1)}, u32[]{:S(2)}, u32[]{:S(2)}) collective-permute-start(bf16[4,32,128]{2,1,0:T(8,128)(2,1)} %get-tuple-element.33), channel_id=1, source_target_pairs={{0,1},{1,0},{2,3},{3,2},{4,5},{5,4},{6,7},{7,6},{8,9},{9,8},{10,11... | collective-permute-start | bytes 98312 | tf_op jit(solution)/shard_map/ppermute | solution.py:204
  18.1 0.7 collective-permute-start.3
  18.7 4.3 %left_factor.1 = (bf16[32,5,64,64]{3,2,1,0:T(8,128)(2,1)S(1)}, bf16[32,64,128]{2,1,0:T(8,128)(2,1)S(1)}) custom-call(bf16[32,32,128]{2,1,0:T(8,128)(2,1)} %bitcast.19, bf16[32,64,320]{2,1,0:T(8,128)(2,1)} %bitcast.20), custom_call_target="tpu_custom_call" | custom-call | flops 671088640 | bytes 2880000 | tf_op jit(solution)/shard_map/left_factor/pallas_call | solution.py:211
  23.0 0.0 collective-permute-done.2.refs_4_
  23.0 0.0 collective-permute-done.3.refs_5_
  23.0 0.0 collective-permute-done.refs_2_
  23.1 0.0 collective-permute-done.1.refs_3_
  23.1 0.0 copy-done.3
  23.1 0.0 copy-done.2
  23.1 0.0 copy-done
  23.1 0.0 copy-done.1
  23.1 2.5 %partial_blocks.1 = (bf16[16,208,128]{2,1,0:T(8,128)(2,1)S(1)}, bf16[16,64,128]{2,1,0:T(8,128)(2,1)S(1)}) custom-call(bf16[32,5,64,64]{3,2,1,0:T(8,128)(2,1)S(1)} %get-tuple-element.29.refs_0_, bf16[32,64,128]{2,1,0:T(8,128)(2,1)S(1)} %get-tuple-element.30.refs_1_, bf16[8,32,128]{2,1,0:T(8,128)(2,1)S(1)} %collective-permute-done.refs_2_, ...), custom_call_target="tpu_custom_call" | custom-call | tf_op jit(solution)/shard_map/partial_blocks/pallas_call | solution.py:232
  25.6 64.1 %all_to_all.15.refs_0_ = bf16[16,208,128]{2,1,0:T(8,128)(2,1)S(1)} all-to-all(bf16[16,208,128]{2,1,0:T(8,128)(2,1)S(1)} %get-tuple-element.35), channel_id=1, replica_groups={{0,1,2,3,4,5,6,7,8,9,10,11,12,13,14,15},{16,17,18,19,20,21,22,23,24,25,..., dimensions={0} | all-to-all | bytes 1703936 | tf_op jit(solution)/shard_map/all_to_all | solution.py:262
  89.7 1.8 %ring_sums.1 = (bf16[64,32,128]{2,1,0:T(8,128)(2,1)S(1)}, s32[1]{0:T(128)}) custom-call(bf16[16,208,128]{2,1,0:T(8,128)(2,1)S(1)} %all_to_all.15.refs_0_, s32[16,9]{1,0:T(8,128)S(1)} %fusion.refs_1_), custom_call_target="tpu_custom_call" | custom-call | tf_op jit(solution)/shard_map/ring_sums/pallas_call | solution.py:269
  92.2 10.9 %all_to_all.16 = bf16[4,512,128]{2,1,0:T(8,128)(2,1)S(1)} all-to-all(bf16[4,512,128]{2,1,0:T(8,128)(2,1)S(1)} %bitcast.18), channel_id=1, replica_groups={{0,16,32,48},{1,17,33,49},{2,18,34,50},{3,19,35,51},{4,20,36,52},{5,21,..., dimensions={0} | all-to-all | bytes 1048576 | tf_op jit(solution)/shard_map/all_to_all | solution.py:288
  103.1 0.7 reduce_sum.12
  (3 shorter events, 0.0 us)
Async XLA Ops:
  0.0 23.1 %copy-start.3 = (s32[1,32]{1,0:T(1,128)S(1)}, s32[1,32]{1,0:T(1,128)}, u32[]{:S(2)}) copy-start(s32[1,32]{1,0:T(1,128)} %param.13) | copy-start | bytes 388
  0.0 23.1 %copy-start.2 = (s32[1,32,1]{1,2,0:T(1,128)S(1)}, s32[1,32,1]{1,2,0:T(1,128)}, u32[]{:S(2)}) copy-start(s32[1,32,1]{1,2,0:T(1,128)} %param.12) | copy-start | bytes 388
  0.0 23.1 %copy-start = (s32[4,8,5]{1,0,2:T(4,128)S(1)}, s32[4,8,5]{1,0,2:T(4,128)}, u32[]{:S(2)}) copy-start(s32[4,8,5]{1,0,2:T(4,128)} %param.11) | copy-start | bytes 1924
  0.0 23.1 %copy-start.1 = (s32[4,8,4]{1,2,0:T(4,128)S(1)}, s32[4,8,4]{1,2,0:T(4,128)}, u32[]{:S(2)}) copy-start(s32[4,8,4]{1,2,0:T(4,128)} %param.10) | copy-start | bytes 1540
  7.1 15.9 %collective-permute-start = (bf16[8,32,128]{2,1,0:T(8,128)(2,1)}, bf16[8,32,128]{2,1,0:T(8,128)(2,1)S(1)}, u32[]{:S(2)}, u32[]{:S(2)}) collective-permute-start(bf16[8,32,128]{2,1,0:T(8,128)(2,1)} %get-tuple-element.31), channel_id=1, source_target_pairs={{0,64},{64,0},{128,192},{192,128},{256,320},{320,256},{384,448},{4... | collective-permute-start | bytes 196616 | tf_op jit(solution)/shard_map/ppermute | solution.py:204
  9.7 13.3 %collective-permute-start.1 = (bf16[8,32,128]{2,1,0:T(8,128)(2,1)}, bf16[8,32,128]{2,1,0:T(8,128)(2,1)S(1)}, u32[]{:S(2)}, u32[]{:S(2)}) collective-permute-start(bf16[8,32,128]{2,1,0:T(8,128)(2,1)} %get-tuple-element.32), channel_id=1, source_target_pairs={{64,128},{192,256},{320,384},{448,512},{576,640},{704,768},{832,89... | collective-permute-start | bytes 196616 | tf_op jit(solution)/shard_map/ppermute | solution.py:205
  14.0 9.0 %collective-permute-start.2 = (bf16[4,32,128]{2,1,0:T(8,128)(2,1)}, bf16[4,32,128]{2,1,0:T(8,128)(2,1)S(1)}, u32[]{:S(2)}, u32[]{:S(2)}) collective-permute-start(bf16[4,32,128]{2,1,0:T(8,128)(2,1)} %get-tuple-element.33), channel_id=1, source_target_pairs={{0,1},{1,0},{2,3},{3,2},{4,5},{5,4},{6,7},{7,6},{8,9},{9,8},{10,11... | collective-permute-start | bytes 98312 | tf_op jit(solution)/shard_map/ppermute | solution.py:204
  18.1 5.0 %collective-permute-start.3 = (bf16[4,32,128]{2,1,0:T(8,128)(2,1)}, bf16[4,32,128]{2,1,0:T(8,128)(2,1)S(1)}, u32[]{:S(2)}, u32[]{:S(2)}) collective-permute-start(bf16[4,32,128]{2,1,0:T(8,128)(2,1)} %get-tuple-element.34), channel_id=1, source_target_pairs={{1,2},{3,4},{5,6},{7,8},{9,10},{11,12},{13,14},{15,16},{17,18},{19... | collective-permute-start | bytes 98312 | tf_op jit(solution)/shard_map/ppermute | solution.py:205

commit v7 on v6

--- a/solution.py
+++ b/solution.py
@@ -24,25 +24,6 @@
 
 def in_hbm(array):
     return pltpu.with_memory_space_constraint(array, pltpu.HBM)
-
-
-def edge_kernel(cx, cy, prolong_hbm, near_x_ref, far_x_ref, near_y_ref, far_y_ref, sems):
-    even_x = lax.axis_index("gx") % 2 == 0
-    even_y = lax.axis_index("gy") % 2 == 0
-    copies = [
-        pltpu.make_async_copy(prolong_hbm.at[jnp.where(even_x, cx - 1, 0)], near_x_ref, sems.at[0]),
-        pltpu.make_async_copy(prolong_hbm.at[jnp.where(even_x, 0, cx - 1)], far_x_ref, sems.at[1]),
-        pltpu.make_async_copy(
-            prolong_hbm.at[:, jnp.where(even_y, cy - 1, 0)], near_y_ref, sems.at[2]
-        ),
-        pltpu.make_async_copy(
-            prolong_hbm.at[:, jnp.where(even_y, 0, cy - 1)], far_y_ref, sems.at[3]
-        ),
-    ]
-    for copy in copies:
-        copy.start()
-    for copy in copies:
-        copy.wait()
 
 
 def left_kernel(
@@ -186,27 +167,19 @@
     aside = [[x * RING + z for x in range(across)] for z in range(RING)]
     owned = 16
 
-    edges = pl.pallas_call(
-        lambda *refs: edge_kernel(cx, cy, *refs),
-        out_shape=(jax.ShapeDtypeStruct((cy, 32, 128), jnp.bfloat16),) * 2
-        + (jax.ShapeDtypeStruct((cx, 32, 128), jnp.bfloat16),) * 2,
-        in_specs=[ANY],
-        out_specs=(ANY,) * 4,
-        scratch_shapes=[pltpu.SemaphoreType.DMA((4,))],
-        name="edge_blocks",
-    )(in_hbm(prolong))
-
-    def swapped(near, far, axis):
+    def swapped(head, tail, axis):
         size = lax.axis_size(axis)
-        pairs = [(i, i + 1) for i in range(1, size - 1, 2)]
-        pairs = pairs + [(j, i) for i, j in pairs]
+        even = lax.axis_index(axis) % 2 == 0
+        near = [(i, i ^ 1) for i in range(size)]
+        far = [(i, i + 1) for i in range(1, size - 1, 2)]
+        far = far + [(j, i) for i, j in far]
         return (
-            lax.ppermute(near, axis, [(i, i ^ 1) for i in range(size)]),
-            lax.ppermute(far, axis, pairs),
+            lax.ppermute(jnp.where(even, tail, head), axis, near),
+            lax.ppermute(jnp.where(even, head, tail), axis, far),
         )
 
-    near_x, far_x = swapped(edges[0], edges[1], "gx")
-    near_y, far_y = swapped(edges[2], edges[3], "gy")
+    near_x, far_x = swapped(prolong[0], prolong[cx - 1], "gx")
+    near_y, far_y = swapped(prolong[:, 0], prolong[:, cy - 1], "gy")
 
     left, rows = pl.pallas_call(
         left_kernel,

time: 104 us -> 99.8 us (0.960)
  the two profiles are of different devices: /device:TPU:25 before, /device:TPU:24 now
where the time goes in v7:
time: 99.8 us; the launch traced here: 99.4 us
  blocking collectives  72.2 us (72%)
  starting transfers between devices  15.3 us (15%)
  Pallas kernels  8.58 us (9%)
  other arithmetic  2.45 us (2%)
    all_to_all x1, blocking collectives, exchange(): lax.all_to_all(array, 'gy', 0, 0, axis_index_groups=along, tiled=True)  60.1 us
    ppermute x2, starting transfers between devices, swapped(): lax.ppermute(jnp.where(even, tail, head), axis, near)  12.7 us
    all_to_all x1, blocking collectives, shards(): lax.all_to_all(dense.reshape(across, owned * 32, 128), 'gy', 0, 0, axis_i...  12.2 us
    pallas_call x1, Pallas kernels, shards(): pl.pallas_call(left_kernel, out_shape=(jax.ShapeDtypeStruct((cells, 5, 64...  4.29 us
    ppermute x2, starting transfers between devices, swapped(): lax.ppermute(jnp.where(even, head, tail), axis, far)  2.58 us
    pallas_call x1, Pallas kernels, shards(): pl.pallas_call(lambda *refs: partial_kernel(cx, cy, *refs), out_shape=(ja...  2.49 us
  transfers between devices with their start and end apart: 4, of which 0 were waited for; matrix products, arithmetic and copies ran while one was open for 1% of the time, Pallas kernels for 4%

profile of v7, /device:TPU:24, one launch (start us, length us, event | category | flops | bytes accessed | tf_op | source)
XLA Modules:
  0.0 99.4 jit_solution(10956597023754479155)
XLA Ops:
  0.0 0.0 copy-start.3
  0.0 0.0 copy-start.2
  0.0 0.0 copy-start
  0.0 0.0 copy-start.1
  0.0 0.9 select_bitcast_fusion
  0.9 1.9 %collective-permute-start.1 = (bf16[8,32,128]{2,1,0:T(8,128)(2,1)S(1)}, bf16[8,32,128]{2,1,0:T(8,128)(2,1)S(1)}, u32[]{:S(2)}, u32[]{:S(2)}) collective-permute-start(bf16[8,32,128]{2,1,0:T(8,128)(2,1)S(1)} %get-tuple-element.36), channel_id=1, source_target_pairs={{64,128},{192,256},{320,384},{448,512},{576,640},{704,768},{832,89... | collective-permute-start | bytes 196616 | tf_op jit(solution)/shard_map/ppermute | solution.py:178
  2.9 4.8 %collective-permute-start = (bf16[8,32,128]{2,1,0:T(8,128)(2,1)S(1)}, bf16[8,32,128]{2,1,0:T(8,128)(2,1)S(1)}, u32[]{:S(2)}, u32[]{:S(2)}) collective-permute-start(bf16[8,32,128]{2,1,0:T(8,128)(2,1)S(1)} %get-tuple-element.37), channel_id=1, source_target_pairs={{0,64},{64,0},{128,192},{192,128},{256,320},{320,256},{384,448},{4... | collective-permute-start | bytes 196616 | tf_op jit(solution)/shard_map/ppermute | solution.py:177
  7.7 0.8 fusion.1
  8.5 0.7 collective-permute-start.3
  9.1 7.9 %collective-permute-start.2 = (bf16[4,32,128]{2,1,0:T(8,128)(2,1)S(1)}, bf16[4,32,128]{2,1,0:T(8,128)(2,1)S(1)}, u32[]{:S(2)}, u32[]{:S(2)}) collective-permute-start(bf16[4,32,128]{2,1,0:T(8,128)(2,1)S(1)} %get-tuple-element.35), channel_id=1, source_target_pairs={{0,1},{1,0},{2,3},{3,2},{4,5},{5,4},{6,7},{7,6},{8,9},{9,8},{10,11... | collective-permute-start | bytes 98312 | tf_op jit(solution)/shard_map/ppermute | solution.py:177
  17.1 4.3 %left_factor.1 = (bf16[32,5,64,64]{3,2,1,0:T(8,128)(2,1)S(1)}, bf16[32,64,128]{2,1,0:T(8,128)(2,1)S(1)}) custom-call(bf16[32,32,128]{2,1,0:T(8,128)(2,1)} %bitcast.37, bf16[32,64,320]{2,1,0:T(8,128)(2,1)} %bitcast.38), custom_call_target="tpu_custom_call" | custom-call | flops 671088640 | bytes 2880000 | tf_op jit(solution)/shard_map/left_factor/pallas_call | solution.py:184
  21.4 0.0 collective-permute-done.3.refs_5_
  21.4 0.0 collective-permute-done.2.refs_4_
  21.4 0.0 collective-permute-done.1.refs_3_
  21.4 0.0 collective-permute-done.refs_2_
  21.4 0.0 copy-done.3
  21.4 0.0 copy-done.2
  21.4 0.0 copy-done
  21.4 0.0 copy-done.1
  21.4 2.5 %partial_blocks.1 = (bf16[16,208,128]{2,1,0:T(8,128)(2,1)S(1)}, bf16[16,64,128]{2,1,0:T(8,128)(2,1)S(1)}) custom-call(bf16[32,5,64,64]{3,2,1,0:T(8,128)(2,1)S(1)} %get-tuple-element.25.refs_0_, bf16[32,64,128]{2,1,0:T(8,128)(2,1)S(1)} %get-tuple-element.26.refs_1_, bf16[8,32,128]{2,1,0:T(8,128)(2,1)S(1)} %collective-permute-done.refs_2_, ...), custom_call_target="tpu_custom_call" | custom-call | tf_op jit(solution)/shard_map/partial_blocks/pallas_call | solution.py:205
  23.9 60.1 %all_to_all.15.refs_0_ = bf16[16,208,128]{2,1,0:T(8,128)(2,1)S(1)} all-to-all(bf16[16,208,128]{2,1,0:T(8,128)(2,1)S(1)} %get-tuple-element.27), channel_id=1, replica_groups={{0,1,2,3,4,5,6,7,8,9,10,11,12,13,14,15},{16,17,18,19,20,21,22,23,24,25,..., dimensions={0} | all-to-all | bytes 1703936 | tf_op jit(solution)/shard_map/all_to_all | solution.py:235
  84.0 1.8 %ring_sums.1 = (bf16[64,32,128]{2,1,0:T(8,128)(2,1)S(1)}, s32[1]{0:T(128)}) custom-call(bf16[16,208,128]{2,1,0:T(8,128)(2,1)S(1)} %all_to_all.15.refs_0_, s32[16,9]{1,0:T(8,128)S(1)} %fusion.2.refs_1_), custom_call_target="tpu_custom_call" | custom-call | tf_op jit(solution)/shard_map/ring_sums/pallas_call | solution.py:242
  86.5 12.2 %all_to_all.16 = bf16[4,512,128]{2,1,0:T(8,128)(2,1)S(1)} all-to-all(bf16[4,512,128]{2,1,0:T(8,128)(2,1)S(1)} %bitcast.36), channel_id=1, replica_groups={{0,16,32,48},{1,17,33,49},{2,18,34,50},{3,19,35,51},{4,20,36,52},{5,21,..., dimensions={0} | all-to-all | bytes 1048576 | tf_op jit(solution)/shard_map/all_to_all | solution.py:261
  98.7 0.7 reduce_sum.12
  (3 shorter events, 0.0 us)
Async XLA Ops:
  0.0 21.4 %copy-start.3 = (s32[1,32]{1,0:T(1,128)S(1)}, s32[1,32]{1,0:T(1,128)}, u32[]{:S(2)}) copy-start(s32[1,32]{1,0:T(1,128)} %param.13) | copy-start | bytes 388
  0.0 21.4 %copy-start.2 = (s32[1,32,1]{1,2,0:T(1,128)S(1)}, s32[1,32,1]{1,2,0:T(1,128)}, u32[]{:S(2)}) copy-start(s32[1,32,1]{1,2,0:T(1,128)} %param.12) | copy-start | bytes 388
  0.0 21.4 %copy-start = (s32[4,8,5]{1,0,2:T(4,128)S(1)}, s32[4,8,5]{1,0,2:T(4,128)}, u32[]{:S(2)}) copy-start(s32[4,8,5]{1,0,2:T(4,128)} %param.11) | copy-start | bytes 1924
  0.0 21.4 %copy-start.1 = (s32[4,8,4]{1,2,0:T(4,128)S(1)}, s32[4,8,4]{1,2,0:T(4,128)}, u32[]{:S(2)}) copy-start(s32[4,8,4]{1,2,0:T(4,128)} %param.10) | copy-start | bytes 1540
  0.9 20.4 %collective-permute-start.1 = (bf16[8,32,128]{2,1,0:T(8,128)(2,1)S(1)}, bf16[8,32,128]{2,1,0:T(8,128)(2,1)S(1)}, u32[]{:S(2)}, u32[]{:S(2)}) collective-permute-start(bf16[8,32,128]{2,1,0:T(8,128)(2,1)S(1)} %get-tuple-element.36), channel_id=1, source_target_pairs={{64,128},{192,256},{320,384},{448,512},{576,640},{704,768},{832,89... | collective-permute-start | bytes 196616 | tf_op jit(solution)/shard_map/ppermute | solution.py:178
  2.9 18.5 %collective-permute-start = (bf16[8,32,128]{2,1,0:T(8,128)(2,1)S(1)}, bf16[8,32,128]{2,1,0:T(8,128)(2,1)S(1)}, u32[]{:S(2)}, u32[]{:S(2)}) collective-permute-start(bf16[8,32,128]{2,1,0:T(8,128)(2,1)S(1)} %get-tuple-element.37), channel_id=1, source_target_pairs={{0,64},{64,0},{128,192},{192,128},{256,320},{320,256},{384,448},{4... | collective-permute-start | bytes 196616 | tf_op jit(solution)/shard_map/ppermute | solution.py:177
  8.5 12.9 %collective-permute-start.3 = (bf16[4,32,128]{2,1,0:T(8,128)(2,1)S(1)}, bf16[4,32,128]{2,1,0:T(8,128)(2,1)S(1)}, u32[]{:S(2)}, u32[]{:S(2)}) collective-permute-start(bf16[4,32,128]{2,1,0:T(8,128)(2,1)S(1)} %get-tuple-element.34), channel_id=1, source_target_pairs={{1,2},{3,4},{5,6},{7,8},{9,10},{11,12},{13,14},{15,16},{17,18},{19... | collective-permute-start | bytes 98312 | tf_op jit(solution)/shard_map/ppermute | solution.py:178
  9.1 12.2 %collective-permute-start.2 = (bf16[4,32,128]{2,1,0:T(8,128)(2,1)S(1)}, bf16[4,32,128]{2,1,0:T(8,128)(2,1)S(1)}, u32[]{:S(2)}, u32[]{:S(2)}) collective-permute-start(bf16[4,32,128]{2,1,0:T(8,128)(2,1)S(1)} %get-tuple-element.35), channel_id=1, source_target_pairs={{0,1},{1,0},{2,3},{3,2},{4,5},{5,4},{6,7},{7,6},{8,9},{9,8},{10,11... | collective-permute-start | bytes 98312 | tf_op jit(solution)/shard_map/ppermute | solution.py:177

commit v8 on v7

--- a/solution.py
+++ b/solution.py
@@ -7,7 +7,7 @@
 
 RING = 16
 SLOTS = 8
-FIRST = 6
+FIRST = 4
 VMEM = pl.BlockSpec(memory_space=pltpu.VMEM)
 ANY = pl.BlockSpec(memory_space=pl.ANY)
 CHUNKS = 8

time: 99.8 us -> 125 us (1.25)
  blocking collectives: 72.2 us -> 95.6 us
  Pallas kernels: 8.58 us -> 10.3 us
    all_to_all x1 -> x2, blocking collectives: 60.1 us -> 83.4 us  [exchange(): lax.all_to_all(array, 'gy', 0, 0, axis_index_groups=along, tiled=True)]
    pallas_call x1 -> x2, Pallas kernels: 1.79 us -> 3.52 us  [ring_sums(): pl.pallas_call(lambda *refs: ring_kernel(blocks, len(arrays) == 2, *refs)...]
  transfers between devices with their start and end apart: 4 -> 4, of which waited for: 0 -> 0; matrix products, arithmetic and copies ran while one was open for 1% -> 1% of each run, Pallas kernels for 4% -> 3%
where the time goes in v8:
time: 125 us; the launch traced here: 124 us
  blocking collectives  95.6 us (76%)
  starting transfers between devices  15.3 us (12%)
  Pallas kernels  10.3 us (8%)
  other arithmetic  2.45 us (2%)
    all_to_all x2, blocking collectives, exchange(): lax.all_to_all(array, 'gy', 0, 0, axis_index_groups=along, tiled=True)  83.4 us
    ppermute x2, starting transfers between devices, swapped(): lax.ppermute(jnp.where(even, tail, head), axis, near)  12.7 us
    all_to_all x1, blocking collectives, shards(): lax.all_to_all(dense.reshape(across, owned * 32, 128), 'gy', 0, 0, axis_i...  12.2 us
    pallas_call x1, Pallas kernels, shards(): pl.pallas_call(left_kernel, out_shape=(jax.ShapeDtypeStruct((cells, 5, 64...  4.29 us
    pallas_call x2, Pallas kernels, ring_sums(): pl.pallas_call(lambda *refs: ring_kernel(blocks, len(arrays) == 2, *refs)...  3.52 us
    ppermute x2, starting transfers between devices, swapped(): lax.ppermute(jnp.where(even, head, tail), axis, far)  2.58 us
  transfers between devices with their start and end apart: 4, of which 0 were waited for; matrix products, arithmetic and copies ran while one was open for 1% of the time, Pallas kernels for 3%

profile of v8, /device:TPU:24, one launch (start us, length us, event | category | flops | bytes accessed | tf_op | source)
XLA Modules:
  0.0 124.5 jit_solution(3767702321611525013)
XLA Ops:
  0.0 0.0 copy-start.3
  0.0 0.0 copy-start.2
  0.0 0.0 copy-start
  0.0 0.0 copy-start.1
  0.0 0.9 select_bitcast_fusion
  0.9 1.9 %collective-permute-start.1 = (bf16[8,32,128]{2,1,0:T(8,128)(2,1)S(1)}, bf16[8,32,128]{2,1,0:T(8,128)(2,1)S(1)}, u32[]{:S(2)}, u32[]{:S(2)}) collective-permute-start(bf16[8,32,128]{2,1,0:T(8,128)(2,1)S(1)} %get-tuple-element.36), channel_id=1, source_target_pairs={{64,128},{192,256},{320,384},{448,512},{576,640},{704,768},{832,89... | collective-permute-start | bytes 196616 | tf_op jit(solution)/shard_map/ppermute | solution.py:178
  2.9 4.8 %collective-permute-start = (bf16[8,32,128]{2,1,0:T(8,128)(2,1)S(1)}, bf16[8,32,128]{2,1,0:T(8,128)(2,1)S(1)}, u32[]{:S(2)}, u32[]{:S(2)}) collective-permute-start(bf16[8,32,128]{2,1,0:T(8,128)(2,1)S(1)} %get-tuple-element.37), channel_id=1, source_target_pairs={{0,64},{64,0},{128,192},{192,128},{256,320},{320,256},{384,448},{4... | collective-permute-start | bytes 196616 | tf_op jit(solution)/shard_map/ppermute | solution.py:177
  7.7 0.8 fusion.1
  8.5 0.7 collective-permute-start.3
  9.1 7.9 %collective-permute-start.2 = (bf16[4,32,128]{2,1,0:T(8,128)(2,1)S(1)}, bf16[4,32,128]{2,1,0:T(8,128)(2,1)S(1)}, u32[]{:S(2)}, u32[]{:S(2)}) collective-permute-start(bf16[4,32,128]{2,1,0:T(8,128)(2,1)S(1)} %get-tuple-element.35), channel_id=1, source_target_pairs={{0,1},{1,0},{2,3},{3,2},{4,5},{5,4},{6,7},{7,6},{8,9},{9,8},{10,11... | collective-permute-start | bytes 98312 | tf_op jit(solution)/shard_map/ppermute | solution.py:177
  17.1 4.3 %left_factor.1 = (bf16[32,5,64,64]{3,2,1,0:T(8,128)(2,1)S(1)}, bf16[32,64,128]{2,1,0:T(8,128)(2,1)S(1)}) custom-call(bf16[32,32,128]{2,1,0:T(8,128)(2,1)} %bitcast.37, bf16[32,64,320]{2,1,0:T(8,128)(2,1)} %bitcast.38), custom_call_target="tpu_custom_call" | custom-call | flops 671088640 | bytes 2880000 | tf_op jit(solution)/shard_map/left_factor/pallas_call | solution.py:184
  21.4 0.0 collective-permute-done.3.refs_5_
  21.4 0.0 collective-permute-done.2.refs_4_
  21.4 0.0 collective-permute-done.1.refs_3_
  21.4 0.0 collective-permute-done.refs_2_
  21.4 0.0 copy-done.3
  21.4 0.0 copy-done.2
  21.4 0.0 copy-done
  21.4 0.0 copy-done.1
  21.4 2.5 %partial_blocks.1 = (bf16[16,144,128]{2,1,0:T(8,128)(2,1)S(1)}, bf16[16,128,128]{2,1,0:T(8,128)(2,1)S(1)}) custom-call(bf16[32,5,64,64]{3,2,1,0:T(8,128)(2,1)S(1)} %get-tuple-element.25.refs_0_, bf16[32,64,128]{2,1,0:T(8,128)(2,1)S(1)} %get-tuple-element.26.refs_1_, bf16[8,32,128]{2,1,0:T(8,128)(2,1)S(1)} %collective-permute-done.refs_2_, ...), custom_call_target="tpu_custom_call" | custom-call | tf_op jit(solution)/shard_map/partial_blocks/pallas_call | solution.py:205
  23.9 51.6 %all_to_all.15.refs_0_ = bf16[16,144,128]{2,1,0:T(8,128)(2,1)S(1)} all-to-all(bf16[16,144,128]{2,1,0:T(8,128)(2,1)S(1)} %get-tuple-element.27), channel_id=1, replica_groups={{0,1,2,3,4,5,6,7,8,9,10,11,12,13,14,15},{16,17,18,19,20,21,22,23,24,25,..., dimensions={0} | all-to-all | bytes 1179648 | tf_op jit(solution)/shard_map/all_to_all | solution.py:235
  75.6 1.6 %ring_sums.1 = (bf16[64,32,128]{2,1,0:T(8,128)(2,1)S(1)}, s32[1]{0:T(128)}) custom-call(bf16[16,144,128]{2,1,0:T(8,128)(2,1)S(1)} %all_to_all.15.refs_0_, s32[16,9]{1,0:T(8,128)S(1)} %fusion.2.refs_1_), custom_call_target="tpu_custom_call" | custom-call | tf_op jit(solution)/shard_map/ring_sums/pallas_call | solution.py:242
  77.8 33.7 %conditional.1 = (bf16[64,32,128]{2,1,0:T(8,128)(2,1)S(1)}) conditional(s32[]{:T(128)} %bitcast.11, bf16[64,32,128]{2,1,0:T(8,128)(2,1)S(1)} %get-tuple-element.29, (bf16[16,128,128]{2,1,0:T(8,128)(2,1)S(1)}, bf16[16,144,128]{2,1,0:T(8,128)(2,1)S(1)}, s32[16,9]{1,0:T(8,128)S(1)}) %tuple.11), branch_computations={%region_0.1_spmd, %region_1.2_spmd} | conditional | bytes 1048584 | solution.py:256
  77.8 31.8 %all_to_all.14.refs_1_ = bf16[16,128,128]{2,1,0:T(8,128)(2,1)S(1)} all-to-all(bf16[16,128,128]{2,1,0:T(8,128)(2,1)S(1)} %get-tuple-element.16), channel_id=1, replica_groups={{0,1,2,3,4,5,6,7,8,9,10,11,12,13,14,15},{16,17,18,19,20,21,22,23,24,25,..., dimensions={0} | all-to-all | bytes 1048576 | tf_op jit(solution)/shard_map/cond/branch_1_fun/all_to_all | solution.py:235
  109.6 1.9 %ring_sums_late.1 = (bf16[64,32,128]{2,1,0:T(8,128)(2,1)S(1)}, s32[1]{0:T(128)}) custom-call(bf16[16,144,128]{2,1,0:T(8,128)(2,1)S(1)} %get-tuple-element.15.refs_0_, bf16[16,128,128]{2,1,0:T(8,128)(2,1)S(1)} %all_to_all.14.refs_1_, s32[16,9]{1,0:T(8,128)S(1)} %get-tuple-element.17.refs_2_), custom_call_target="tpu_custom_call" | custom-call | tf_op jit(solution)/shard_map/cond/branch_1_fun/ring_sums_late/pallas_call | solution.py:242
  111.5 12.2 %all_to_all.16 = bf16[4,512,128]{2,1,0:T(8,128)(2,1)S(1)} all-to-all(bf16[4,512,128]{2,1,0:T(8,128)(2,1)S(1)} %bitcast.36), channel_id=1, replica_groups={{0,16,32,48},{1,17,33,49},{2,18,34,50},{3,19,35,51},{4,20,36,52},{5,21,..., dimensions={0} | all-to-all | bytes 1048576 | tf_op jit(solution)/shard_map/all_to_all | solution.py:261
  123.7 0.7 reduce_sum.12
  (2 shorter events, 0.0 us)
Async XLA Ops:
  0.0 21.4 %copy-start.3 = (s32[1,32]{1,0:T(1,128)S(1)}, s32[1,32]{1,0:T(1,128)}, u32[]{:S(2)}) copy-start(s32[1,32]{1,0:T(1,128)} %param.13) | copy-start | bytes 388
  0.0 21.4 %copy-start.2 = (s32[1,32,1]{1,2,0:T(1,128)S(1)}, s32[1,32,1]{1,2,0:T(1,128)}, u32[]{:S(2)}) copy-start(s32[1,32,1]{1,2,0:T(1,128)} %param.12) | copy-start | bytes 388
  0.0 21.4 %copy-start = (s32[4,8,5]{1,0,2:T(4,128)S(1)}, s32[4,8,5]{1,0,2:T(4,128)}, u32[]{:S(2)}) copy-start(s32[4,8,5]{1,0,2:T(4,128)} %param.11) | copy-start | bytes 1924
  0.0 21.4 %copy-start.1 = (s32[4,8,4]{1,2,0:T(4,128)S(1)}, s32[4,8,4]{1,2,0:T(4,128)}, u32[]{:S(2)}) copy-start(s32[4,8,4]{1,2,0:T(4,128)} %param.10) | copy-start | bytes 1540
  0.9 20.4 %collective-permute-start.1 = (bf16[8,32,128]{2,1,0:T(8,128)(2,1)S(1)}, bf16[8,32,128]{2,1,0:T(8,128)(2,1)S(1)}, u32[]{:S(2)}, u32[]{:S(2)}) collective-permute-start(bf16[8,32,128]{2,1,0:T(8,128)(2,1)S(1)} %get-tuple-element.36), channel_id=1, source_target_pairs={{64,128},{192,256},{320,384},{448,512},{576,640},{704,768},{832,89... | collective-permute-start | bytes 196616 | tf_op jit(solution)/shard_map/ppermute | solution.py:178
  2.9 18.5 %collective-permute-start = (bf16[8,32,128]{2,1,0:T(8,128)(2,1)S(1)}, bf16[8,32,128]{2,1,0:T(8,128)(2,1)S(1)}, u32[]{:S(2)}, u32[]{:S(2)}) collective-permute-start(bf16[8,32,128]{2,1,0:T(8,128)(2,1)S(1)} %get-tuple-element.37), channel_id=1, source_target_pairs={{0,64},{64,0},{128,192},{192,128},{256,320},{320,256},{384,448},{4... | collective-permute-start | bytes 196616 | tf_op jit(solution)/shard_map/ppermute | solution.py:177
  8.5 12.9 %collective-permute-start.3 = (bf16[4,32,128]{2,1,0:T(8,128)(2,1)S(1)}, bf16[4,32,128]{2,1,0:T(8,128)(2,1)S(1)}, u32[]{:S(2)}, u32[]{:S(2)}) collective-permute-start(bf16[4,32,128]{2,1,0:T(8,128)(2,1)S(1)} %get-tuple-element.34), channel_id=1, source_target_pairs={{1,2},{3,4},{5,6},{7,8},{9,10},{11,12},{13,14},{15,16},{17,18},{19... | collective-permute-start | bytes 98312 | tf_op jit(solution)/shard_map/ppermute | solution.py:178
  9.1 12.2 %collective-permute-start.2 = (bf16[4,32,128]{2,1,0:T(8,128)(2,1)S(1)}, bf16[4,32,128]{2,1,0:T(8,128)(2,1)S(1)}, u32[]{:S(2)}, u32[]{:S(2)}) collective-permute-start(bf16[4,32,128]{2,1,0:T(8,128)(2,1)S(1)} %get-tuple-element.35), channel_id=1, source_target_pairs={{0,1},{1,0},{2,3},{3,2},{4,5},{5,4},{6,7},{7,6},{8,9},{9,8},{10,11... | collective-permute-start | bytes 98312 | tf_op jit(solution)/shard_map/ppermute | solution.py:177

commit v9 on v7

--- a/solution.py
+++ b/solution.py
@@ -57,6 +57,7 @@
 def partial_kernel(
     cx,
     cy,
+    sizes,
     left_ref,
     rows_ref,
     near_x_ref,
@@ -77,7 +78,7 @@
     count = cx * cy
     sums_ref[...] = jnp.zeros_like(sums_ref)
 
-    def add(block, users):
+    def add(block, users, outside=False):
         stack = [left_ref[x * cy + y, d] for x, y, d in users]
         stack = stack[0] if len(stack) == 1 else jnp.concatenate(stack, axis=0)
         terms = jnp.dot(stack, block, preferred_element_type=jnp.float32)
@@ -85,6 +86,8 @@
             entry = entries_ref[d, x, y]
             if not isinstance(d, int) or d > 0:
                 entry = jnp.where(present_ref[x, d - 1, y] != 0, entry, count)
+            if outside is not False:
+                entry = jnp.where(outside, count, entry)
             sums_ref[entry] = sums_ref[entry] + terms[n * 64 : n * 64 + 64]
 
     for x in range(cx):
@@ -98,14 +101,16 @@
         ("gy", 0, near_y_ref),
         ("gy", 1, far_y_ref),
     ):
-        is_next = lax.axis_index(axis) % 2 == far
+        index = lax.axis_index(axis)
+        is_next = index % 2 == far
+        outside = ((index == 0) | (index == sizes[axis] - 1)) if far else False
         for n in range(cy if axis == "gx" else cx):
             block = unpacked(block_ref[n], wide_ref.at[n % 4])
             if axis == "gx":
                 user = (jnp.where(is_next, cx - 1, 0), n, jnp.where(is_next, 1, 2))
             else:
                 user = (n, jnp.where(is_next, cy - 1, 0), jnp.where(is_next, 3, 4))
-            add(block, [user])
+            add(block, [user], outside)
 
     for ring in range(RING):
         count_ref[ring] = 0
@@ -162,6 +167,7 @@
 def shards(couplings, prolong, present, entries, owners, targets):
     cx, cy = prolong.shape[0], prolong.shape[1]
     cells = cx * cy
+    sizes = {axis: lax.axis_size(axis) for axis in ("gx", "gy")}
     across = lax.axis_size("gy") // RING
     along = [[x * RING + z for z in range(RING)] for x in range(across)]
     aside = [[x * RING + z for x in range(across)] for z in range(RING)]
@@ -171,8 +177,7 @@
         size = lax.axis_size(axis)
         even = lax.axis_index(axis) % 2 == 0
         near = [(i, i ^ 1) for i in range(size)]
-        far = [(i, i + 1) for i in range(1, size - 1, 2)]
-        far = far + [(j, i) for i, j in far]
+        far = [(i, (i + 1 if i % 2 else i - 1) % size) for i in range(size)]
         return (
             lax.ppermute(jnp.where(even, tail, head), axis, near),
             lax.ppermute(jnp.where(even, head, tail), axis, far),
@@ -203,7 +208,7 @@
     )(in_hbm(prolong.reshape(cells, 32, 128)), in_hbm(couplings.reshape(cells, 64, 320)))
 
     outgoing, outgoing_late = pl.pallas_call(
-        lambda *refs: partial_kernel(cx, cy, *refs),
+        lambda *refs: partial_kernel(cx, cy, sizes, *refs),
         out_shape=(
             jax.ShapeDtypeStruct((RING, FIRST * 32 + 16, 128), jnp.bfloat16),
             jax.ShapeDtypeStruct((RING, (SLOTS - FIRST) * 32, 128), jnp.bfloat16),

time: 99.8 us -> 99.8 us (level)
  blocking collectives: 72.2 us -> 58.4 us
  starting transfers between devices: 15.3 us -> 29 us
    ppermute x2, starting transfers between devices: 2.58 us -> 22.3 us  [swapped(): lax.ppermute(jnp.where(even, head, tail), axis, far)]
    all_to_all x1, blocking collectives: 60.1 us -> 46.4 us  [exchange(): lax.all_to_all(array, 'gy', 0, 0, axis_index_groups=along, tiled=True)]
    ppermute x2, starting transfers between devices: 12.7 us -> 6.72 us  [swapped(): lax.ppermute(jnp.where(even, tail, head), axis, near)]
where the time goes in v9:
time: 99.8 us; the launch traced here: 99.4 us
  blocking collectives  58.4 us (59%)
  starting transfers between devices  29 us (29%)
  Pallas kernels  8.54 us (9%)
  other arithmetic  2.45 us (2%)
    all_to_all x1, blocking collectives, exchange(): lax.all_to_all(array, 'gy', 0, 0, axis_index_groups=along, tiled=True)  46.4 us
    ppermute x2, starting transfers between devices, swapped(): lax.ppermute(jnp.where(even, head, tail), axis, far)  22.3 us
    all_to_all x1, blocking collectives, shards(): lax.all_to_all(dense.reshape(across, owned * 32, 128), 'gy', 0, 0, axis_i...  12 us
    ppermute x2, starting transfers between devices, swapped(): lax.ppermute(jnp.where(even, tail, head), axis, near)  6.72 us
    pallas_call x1, Pallas kernels, shards(): pl.pallas_call(left_kernel, out_shape=(jax.ShapeDtypeStruct((cells, 5, 64...  4.29 us
    pallas_call x1, Pallas kernels, shards(): pl.pallas_call(lambda *refs: partial_kernel(cx, cy, sizes, *refs), out_sh...  2.48 us
  transfers between devices with their start and end apart: 4, of which 0 were waited for; matrix products, arithmetic and copies ran while one was open for 1% of the time, Pallas kernels for 4%

profile of v9, /device:TPU:24, one launch (start us, length us, event | category | flops | bytes accessed | tf_op | source)
XLA Modules:
  0.0 99.4 jit_solution(15729201554448781039)
XLA Ops:
  0.0 0.0 copy-start.3
  0.0 0.0 copy-start.2
  0.0 0.0 copy-start
  0.0 0.0 copy-start.1
  0.0 0.9 select_bitcast_fusion
  0.9 1.9 %collective-permute-start.1 = (bf16[8,32,128]{2,1,0:T(8,128)(2,1)S(1)}, bf16[8,32,128]{2,1,0:T(8,128)(2,1)S(1)}, u32[]{:S(2)}, u32[]{:S(2)}) collective-permute-start(bf16[8,32,128]{2,1,0:T(8,128)(2,1)S(1)} %get-tuple-element.36), channel_id=1, source_target_pairs={{0,960},{64,128},{128,64},{192,256},{256,192},{320,384},{384,320},... | collective-permute-start | bytes 196616 | tf_op jit(solution)/shard_map/ppermute | solution.py:183
  2.9 4.8 %collective-permute-start = (bf16[8,32,128]{2,1,0:T(8,128)(2,1)S(1)}, bf16[8,32,128]{2,1,0:T(8,128)(2,1)S(1)}, u32[]{:S(2)}, u32[]{:S(2)}) collective-permute-start(bf16[8,32,128]{2,1,0:T(8,128)(2,1)S(1)} %get-tuple-element.37), channel_id=1, source_target_pairs={{0,64},{64,0},{128,192},{192,128},{256,320},{320,256},{384,448},{4... | collective-permute-start | bytes 196616 | tf_op jit(solution)/shard_map/ppermute | solution.py:182
  7.7 0.8 fusion.1
  8.5 20.4 %collective-permute-start.3 = (bf16[4,32,128]{2,1,0:T(8,128)(2,1)S(1)}, bf16[4,32,128]{2,1,0:T(8,128)(2,1)S(1)}, u32[]{:S(2)}, u32[]{:S(2)}) collective-permute-start(bf16[4,32,128]{2,1,0:T(8,128)(2,1)S(1)} %get-tuple-element.34), channel_id=1, source_target_pairs={{0,63},{1,2},{2,1},{3,4},{4,3},{5,6},{6,5},{7,8},{8,7},{9,10},{10,... | collective-permute-start | bytes 98312 | tf_op jit(solution)/shard_map/ppermute | solution.py:183
  28.9 1.9 %collective-permute-start.2 = (bf16[4,32,128]{2,1,0:T(8,128)(2,1)S(1)}, bf16[4,32,128]{2,1,0:T(8,128)(2,1)S(1)}, u32[]{:S(2)}, u32[]{:S(2)}) collective-permute-start(bf16[4,32,128]{2,1,0:T(8,128)(2,1)S(1)} %get-tuple-element.35), channel_id=1, source_target_pairs={{0,1},{1,0},{2,3},{3,2},{4,5},{5,4},{6,7},{7,6},{8,9},{9,8},{10,11... | collective-permute-start | bytes 98312 | tf_op jit(solution)/shard_map/ppermute | solution.py:182
  30.8 4.3 %left_factor.1 = (bf16[32,5,64,64]{3,2,1,0:T(8,128)(2,1)S(1)}, bf16[32,64,128]{2,1,0:T(8,128)(2,1)S(1)}) custom-call(bf16[32,32,128]{2,1,0:T(8,128)(2,1)} %bitcast.37, bf16[32,64,320]{2,1,0:T(8,128)(2,1)} %bitcast.38), custom_call_target="tpu_custom_call" | custom-call | flops 671088640 | bytes 2880000 | tf_op jit(solution)/shard_map/left_factor/pallas_call | solution.py:189
  35.1 0.0 collective-permute-done.3.refs_5_
  35.1 0.0 collective-permute-done.2.refs_4_
  35.1 0.0 collective-permute-done.1.refs_3_
  35.2 0.0 collective-permute-done.refs_2_
  35.2 0.0 copy-done.3
  35.2 0.0 copy-done.2
  35.2 0.0 copy-done
  35.2 0.0 copy-done.1
  35.2 2.5 %partial_blocks.1 = (bf16[16,208,128]{2,1,0:T(8,128)(2,1)S(1)}, bf16[16,64,128]{2,1,0:T(8,128)(2,1)S(1)}) custom-call(bf16[32,5,64,64]{3,2,1,0:T(8,128)(2,1)S(1)} %get-tuple-element.25.refs_0_, bf16[32,64,128]{2,1,0:T(8,128)(2,1)S(1)} %get-tuple-element.26.refs_1_, bf16[8,32,128]{2,1,0:T(8,128)(2,1)S(1)} %collective-permute-done.refs_2_, ...), custom_call_target="tpu_custom_call" | custom-call | tf_op jit(solution)/shard_map/partial_blocks/pallas_call | solution.py:210
  37.7 46.4 %all_to_all.15.refs_0_ = bf16[16,208,128]{2,1,0:T(8,128)(2,1)S(1)} all-to-all(bf16[16,208,128]{2,1,0:T(8,128)(2,1)S(1)} %get-tuple-element.27), channel_id=1, replica_groups={{0,1,2,3,4,5,6,7,8,9,10,11,12,13,14,15},{16,17,18,19,20,21,22,23,24,25,..., dimensions={0} | all-to-all | bytes 1703936 | tf_op jit(solution)/shard_map/all_to_all | solution.py:240
  84.1 1.8 %ring_sums.1 = (bf16[64,32,128]{2,1,0:T(8,128)(2,1)S(1)}, s32[1]{0:T(128)}) custom-call(bf16[16,208,128]{2,1,0:T(8,128)(2,1)S(1)} %all_to_all.15.refs_0_, s32[16,9]{1,0:T(8,128)S(1)} %fusion.2.refs_1_), custom_call_target="tpu_custom_call" | custom-call | tf_op jit(solution)/shard_map/ring_sums/pallas_call | solution.py:247
  86.6 12.0 %all_to_all.16 = bf16[4,512,128]{2,1,0:T(8,128)(2,1)S(1)} all-to-all(bf16[4,512,128]{2,1,0:T(8,128)(2,1)S(1)} %bitcast.36), channel_id=1, replica_groups={{0,16,32,48},{1,17,33,49},{2,18,34,50},{3,19,35,51},{4,20,36,52},{5,21,..., dimensions={0} | all-to-all | bytes 1048576 | tf_op jit(solution)/shard_map/all_to_all | solution.py:266
  98.6 0.7 reduce_sum.12
  (3 shorter events, 0.0 us)
Async XLA Ops:
  0.0 35.2 %copy-start.3 = (s32[1,32]{1,0:T(1,128)S(1)}, s32[1,32]{1,0:T(1,128)}, u32[]{:S(2)}) copy-start(s32[1,32]{1,0:T(1,128)} %param.13) | copy-start | bytes 388
  0.0 35.2 %copy-start.2 = (s32[1,32,1]{1,2,0:T(1,128)S(1)}, s32[1,32,1]{1,2,0:T(1,128)}, u32[]{:S(2)}) copy-start(s32[1,32,1]{1,2,0:T(1,128)} %param.12) | copy-start | bytes 388
  0.0 35.2 %copy-start = (s32[4,8,5]{1,0,2:T(4,128)S(1)}, s32[4,8,5]{1,0,2:T(4,128)}, u32[]{:S(2)}) copy-start(s32[4,8,5]{1,0,2:T(4,128)} %param.11) | copy-start | bytes 1924
  0.0 35.2 %copy-start.1 = (s32[4,8,4]{1,2,0:T(4,128)S(1)}, s32[4,8,4]{1,2,0:T(4,128)}, u32[]{:S(2)}) copy-start(s32[4,8,4]{1,2,0:T(4,128)} %param.10) | copy-start | bytes 1540
  0.9 34.2 %collective-permute-start.1 = (bf16[8,32,128]{2,1,0:T(8,128)(2,1)S(1)}, bf16[8,32,128]{2,1,0:T(8,128)(2,1)S(1)}, u32[]{:S(2)}, u32[]{:S(2)}) collective-permute-start(bf16[8,32,128]{2,1,0:T(8,128)(2,1)S(1)} %get-tuple-element.36), channel_id=1, source_target_pairs={{0,960},{64,128},{128,64},{192,256},{256,192},{320,384},{384,320},... | collective-permute-start | bytes 196616 | tf_op jit(solution)/shard_map/ppermute | solution.py:183
  2.9 32.3 %collective-permute-start = (bf16[8,32,128]{2,1,0:T(8,128)(2,1)S(1)}, bf16[8,32,128]{2,1,0:T(8,128)(2,1)S(1)}, u32[]{:S(2)}, u32[]{:S(2)}) collective-permute-start(bf16[8,32,128]{2,1,0:T(8,128)(2,1)S(1)} %get-tuple-element.37), channel_id=1, source_target_pairs={{0,64},{64,0},{128,192},{192,128},{256,320},{320,256},{384,448},{4... | collective-permute-start | bytes 196616 | tf_op jit(solution)/shard_map/ppermute | solution.py:182
  8.5 26.6 %collective-permute-start.3 = (bf16[4,32,128]{2,1,0:T(8,128)(2,1)S(1)}, bf16[4,32,128]{2,1,0:T(8,128)(2,1)S(1)}, u32[]{:S(2)}, u32[]{:S(2)}) collective-permute-start(bf16[4,32,128]{2,1,0:T(8,128)(2,1)S(1)} %get-tuple-element.34), channel_id=1, source_target_pairs={{0,63},{1,2},{2,1},{3,4},{4,3},{5,6},{6,5},{7,8},{8,7},{9,10},{10,... | collective-permute-start | bytes 98312 | tf_op jit(solution)/shard_map/ppermute | solution.py:183
  28.9 6.2 %collective-permute-start.2 = (bf16[4,32,128]{2,1,0:T(8,128)(2,1)S(1)}, bf16[4,32,128]{2,1,0:T(8,128)(2,1)S(1)}, u32[]{:S(2)}, u32[]{:S(2)}) collective-permute-start(bf16[4,32,128]{2,1,0:T(8,128)(2,1)S(1)} %get-tuple-element.35), channel_id=1, source_target_pairs={{0,1},{1,0},{2,3},{3,2},{4,5},{5,4},{6,7},{7,6},{8,9},{9,8},{10,11... | collective-permute-start | bytes 98312 | tf_op jit(solution)/shard_map/ppermute | solution.py:182

commit v10 on v9

--- a/solution.py
+++ b/solution.py
@@ -42,7 +42,7 @@
     for cell in range(prolong_hbm.shape[0]):
         if cell % size == 0:
             fetch[1 + cell // size].wait()
-        rows = unpacked(prolong_ref[cell], wide_ref.at[cell % 4])
+        rows = unpacked(prolong_ref[cell], wide_ref.at[cell])
         rows_ref[cell] = rows
         product = lax.dot_general(
             rows[:, :64],
@@ -95,6 +95,7 @@
             users = [(x, y, 0), (x - 1, y, 1), (x + 1, y, 2), (x, y - 1, 3), (x, y + 1, 4)]
             users = [u for u in users if 0 <= u[0] < cx and 0 <= u[1] < cy]
             add(rows_ref[x * cy + y], users)
+    used = 0
     for axis, far, block_ref in (
         ("gx", 0, near_x_ref),
         ("gx", 1, far_x_ref),
@@ -105,7 +106,8 @@
         is_next = index % 2 == far
         outside = ((index == 0) | (index == sizes[axis] - 1)) if far else False
         for n in range(cy if axis == "gx" else cx):
-            block = unpacked(block_ref[n], wide_ref.at[n % 4])
+            block = unpacked(block_ref[n], wide_ref.at[used])
+            used += 1
             if axis == "gx":
                 user = (jnp.where(is_next, cx - 1, 0), n, jnp.where(is_next, 1, 2))
             else:
@@ -197,7 +199,7 @@
         scratch_shapes=[
             pltpu.VMEM((cells, 32, 128), jnp.bfloat16),
             pltpu.VMEM((cells, 64, 320), jnp.bfloat16),
-            pltpu.VMEM((4, 64, 128), jnp.float32),
+            pltpu.VMEM((cells, 64, 128), jnp.float32),
             pltpu.SemaphoreType.DMA((CHUNKS + 1,)),
         ],
         compiler_params=PARAMS,
@@ -217,7 +219,7 @@
         out_specs=(VMEM, VMEM),
         scratch_shapes=[
             pltpu.VMEM((cells + 1, 64, 128), jnp.float32),
-            pltpu.VMEM((4, 64, 128), jnp.float32),
+            pltpu.VMEM((2 * (cx + cy), 64, 128), jnp.float32),
             pltpu.VMEM((RING, SLOTS * 32, 128), jnp.bfloat16),
             pltpu.SMEM((RING,), jnp.int32),
         ],

time: 99.8 us -> 99.8 us (level)
  no operation moved by 1% of the time
where the time goes in v10:
time: 99.8 us; the launch traced here: 99.4 us
  blocking collectives  58.4 us (59%)
  starting transfers between devices  29 us (29%)
  Pallas kernels  8.56 us (9%)
  other arithmetic  2.45 us (2%)
    all_to_all x1, blocking collectives, exchange(): lax.all_to_all(array, 'gy', 0, 0, axis_index_groups=along, tiled=True)  46.4 us
    ppermute x2, starting transfers between devices, swapped(): lax.ppermute(jnp.where(even, head, tail), axis, far)  22.3 us
    all_to_all x1, blocking collectives, shards(): lax.all_to_all(dense.reshape(across, owned * 32, 128), 'gy', 0, 0, axis_i...  12 us
    ppermute x2, starting transfers between devices, swapped(): lax.ppermute(jnp.where(even, tail, head), axis, near)  6.72 us
    pallas_call x1, Pallas kernels, shards(): pl.pallas_call(left_kernel, out_shape=(jax.ShapeDtypeStruct((cells, 5, 64...  4.29 us
    pallas_call x1, Pallas kernels, shards(): pl.pallas_call(lambda *refs: partial_kernel(cx, cy, sizes, *refs), out_sh...  2.48 us
  transfers between devices with their start and end apart: 4, of which 0 were waited for; matrix products, arithmetic and copies ran while one was open for 1% of the time, Pallas kernels for 4%

profile of v10, /device:TPU:24, one launch (start us, length us, event | category | flops | bytes accessed | tf_op | source)
XLA Modules:
  0.0 99.4 jit_solution(7695617462999333114)
XLA Ops:
  0.0 0.0 copy-start.3
  0.0 0.0 copy-start.2
  0.0 0.0 copy-start
  0.0 0.0 copy-start.1
  0.0 0.9 select_bitcast_fusion
  0.9 1.9 %collective-permute-start.1 = (bf16[8,32,128]{2,1,0:T(8,128)(2,1)S(1)}, bf16[8,32,128]{2,1,0:T(8,128)(2,1)S(1)}, u32[]{:S(2)}, u32[]{:S(2)}) collective-permute-start(bf16[8,32,128]{2,1,0:T(8,128)(2,1)S(1)} %get-tuple-element.36), channel_id=1, source_target_pairs={{0,960},{64,128},{128,64},{192,256},{256,192},{320,384},{384,320},... | collective-permute-start | bytes 196616 | tf_op jit(solution)/shard_map/ppermute | solution.py:185
  2.9 4.8 %collective-permute-start = (bf16[8,32,128]{2,1,0:T(8,128)(2,1)S(1)}, bf16[8,32,128]{2,1,0:T(8,128)(2,1)S(1)}, u32[]{:S(2)}, u32[]{:S(2)}) collective-permute-start(bf16[8,32,128]{2,1,0:T(8,128)(2,1)S(1)} %get-tuple-element.37), channel_id=1, source_target_pairs={{0,64},{64,0},{128,192},{192,128},{256,320},{320,256},{384,448},{4... | collective-permute-start | bytes 196616 | tf_op jit(solution)/shard_map/ppermute | solution.py:184
  7.7 0.8 fusion.1
  8.5 20.4 %collective-permute-start.3 = (bf16[4,32,128]{2,1,0:T(8,128)(2,1)S(1)}, bf16[4,32,128]{2,1,0:T(8,128)(2,1)S(1)}, u32[]{:S(2)}, u32[]{:S(2)}) collective-permute-start(bf16[4,32,128]{2,1,0:T(8,128)(2,1)S(1)} %get-tuple-element.34), channel_id=1, source_target_pairs={{0,63},{1,2},{2,1},{3,4},{4,3},{5,6},{6,5},{7,8},{8,7},{9,10},{10,... | collective-permute-start | bytes 98312 | tf_op jit(solution)/shard_map/ppermute | solution.py:185
  28.9 1.9 %collective-permute-start.2 = (bf16[4,32,128]{2,1,0:T(8,128)(2,1)S(1)}, bf16[4,32,128]{2,1,0:T(8,128)(2,1)S(1)}, u32[]{:S(2)}, u32[]{:S(2)}) collective-permute-start(bf16[4,32,128]{2,1,0:T(8,128)(2,1)S(1)} %get-tuple-element.35), channel_id=1, source_target_pairs={{0,1},{1,0},{2,3},{3,2},{4,5},{5,4},{6,7},{7,6},{8,9},{9,8},{10,11... | collective-permute-start | bytes 98312 | tf_op jit(solution)/shard_map/ppermute | solution.py:184
  30.8 4.3 %left_factor.1 = (bf16[32,5,64,64]{3,2,1,0:T(8,128)(2,1)S(1)}, bf16[32,64,128]{2,1,0:T(8,128)(2,1)S(1)}) custom-call(bf16[32,32,128]{2,1,0:T(8,128)(2,1)} %bitcast.37, bf16[32,64,320]{2,1,0:T(8,128)(2,1)} %bitcast.38), custom_call_target="tpu_custom_call" | custom-call | flops 671088640 | bytes 2880000 | tf_op jit(solution)/shard_map/left_factor/pallas_call | solution.py:191
  35.1 0.0 collective-permute-done.3.refs_5_
  35.1 0.0 collective-permute-done.2.refs_4_
  35.1 0.0 collective-permute-done.1.refs_3_
  35.2 0.0 collective-permute-done.refs_2_
  35.2 0.0 copy-done.3
  35.2 0.0 copy-done.2
  35.2 0.0 copy-done
  35.2 0.0 copy-done.1
  35.2 2.5 %partial_blocks.1 = (bf16[16,208,128]{2,1,0:T(8,128)(2,1)S(1)}, bf16[16,64,128]{2,1,0:T(8,128)(2,1)S(1)}) custom-call(bf16[32,5,64,64]{3,2,1,0:T(8,128)(2,1)S(1)} %get-tuple-element.25.refs_0_, bf16[32,64,128]{2,1,0:T(8,128)(2,1)S(1)} %get-tuple-element.26.refs_1_, bf16[8,32,128]{2,1,0:T(8,128)(2,1)S(1)} %collective-permute-done.refs_2_, ...), custom_call_target="tpu_custom_call" | custom-call | tf_op jit(solution)/shard_map/partial_blocks/pallas_call | solution.py:212
  37.7 46.4 %all_to_all.15.refs_0_ = bf16[16,208,128]{2,1,0:T(8,128)(2,1)S(1)} all-to-all(bf16[16,208,128]{2,1,0:T(8,128)(2,1)S(1)} %get-tuple-element.27), channel_id=1, replica_groups={{0,1,2,3,4,5,6,7,8,9,10,11,12,13,14,15},{16,17,18,19,20,21,22,23,24,25,..., dimensions={0} | all-to-all | bytes 1703936 | tf_op jit(solution)/shard_map/all_to_all | solution.py:242
  84.1 1.8 %ring_sums.1 = (bf16[64,32,128]{2,1,0:T(8,128)(2,1)S(1)}, s32[1]{0:T(128)}) custom-call(bf16[16,208,128]{2,1,0:T(8,128)(2,1)S(1)} %all_to_all.15.refs_0_, s32[16,9]{1,0:T(8,128)S(1)} %fusion.2.refs_1_), custom_call_target="tpu_custom_call" | custom-call | tf_op jit(solution)/shard_map/ring_sums/pallas_call | solution.py:249
  86.6 12.0 %all_to_all.16 = bf16[4,512,128]{2,1,0:T(8,128)(2,1)S(1)} all-to-all(bf16[4,512,128]{2,1,0:T(8,128)(2,1)S(1)} %bitcast.36), channel_id=1, replica_groups={{0,16,32,48},{1,17,33,49},{2,18,34,50},{3,19,35,51},{4,20,36,52},{5,21,..., dimensions={0} | all-to-all | bytes 1048576 | tf_op jit(solution)/shard_map/all_to_all | solution.py:268
  98.6 0.7 reduce_sum.12
  (3 shorter events, 0.0 us)
Async XLA Ops:
  0.0 35.2 %copy-start.3 = (s32[1,32]{1,0:T(1,128)S(1)}, s32[1,32]{1,0:T(1,128)}, u32[]{:S(2)}) copy-start(s32[1,32]{1,0:T(1,128)} %param.13) | copy-start | bytes 388
  0.0 35.2 %copy-start.2 = (s32[1,32,1]{1,2,0:T(1,128)S(1)}, s32[1,32,1]{1,2,0:T(1,128)}, u32[]{:S(2)}) copy-start(s32[1,32,1]{1,2,0:T(1,128)} %param.12) | copy-start | bytes 388
  0.0 35.2 %copy-start = (s32[4,8,5]{1,0,2:T(4,128)S(1)}, s32[4,8,5]{1,0,2:T(4,128)}, u32[]{:S(2)}) copy-start(s32[4,8,5]{1,0,2:T(4,128)} %param.11) | copy-start | bytes 1924
  0.0 35.2 %copy-start.1 = (s32[4,8,4]{1,2,0:T(4,128)S(1)}, s32[4,8,4]{1,2,0:T(4,128)}, u32[]{:S(2)}) copy-start(s32[4,8,4]{1,2,0:T(4,128)} %param.10) | copy-start | bytes 1540
  0.9 34.2 %collective-permute-start.1 = (bf16[8,32,128]{2,1,0:T(8,128)(2,1)S(1)}, bf16[8,32,128]{2,1,0:T(8,128)(2,1)S(1)}, u32[]{:S(2)}, u32[]{:S(2)}) collective-permute-start(bf16[8,32,128]{2,1,0:T(8,128)(2,1)S(1)} %get-tuple-element.36), channel_id=1, source_target_pairs={{0,960},{64,128},{128,64},{192,256},{256,192},{320,384},{384,320},... | collective-permute-start | bytes 196616 | tf_op jit(solution)/shard_map/ppermute | solution.py:185
  2.9 32.3 %collective-permute-start = (bf16[8,32,128]{2,1,0:T(8,128)(2,1)S(1)}, bf16[8,32,128]{2,1,0:T(8,128)(2,1)S(1)}, u32[]{:S(2)}, u32[]{:S(2)}) collective-permute-start(bf16[8,32,128]{2,1,0:T(8,128)(2,1)S(1)} %get-tuple-element.37), channel_id=1, source_target_pairs={{0,64},{64,0},{128,192},{192,128},{256,320},{320,256},{384,448},{4... | collective-permute-start | bytes 196616 | tf_op jit(solution)/shard_map/ppermute | solution.py:184
  8.5 26.6 %collective-permute-start.3 = (bf16[4,32,128]{2,1,0:T(8,128)(2,1)S(1)}, bf16[4,32,128]{2,1,0:T(8,128)(2,1)S(1)}, u32[]{:S(2)}, u32[]{:S(2)}) collective-permute-start(bf16[4,32,128]{2,1,0:T(8,128)(2,1)S(1)} %get-tuple-element.34), channel_id=1, source_target_pairs={{0,63},{1,2},{2,1},{3,4},{4,3},{5,6},{6,5},{7,8},{8,7},{9,10},{10,... | collective-permute-start | bytes 98312 | tf_op jit(solution)/shard_map/ppermute | solution.py:185
  28.9 6.2 %collective-permute-start.2 = (bf16[4,32,128]{2,1,0:T(8,128)(2,1)S(1)}, bf16[4,32,128]{2,1,0:T(8,128)(2,1)S(1)}, u32[]{:S(2)}, u32[]{:S(2)}) collective-permute-start(bf16[4,32,128]{2,1,0:T(8,128)(2,1)S(1)} %get-tuple-element.35), channel_id=1, source_target_pairs={{0,1},{1,0},{2,3},{3,2},{4,5},{5,4},{6,7},{7,6},{8,9},{9,8},{10,11... | collective-permute-start | bytes 98312 | tf_op jit(solution)/shard_map/ppermute | solution.py:184
